TPU v7x, 32 devices: a whole 2x2x4 slice. The times are simulated.
32 devices in a mesh: dp: 8 (over z, y), mp: 4 (over x, core).
Axes of the slice: x: 2, y: 2, z: 4, core: 2. Of those that a mesh axis runs over, the one named last changes fastest.
Arguments:
- clean_latent: float32 [16, 768, 20], P('dp', 'mp'), may hold values from -6 to 6
- noise_draw: float32 [16, 768, 20], P('dp', 'mp'), may hold values from -6 to 6
- captions: bfloat16 [16, 256, 768], P('dp'), may hold values from -6 to 6
- caption_len: int32 [16], P('dp'), may hold values from 5 to 256, as said below
- timestep: int32 [16], P('dp'), may hold values from 0 to 999
- step_weight: float32 [1000], replicated, may hold values from 0.25 to 4
- step_count: int32 [1], replicated, may hold values from 2 to 20
- unit_slot: int32 [26], replicated, may hold values from 0 to 39, as said below
- master: float32 [40, 768, 768], P('dp', 'mp'), may hold values from -0.21875 to 0.21875
- first_moment: float32 [40, 768, 768], P('dp', 'mp'), may hold values from -8.34465e-07 to 8.34465e-07
- second_moment: float32 [40, 768, 768], P('dp', 'mp'), may hold values from 2.6031255e-16 to 1.0412502e-15
- latent_master: float32 [2, 20, 768], replicated, may hold values from -0.21875 to 0.21875
- latent_first: float32 [2, 20, 768], replicated, may hold values from -4.7683716e-06 to 4.7683716e-06
- latent_second: float32 [2, 20, 768], replicated, may hold values from 9.300595e-15 to 3.720238e-14
Outputs:
- updated_master: float32 [40, 768, 768], P('dp', 'mp')
- updated_first: float32 [40, 768, 768], P('dp', 'mp')
- updated_second: float32 [40, 768, 768], P('dp', 'mp')
- latent_updated: float32 [2, 20, 768], replicated
- latent_first_out: float32 [2, 20, 768], replicated
- latent_second_out: float32 [2, 20, 768], replicated
- grad_norm: float32 [], replicated
- loss_value: float32 [], replicated
Inputs may be any that keep to these rules, and one draw needn't show every extreme that they name: Clip b's caption occupies its first caption_len[b] token slots; some clip uses all 256. All entries differ, so every place holds at most one matrix; matrix u is owned by dp index unit_slot[u] // 5 in its place unit_slot[u] % 5; some dp index owns 5 matrices, every other index owns 0 to 5.
All inputs are finite; a program needn't handle non-finite values.
Results may differ from a plain program's by a relative error of at most 0.017.
Values may be sent and summed in bfloat16 or wider, within the bound.
No kernel may reach another device: no remote copies, remote signals or barrier semaphores. Data moves between devices by JAX's collectives and lax.ppermute only.
A program may use at most 192 MiB of HBM per device.

v0:
```python
import math

import jax
import jax.numpy as jnp
from jax import lax
from jax.sharding import PartitionSpec as P

D = 768
HD = 64
C = 20
FRAMES = 768
NT = 1000
UNITS = 26


highest = lax.Precision.HIGHEST
beta_first = 0.9
beta_second = 0.999
adam_epsilon = 1e-08
learn_rate = 0.02
decay_rate = 0.1
clip_limit = 0.002
norm_epsilon = 1e-06
masked_score = -1e30
bfloat = jnp.bfloat16
single = jnp.float32


def broadcast(array, axis, root):
    mine = lax.axis_index(axis) == root
    return lax.psum(jnp.where(mine, array, jnp.zeros_like(array)), axis)


def normed(values):
    center = values - jnp.mean(values, axis=-1, keepdims=True)
    spread_sq = jnp.mean(center * center, axis=-1, keepdims=True)
    return center * lax.rsqrt(spread_sq + norm_epsilon)


def modulate(values, shift, scale):
    return normed(values) * (1.0 + scale[:, None, :]) + shift[:, None, :]


def modulate_back(values, shift, scale, grad):
    _, pullback = jax.vjp(modulate, values, shift, scale)
    return pullback(grad)


def adamw(weight, moment, square, grad, count):
    moment = beta_first * moment + (1.0 - beta_first) * grad
    square = beta_second * square + (1.0 - beta_second) * grad * grad
    first_fix = 1.0 - jnp.power(beta_first, count)
    second_fix = 1.0 - jnp.power(beta_second, count)
    update = (
        moment / first_fix / (jnp.sqrt(square / second_fix) + adam_epsilon) + decay_rate * weight
    )
    return (weight - learn_rate * update, moment, square)


def sinusoid(timestep):
    half_width = D // 2
    frequency = jnp.exp(-math.log(10000.0) * jnp.arange(half_width).astype(single) / half_width)
    angles = timestep.astype(single)[:, None] * frequency[None, :]
    return jnp.concatenate([jnp.cos(angles), jnp.sin(angles)], axis=1)


def matmul(form, left, right):
    return jnp.einsum(form, left, right, preferred_element_type=single)


def masked_scores(query, keys, mask):
    scores = matmul("fhk,ghk->hfg", query, keys) * HD ** (-0.5)
    return jnp.where(mask[None, None, :], scores, masked_score)


def attend_forward(parts):
    query, keys, values, mask = parts
    scores = masked_scores(query, keys, mask)
    row_max = jnp.max(scores, axis=-1, keepdims=True)
    shifted = jnp.exp(scores - row_max)
    row_total = jnp.sum(shifted, axis=-1, keepdims=True)
    probs = shifted / row_total
    output = matmul("hfg,ghk->fhk", probs.astype(bfloat), values)
    return (output.astype(bfloat), (row_max + jnp.log(row_total))[..., 0])


def attend_backward(parts):
    query, keys, values, mask, grad_out, log_total = parts
    probs = jnp.exp(masked_scores(query, keys, mask) - log_total[..., None])
    grad_probs = matmul("fhk,ghk->hfg", grad_out, values)
    inner = jnp.sum(probs * grad_probs, axis=-1, keepdims=True)
    grad_scores = (probs * (grad_probs - inner)).astype(bfloat)
    grad_query = matmul("hfg,ghk->fhk", grad_scores, keys) * HD ** (-0.5)
    grad_keys = matmul("hfg,fhk->ghk", grad_scores, query) * HD ** (-0.5)
    grad_values = matmul("hfg,fhk->ghk", probs.astype(bfloat), grad_out)
    return (grad_query.astype(bfloat), grad_keys.astype(bfloat), grad_values.astype(bfloat))


def split_heads(values):
    return values.reshape(values.shape[0], values.shape[1], -1, HD)


def merge_heads(values):
    return values.reshape(values.shape[0], values.shape[1], -1)


def attention(query, keys, values, mask):
    output, log_total = lax.map(
        attend_forward, (split_heads(query), split_heads(keys), split_heads(values), mask)
    )
    return (merge_heads(output), log_total)


def attention_back(query, keys, values, mask, grad_out, log_total):
    grads = lax.map(
        attend_backward,
        (
            split_heads(query),
            split_heads(keys),
            split_heads(values),
            mask,
            split_heads(grad_out),
            log_total,
        ),
    )
    return tuple((merge_heads(item) for item in grads))


def spread(values):
    return lax.all_gather(values, "mp", axis=1, tiled=True)


def collect(values):
    return lax.psum_scatter(
        values.astype(jnp.bfloat16), "mp", scatter_dimension=1, tiled=True
    ).astype(jnp.float32)


def side_by_side(stack):
    return jnp.transpose(stack, (1, 0, 2)).reshape(stack.shape[1], -1)


def body(
    clean_latent,
    noise_draw,
    captions,
    caption_len,
    timestep,
    step_weight,
    step_count,
    unit_slot,
    master,
    first_moment,
    second_moment,
    latent_master,
    latent_first,
    latent_second,
):
    slots = master.shape[0]
    owner = unit_slot // slots
    place = unit_slot % slots

    def fetch_one(running, index):
        local = lax.dynamic_index_in_dim(master, place[index], 0, keepdims=False).astype(bfloat)
        return (running, broadcast(local, "dp", owner[index]))

    _, fetched = lax.scan(fetch_one, 0, jnp.arange(UNITS))
    weights = jnp.swapaxes(fetched, 1, 2)
    width = weights.shape[2]
    table = jnp.arange(step_weight.shape[0])
    clip_weight = jnp.sum(
        jnp.where(timestep[:, None] == table[None, :], step_weight[None, :], 0.0), axis=1
    )
    weight_total = lax.psum(jnp.sum(clip_weight), "dp")
    level = (timestep.astype(single) + 0.5) / NT
    noisy = (1.0 - level)[:, None, None] * clean_latent + level[:, None, None] * noise_draw
    target = noise_draw - clean_latent
    cap_mask = jnp.arange(captions.shape[1])[None, :] < caption_len[:, None]
    pooled = (
        jnp.sum(jnp.where(cap_mask[:, :, None], captions.astype(single), 0.0), axis=1)
        / caption_len.astype(single)[:, None]
    )
    sinus_low = sinusoid(timestep).astype(bfloat)
    pooled_low = pooled.astype(bfloat)
    cond_part = matmul("bd,de->be", sinus_low, weights[24]) + matmul(
        "bd,de->be", pooled_low, weights[25]
    )
    cond = lax.all_gather(cond_part, "mp", axis=1, tiled=True)
    active = jax.nn.silu(cond).astype(bfloat)
    modulation = lax.all_gather(
        matmul("bd,jde->bje", active, weights[16:24]), "mp", axis=2, tiled=True
    )
    hidden_zero = jnp.einsum("bfc,cd->bfd", noisy, latent_master[0], precision=highest)
    w_attn = side_by_side(weights[0:3])
    first_in = spread(modulate(hidden_zero, modulation[:, 0], modulation[:, 1]).astype(bfloat))
    self_proj = matmul("bfd,de->bfe", first_in, w_attn).astype(bfloat)
    self_query, self_keys, self_values = jnp.split(self_proj, 3, axis=2)
    self_mask = jnp.ones((self_query.shape[0], self_query.shape[1]), bool)
    self_flat, self_total = attention(self_query, self_keys, self_values, self_mask)
    self_branch = collect(matmul("bfk,dk->bfd", self_flat, weights[3]))
    hidden_one = hidden_zero + modulation[:, 2, None, :] * self_branch
    second_in = spread(normed(hidden_one).astype(bfloat))
    cross_query = matmul("bfd,de->bfe", second_in, weights[4]).astype(bfloat)
    w_text = side_by_side(weights[5:7])
    cross_keys, cross_values = jnp.split(
        matmul("bld,de->ble", captions, w_text).astype(bfloat), 2, axis=2
    )
    cross_flat, cross_total = attention(cross_query, cross_keys, cross_values, cap_mask)
    cross_branch = collect(matmul("bfk,dk->bfd", cross_flat, weights[7]))
    hidden_two = hidden_one + cross_branch
    w_up = side_by_side(weights[8:12])
    w_down = side_by_side(weights[12:16])
    third_in = spread(modulate(hidden_two, modulation[:, 3], modulation[:, 4]).astype(bfloat))
    upper_wide = matmul("bfd,dk->bfk", third_in, w_up).astype(bfloat).astype(single)
    activated = jax.nn.gelu(upper_wide, approximate=True).astype(bfloat)
    mlp_branch = collect(matmul("bfk,dk->bfd", activated, w_down))
    hidden_three = hidden_two + modulation[:, 5, None, :] * mlp_branch
    final_wide = (
        modulate(hidden_three, modulation[:, 6], modulation[:, 7]).astype(bfloat).astype(single)
    )
    predicted = jnp.einsum("bfd,cd->bfc", final_wide, latent_master[1], precision=highest)
    error = predicted - target
    loss_local = jnp.sum(clip_weight[:, None, None] * error * error)
    grad_pred = 2.0 / (C * FRAMES) * clip_weight[:, None, None] * error / weight_total
    grad_out_proj = jnp.einsum("bfc,bfd->cd", grad_pred, final_wide, precision=highest)
    grad_final = jnp.einsum("bfc,cd->bfd", grad_pred, latent_master[1], precision=highest)
    grad_three, shift_f, scale_f = modulate_back(
        hidden_three, modulation[:, 6], modulation[:, 7], grad_final
    )
    gate_m_grad = jnp.sum(grad_three * mlp_branch, axis=1)
    grad_mlp = spread((modulation[:, 5, None, :] * grad_three).astype(bfloat))
    grad_act = matmul("bfd,dk->bfk", grad_mlp, w_down)
    grad_w_down = matmul("bfd,bfk->dk", grad_mlp, activated)
    _, gelu_back = jax.vjp(lambda inner_in: jax.nn.gelu(inner_in, approximate=True), upper_wide)
    grad_upper = gelu_back(grad_act)[0].astype(bfloat)
    grad_w_up = matmul("bfd,bfk->dk", third_in, grad_upper)
    grad_third = collect(matmul("bfk,dk->bfd", grad_upper, w_up))
    grad_two, shift_m, scale_m = modulate_back(
        hidden_two, modulation[:, 3], modulation[:, 4], grad_third
    )
    grad_two = grad_two + grad_three
    grad_cross = spread(grad_two.astype(bfloat))
    grad_cross_flat = matmul("bfd,dk->bfk", grad_cross, weights[7]).astype(bfloat)
    grad_w_cross_out = matmul("bfd,bfk->dk", grad_cross, cross_flat)
    cq_grad, ck_grad, cv_grad = attention_back(
        cross_query, cross_keys, cross_values, cap_mask, grad_cross_flat, cross_total
    )
    grad_w_cq = matmul("bfd,bfk->dk", second_in, cq_grad)
    grad_w_text = matmul("bld,ble->de", captions, jnp.concatenate([ck_grad, cv_grad], axis=2))
    grad_second = collect(matmul("bfk,dk->bfd", cq_grad, weights[4]))
    _, norm_back = jax.vjp(normed, hidden_one)
    grad_one = grad_two + norm_back(grad_second)[0]
    gate_a_grad = jnp.sum(grad_one * self_branch, axis=1)
    grad_self = spread((modulation[:, 2, None, :] * grad_one).astype(bfloat))
    grad_self_flat = matmul("bfd,dk->bfk", grad_self, weights[3]).astype(bfloat)
    grad_w_self_out = matmul("bfd,bfk->dk", grad_self, self_flat)
    sq_grad, sk_grad, sv_grad = attention_back(
        self_query, self_keys, self_values, self_mask, grad_self_flat, self_total
    )
    grad_proj = jnp.concatenate([sq_grad, sk_grad, sv_grad], axis=2)
    grad_w_attn = matmul("bfd,bfe->de", first_in, grad_proj)
    grad_first = collect(matmul("bfe,de->bfd", grad_proj, w_attn))
    grad_zero, shift_a, scale_a = modulate_back(
        hidden_zero, modulation[:, 0], modulation[:, 1], grad_first
    )
    grad_zero = grad_zero + grad_one
    grad_in_proj = jnp.einsum("bfc,bfd->cd", noisy, grad_zero, precision=highest)
    grad_mod = jnp.stack(
        [shift_a, scale_a, gate_a_grad, shift_m, scale_m, gate_m_grad, shift_f, scale_f], axis=1
    )
    mod_own = (
        lax.psum_scatter(grad_mod.astype(jnp.bfloat16), "mp", scatter_dimension=2, tiled=True)
        .astype(jnp.float32)
        .astype(bfloat)
    )
    grad_ada = matmul("bd,bje->jde", active, mod_own)
    grad_active = matmul("bje,jde->bd", mod_own, weights[16:24])
    _, silu_back = jax.vjp(jax.nn.silu, cond)
    cond_own = lax.psum_scatter(
        silu_back(grad_active)[0], "mp", scatter_dimension=1, tiled=True
    ).astype(bfloat)
    grad_time = matmul("bd,be->de", sinus_low, cond_own)
    grad_pool = matmul("bd,be->de", pooled_low, cond_own)

    def columns(matrix, count):
        return jnp.transpose(matrix.reshape(matrix.shape[0], count, width), (1, 0, 2))

    grads_cols = jnp.concatenate(
        [
            columns(grad_w_attn, 3),
            grad_w_self_out[None],
            grad_w_cq[None],
            columns(grad_w_text, 2),
            grad_w_cross_out[None],
            columns(grad_w_up, 4),
            columns(grad_w_down, 4),
            grad_ada,
            grad_time[None],
            grad_pool[None],
        ],
        axis=0,
    )
    grads = jnp.swapaxes(grads_cols, 1, 2)
    local_ids = lax.axis_index("dp") * slots + jnp.arange(slots)
    pick = (unit_slot[None, :] == local_ids[:, None]).astype(single)
    live_slot = jnp.sum(pick, axis=1) > 0.5
    summed = lax.psum(grads, "dp")
    owned = jnp.einsum("su,ude->sde", pick, summed, precision=highest)
    latent_grad, loss_sum = lax.psum(
        (jnp.stack([grad_in_proj, grad_out_proj]), loss_local), ("dp", "mp")
    )
    square_sum = lax.psum(jnp.sum(owned * owned), ("dp", "mp")) + jnp.sum(latent_grad * latent_grad)
    grad_norm = jnp.sqrt(square_sum)
    factor = clip_limit / jnp.maximum(grad_norm, clip_limit)
    count = step_count[0].astype(single)
    new_weight, new_moment, new_square = adamw(
        master, first_moment, second_moment, owned * factor, count
    )
    keep = live_slot[:, None, None]
    latent_weight, latent_moment, latent_square = adamw(
        latent_master, latent_first, latent_second, latent_grad * factor, count
    )
    loss_value = loss_sum / (C * FRAMES * weight_total)
    return (
        jnp.where(keep, new_weight, master),
        jnp.where(keep, new_moment, first_moment),
        jnp.where(keep, new_square, second_moment),
        latent_weight,
        latent_moment,
        latent_square,
        grad_norm,
        loss_value,
    )


def solution(mesh):
    placed = (
        P("dp", "mp", None),
        P("dp", "mp", None),
        P("dp", None, None),
        P("dp"),
        P("dp"),
        P(),
        P(),
        P(),
        P("dp", "mp", None),
        P("dp", "mp", None),
        P("dp", "mp", None),
        P(),
        P(),
        P(),
    )
    return jax.shard_map(
        body,
        mesh=mesh,
        in_specs=placed,
        out_specs=(
            P("dp", "mp", None),
            P("dp", "mp", None),
            P("dp", "mp", None),
            P(),
            P(),
            P(),
            P(),
            P(),
        ),
        check_vma=False,
    )
```

profile of v0, /device:TPU:8, one launch (start us, length us, event | category | flops | bytes accessed | tf_op | source)
XLA Modules:
  0.0 3429.3 jit_solution(15511548824490936030)
XLA Ops:
  17.4 2052.2 %while.62 = (s32[]{:T(128)}, bf16[26,192,768]{2,1,0:T(8,128)(2,1)}, s32[26]{0:T(128)S(1)}, s32[26]{0:T(128)S(1)}, s32[26]{0:T(128)S(1)}, /*index=5*/bf16[5,192,7...) while((s32[]{:T(128)}, bf16[26,192,768]{2,1,0:T(8,128)(2,1)}, ...), condition=%wide.region_5.6_spmd, body=%wide.region_3.5_spmd.sunk | while | flops 294924 | bytes 2949439 | solution.py:167
  24.6 71.5 %all-reduce.9.cloned.1.call-done = bf16[1,192,768]{2,1,0:T(8,128)(2,1)} async-done(((bf16[1,192,768]{2,1,0:T(8,128)(2,1)}), bf16[1,192,768]{2,1,0:T(8,128)(2,1)}) %all-reduce.9.cloned.1.call-update) | async-done | bytes 294928 | tf_op jit(solution)/shard_map/while/body/eval_jaxpr/psum | solution.py:31
  104.8 70.1 %all-reduce.9.cloned.1.call-done = bf16[1,192,768]{2,1,0:T(8,128)(2,1)} async-done(((bf16[1,192,768]{2,1,0:T(8,128)(2,1)}), bf16[1,192,768]{2,1,0:T(8,128)(2,1)}) %all-reduce.9.cloned.1.call-update) | async-done | bytes 294928 | tf_op jit(solution)/shard_map/while/body/eval_jaxpr/psum | solution.py:31
  183.7 70.1 %all-reduce.9.cloned.1.call-done = bf16[1,192,768]{2,1,0:T(8,128)(2,1)} async-done(((bf16[1,192,768]{2,1,0:T(8,128)(2,1)}), bf16[1,192,768]{2,1,0:T(8,128)(2,1)}) %all-reduce.9.cloned.1.call-update) | async-done | bytes 294928 | tf_op jit(solution)/shard_map/while/body/eval_jaxpr/psum | solution.py:31
  262.6 70.1 %all-reduce.9.cloned.1.call-done = bf16[1,192,768]{2,1,0:T(8,128)(2,1)} async-done(((bf16[1,192,768]{2,1,0:T(8,128)(2,1)}), bf16[1,192,768]{2,1,0:T(8,128)(2,1)}) %all-reduce.9.cloned.1.call-update) | async-done | bytes 294928 | tf_op jit(solution)/shard_map/while/body/eval_jaxpr/psum | solution.py:31
  341.4 70.1 %all-reduce.9.cloned.1.call-done = bf16[1,192,768]{2,1,0:T(8,128)(2,1)} async-done(((bf16[1,192,768]{2,1,0:T(8,128)(2,1)}), bf16[1,192,768]{2,1,0:T(8,128)(2,1)}) %all-reduce.9.cloned.1.call-update) | async-done | bytes 294928 | tf_op jit(solution)/shard_map/while/body/eval_jaxpr/psum | solution.py:31
  420.3 70.1 %all-reduce.9.cloned.1.call-done = bf16[1,192,768]{2,1,0:T(8,128)(2,1)} async-done(((bf16[1,192,768]{2,1,0:T(8,128)(2,1)}), bf16[1,192,768]{2,1,0:T(8,128)(2,1)}) %all-reduce.9.cloned.1.call-update) | async-done | bytes 294928 | tf_op jit(solution)/shard_map/while/body/eval_jaxpr/psum | solution.py:31
  499.2 70.1 %all-reduce.9.cloned.1.call-done = bf16[1,192,768]{2,1,0:T(8,128)(2,1)} async-done(((bf16[1,192,768]{2,1,0:T(8,128)(2,1)}), bf16[1,192,768]{2,1,0:T(8,128)(2,1)}) %all-reduce.9.cloned.1.call-update) | async-done | bytes 294928 | tf_op jit(solution)/shard_map/while/body/eval_jaxpr/psum | solution.py:31
  578.0 70.1 %all-reduce.9.cloned.1.call-done = bf16[1,192,768]{2,1,0:T(8,128)(2,1)} async-done(((bf16[1,192,768]{2,1,0:T(8,128)(2,1)}), bf16[1,192,768]{2,1,0:T(8,128)(2,1)}) %all-reduce.9.cloned.1.call-update) | async-done | bytes 294928 | tf_op jit(solution)/shard_map/while/body/eval_jaxpr/psum | solution.py:31
  656.9 70.1 %all-reduce.9.cloned.1.call-done = bf16[1,192,768]{2,1,0:T(8,128)(2,1)} async-done(((bf16[1,192,768]{2,1,0:T(8,128)(2,1)}), bf16[1,192,768]{2,1,0:T(8,128)(2,1)}) %all-reduce.9.cloned.1.call-update) | async-done | bytes 294928 | tf_op jit(solution)/shard_map/while/body/eval_jaxpr/psum | solution.py:31
  735.8 70.1 %all-reduce.9.cloned.1.call-done = bf16[1,192,768]{2,1,0:T(8,128)(2,1)} async-done(((bf16[1,192,768]{2,1,0:T(8,128)(2,1)}), bf16[1,192,768]{2,1,0:T(8,128)(2,1)}) %all-reduce.9.cloned.1.call-update) | async-done | bytes 294928 | tf_op jit(solution)/shard_map/while/body/eval_jaxpr/psum | solution.py:31
  814.7 70.1 %all-reduce.9.cloned.1.call-done = bf16[1,192,768]{2,1,0:T(8,128)(2,1)} async-done(((bf16[1,192,768]{2,1,0:T(8,128)(2,1)}), bf16[1,192,768]{2,1,0:T(8,128)(2,1)}) %all-reduce.9.cloned.1.call-update) | async-done | bytes 294928 | tf_op jit(solution)/shard_map/while/body/eval_jaxpr/psum | solution.py:31
  893.5 70.1 %all-reduce.9.cloned.1.call-done = bf16[1,192,768]{2,1,0:T(8,128)(2,1)} async-done(((bf16[1,192,768]{2,1,0:T(8,128)(2,1)}), bf16[1,192,768]{2,1,0:T(8,128)(2,1)}) %all-reduce.9.cloned.1.call-update) | async-done | bytes 294928 | tf_op jit(solution)/shard_map/while/body/eval_jaxpr/psum | solution.py:31
  972.4 70.1 %all-reduce.9.cloned.1.call-done = bf16[1,192,768]{2,1,0:T(8,128)(2,1)} async-done(((bf16[1,192,768]{2,1,0:T(8,128)(2,1)}), bf16[1,192,768]{2,1,0:T(8,128)(2,1)}) %all-reduce.9.cloned.1.call-update) | async-done | bytes 294928 | tf_op jit(solution)/shard_map/while/body/eval_jaxpr/psum | solution.py:31
  1051.3 70.1 %all-reduce.9.cloned.1.call-done = bf16[1,192,768]{2,1,0:T(8,128)(2,1)} async-done(((bf16[1,192,768]{2,1,0:T(8,128)(2,1)}), bf16[1,192,768]{2,1,0:T(8,128)(2,1)}) %all-reduce.9.cloned.1.call-update) | async-done | bytes 294928 | tf_op jit(solution)/shard_map/while/body/eval_jaxpr/psum | solution.py:31
  1130.1 70.1 %all-reduce.9.cloned.1.call-done = bf16[1,192,768]{2,1,0:T(8,128)(2,1)} async-done(((bf16[1,192,768]{2,1,0:T(8,128)(2,1)}), bf16[1,192,768]{2,1,0:T(8,128)(2,1)}) %all-reduce.9.cloned.1.call-update) | async-done | bytes 294928 | tf_op jit(solution)/shard_map/while/body/eval_jaxpr/psum | solution.py:31
  1209.0 70.1 %all-reduce.9.cloned.1.call-done = bf16[1,192,768]{2,1,0:T(8,128)(2,1)} async-done(((bf16[1,192,768]{2,1,0:T(8,128)(2,1)}), bf16[1,192,768]{2,1,0:T(8,128)(2,1)}) %all-reduce.9.cloned.1.call-update) | async-done | bytes 294928 | tf_op jit(solution)/shard_map/while/body/eval_jaxpr/psum | solution.py:31
  1287.9 70.1 %all-reduce.9.cloned.1.call-done = bf16[1,192,768]{2,1,0:T(8,128)(2,1)} async-done(((bf16[1,192,768]{2,1,0:T(8,128)(2,1)}), bf16[1,192,768]{2,1,0:T(8,128)(2,1)}) %all-reduce.9.cloned.1.call-update) | async-done | bytes 294928 | tf_op jit(solution)/shard_map/while/body/eval_jaxpr/psum | solution.py:31
  1366.8 70.1 %all-reduce.9.cloned.1.call-done = bf16[1,192,768]{2,1,0:T(8,128)(2,1)} async-done(((bf16[1,192,768]{2,1,0:T(8,128)(2,1)}), bf16[1,192,768]{2,1,0:T(8,128)(2,1)}) %all-reduce.9.cloned.1.call-update) | async-done | bytes 294928 | tf_op jit(solution)/shard_map/while/body/eval_jaxpr/psum | solution.py:31
  1445.7 70.1 %all-reduce.9.cloned.1.call-done = bf16[1,192,768]{2,1,0:T(8,128)(2,1)} async-done(((bf16[1,192,768]{2,1,0:T(8,128)(2,1)}), bf16[1,192,768]{2,1,0:T(8,128)(2,1)}) %all-reduce.9.cloned.1.call-update) | async-done | bytes 294928 | tf_op jit(solution)/shard_map/while/body/eval_jaxpr/psum | solution.py:31
  1524.6 70.1 %all-reduce.9.cloned.1.call-done = bf16[1,192,768]{2,1,0:T(8,128)(2,1)} async-done(((bf16[1,192,768]{2,1,0:T(8,128)(2,1)}), bf16[1,192,768]{2,1,0:T(8,128)(2,1)}) %all-reduce.9.cloned.1.call-update) | async-done | bytes 294928 | tf_op jit(solution)/shard_map/while/body/eval_jaxpr/psum | solution.py:31
  1603.4 70.1 %all-reduce.9.cloned.1.call-done = bf16[1,192,768]{2,1,0:T(8,128)(2,1)} async-done(((bf16[1,192,768]{2,1,0:T(8,128)(2,1)}), bf16[1,192,768]{2,1,0:T(8,128)(2,1)}) %all-reduce.9.cloned.1.call-update) | async-done | bytes 294928 | tf_op jit(solution)/shard_map/while/body/eval_jaxpr/psum | solution.py:31
  1682.3 70.1 %all-reduce.9.cloned.1.call-done = bf16[1,192,768]{2,1,0:T(8,128)(2,1)} async-done(((bf16[1,192,768]{2,1,0:T(8,128)(2,1)}), bf16[1,192,768]{2,1,0:T(8,128)(2,1)}) %all-reduce.9.cloned.1.call-update) | async-done | bytes 294928 | tf_op jit(solution)/shard_map/while/body/eval_jaxpr/psum | solution.py:31
  1761.2 70.1 %all-reduce.9.cloned.1.call-done = bf16[1,192,768]{2,1,0:T(8,128)(2,1)} async-done(((bf16[1,192,768]{2,1,0:T(8,128)(2,1)}), bf16[1,192,768]{2,1,0:T(8,128)(2,1)}) %all-reduce.9.cloned.1.call-update) | async-done | bytes 294928 | tf_op jit(solution)/shard_map/while/body/eval_jaxpr/psum | solution.py:31
  1840.1 70.1 %all-reduce.9.cloned.1.call-done = bf16[1,192,768]{2,1,0:T(8,128)(2,1)} async-done(((bf16[1,192,768]{2,1,0:T(8,128)(2,1)}), bf16[1,192,768]{2,1,0:T(8,128)(2,1)}) %all-reduce.9.cloned.1.call-update) | async-done | bytes 294928 | tf_op jit(solution)/shard_map/while/body/eval_jaxpr/psum | solution.py:31
  1918.9 70.1 %all-reduce.9.cloned.1.call-done = bf16[1,192,768]{2,1,0:T(8,128)(2,1)} async-done(((bf16[1,192,768]{2,1,0:T(8,128)(2,1)}), bf16[1,192,768]{2,1,0:T(8,128)(2,1)}) %all-reduce.9.cloned.1.call-update) | async-done | bytes 294928 | tf_op jit(solution)/shard_map/while/body/eval_jaxpr/psum | solution.py:31
  1997.8 70.1 %all-reduce.9.cloned.1.call-done = bf16[1,192,768]{2,1,0:T(8,128)(2,1)} async-done(((bf16[1,192,768]{2,1,0:T(8,128)(2,1)}), bf16[1,192,768]{2,1,0:T(8,128)(2,1)}) %all-reduce.9.cloned.1.call-update) | async-done | bytes 294928 | tf_op jit(solution)/shard_map/while/body/eval_jaxpr/psum | solution.py:31
  2099.0 22.4 all-gather.8.cloned.1.call-done
  2140.3 31.5 reduce-scatter.13.cloned.1.call-done
  2176.2 22.3 all-gather.10.cloned.1.call-done
  2214.6 29.8 reduce-scatter.15.cloned.1.call-done
  2251.5 20.8 all-gather.12.cloned.1.call-done
  2283.8 19.7 psum.42
  2324.6 24.0 all-gather.14.cloned.1.call-done
  2360.8 33.0 reduce-scatter.19.cloned.1.call-done
  2401.4 23.8 all-gather.16.cloned.1.call-done
  2429.5 14.6 while.65
  2447.5 33.0 reduce-scatter.21.cloned.1.call-done
  2488.8 23.9 all-gather.18.cloned.1.call-done
  2517.9 30.1 while.66
  2595.7 18.7 reduce-scatter.25.cloned.1.call-done
  2622.3 17.1 reduce-scatter.27.cloned.1.call-done
  2644.7 46.0 %concatenate.16 = f32[26,768,192]{1,0,2:T(8,128)} concatenate(f32[3,768,192]{1,0,2:T(4,128)S(1)} %bitcast.450, f32[1,768,192]{1,0,2:T(1,128)} %copy.315, f32[1,768,192]{1,0,2:T(1,128)} %copy.316, f32[2,768,192]{1,0,2:T(2,128)S(1)} %bitcast.466, f32[1,768,192]{1,0,2:T(1,128)} %copy.317, f32[4,768,192]{1,0,2:T(4,128)} %get-tuple-element.415, f32[4,768,192]{1,0,2:T(4,128)} %get-tuple-element.414, ...), dimensions={0} | concatenate | bytes 30670848 | tf_op jit(solution)/shard_map/concatenate | solution.py:288
  2692.3 76.2 %all-reduce.7.cloned.1.call-done = f32[2,20,768]{2,1,0:T(8,128)} async-done(((f32[2,20,768]{2,1,0:T(8,128)}), f32[2,20,768]{2,1,0:T(8,128)}) %all-reduce.7.cloned.1.call-update) | async-done | bytes 122896 | tf_op jit(solution)/shard_map/psum | solution.py:309
  2770.1 566.7 %all-reduce.5.cloned.1.call-done = f32[26,192,768]{2,0,1:T(8,128)} async-done(((f32[26,192,768]{2,0,1:T(8,128)}), f32[26,192,768]{2,0,1:T(8,128)}) %all-reduce.5.cloned.1.call-update) | async-done | bytes 15335440 | tf_op jit(solution)/shard_map/psum | solution.py:307
  3336.8 12.6 multiply_reduce_fusion.3
  3349.3 41.4 %all-reduce = (f32[]{:T(128)}, f32[]{:T(128)}) all-reduce(f32[]{:T(128)} %get-tuple-element.410, f32[]{:T(128)} %get-tuple-element.412), channel_id=1, replica_groups=mesh['dp'=8,'mp'=4] {'dp','mp'}, use_global_device_ids=true, to_apply=%region_54.55 | all-reduce | flops 2 | bytes 16 | tf_op jit(solution)/shard_map/psum | solution.py:312
  3395.5 15.7 copy_select_fusion
  (691 shorter events, 399.7 us)
Async XLA Ops:
  8.7 2062.1 %copy-start.110 = (f32[2]{0:T(128)}, f32[2]{0:T(128)S(1)}, u32[]{:S(2)}) copy-start(f32[2]{0:T(128)S(1)} %convert_element_type.199) | copy-start | bytes 28
  14.5 2157.2 %copy-start = (f32[2,192,768]{2,1,0:T(8,128)}, f32[2,192,768]{2,1,0:T(8,128)S(1)}, u32[]{:S(2)}) copy-start(f32[2,192,768]{2,1,0:T(8,128)S(1)} %get-tuple-element.408) | copy-start | bytes 3538948
  14.5 2082.0 %copy-start.75 = (f32[2,192]{1,0:T(2,128)}, f32[2,192]{1,0:T(2,128)S(1)}, u32[]{:S(2)}) copy-start(f32[2,192]{1,0:T(2,128)S(1)} %broadcast_multiply_fusion.3) | copy-start | bytes 4612
  14.9 2081.7 %copy-start.88 = (f32[2,192]{1,0:T(2,128)}, f32[2,192]{1,0:T(2,128)S(1)}, u32[]{:S(2)}) copy-start(f32[2,192]{1,0:T(2,128)S(1)} %fusion.188) | copy-start | bytes 4612
  17.1 2052.5 %copy-start.106 = (bf16[2,384]{1,0:T(2,128)(2,1)}, bf16[2,384]{1,0:T(2,128)(2,1)S(1)}, u32[]{:S(2)}) copy-start(bf16[2,384]{1,0:T(2,128)(2,1)S(1)} %get-tuple-element.401) | copy-start | bytes 4612
  17.4 2053.3 %copy-start.92 = (f32[2,768]{1,0:T(2,128)}, f32[2,768]{1,0:T(2,128)S(1)}, u32[]{:S(2)}) copy-start(f32[2,768]{1,0:T(2,128)S(1)} %select_reduce_fusion) | copy-start | bytes 18436
  17.4 78.6 %all-reduce.9.cloned.1.call-start = ((), (), s32[]{:S(2)}) async-start(), calls=%async_computation.24 | async-start | bytes 589824 | tf_op jit(solution)/shard_map/while/body/eval_jaxpr/psum | solution.py:31
  97.8 77.2 %all-reduce.9.cloned.1.call-start = ((), (), s32[]{:S(2)}) async-start(), calls=%async_computation.24 | async-start | bytes 589824 | tf_op jit(solution)/shard_map/while/body/eval_jaxpr/psum | solution.py:31
  176.6 77.2 %all-reduce.9.cloned.1.call-start = ((), (), s32[]{:S(2)}) async-start(), calls=%async_computation.24 | async-start | bytes 589824 | tf_op jit(solution)/shard_map/while/body/eval_jaxpr/psum | solution.py:31
  255.5 77.2 %all-reduce.9.cloned.1.call-start = ((), (), s32[]{:S(2)}) async-start(), calls=%async_computation.24 | async-start | bytes 589824 | tf_op jit(solution)/shard_map/while/body/eval_jaxpr/psum | solution.py:31
  334.4 77.2 %all-reduce.9.cloned.1.call-start = ((), (), s32[]{:S(2)}) async-start(), calls=%async_computation.24 | async-start | bytes 589824 | tf_op jit(solution)/shard_map/while/body/eval_jaxpr/psum | solution.py:31
  413.2 77.2 %all-reduce.9.cloned.1.call-start = ((), (), s32[]{:S(2)}) async-start(), calls=%async_computation.24 | async-start | bytes 589824 | tf_op jit(solution)/shard_map/while/body/eval_jaxpr/psum | solution.py:31
  492.1 77.2 %all-reduce.9.cloned.1.call-start = ((), (), s32[]{:S(2)}) async-start(), calls=%async_computation.24 | async-start | bytes 589824 | tf_op jit(solution)/shard_map/while/body/eval_jaxpr/psum | solution.py:31
  571.0 77.2 %all-reduce.9.cloned.1.call-start = ((), (), s32[]{:S(2)}) async-start(), calls=%async_computation.24 | async-start | bytes 589824 | tf_op jit(solution)/shard_map/while/body/eval_jaxpr/psum | solution.py:31
  649.9 77.2 %all-reduce.9.cloned.1.call-start = ((), (), s32[]{:S(2)}) async-start(), calls=%async_computation.24 | async-start | bytes 589824 | tf_op jit(solution)/shard_map/while/body/eval_jaxpr/psum | solution.py:31
  728.7 77.2 %all-reduce.9.cloned.1.call-start = ((), (), s32[]{:S(2)}) async-start(), calls=%async_computation.24 | async-start | bytes 589824 | tf_op jit(solution)/shard_map/while/body/eval_jaxpr/psum | solution.py:31
  807.6 77.2 %all-reduce.9.cloned.1.call-start = ((), (), s32[]{:S(2)}) async-start(), calls=%async_computation.24 | async-start | bytes 589824 | tf_op jit(solution)/shard_map/while/body/eval_jaxpr/psum | solution.py:31
  886.5 77.2 %all-reduce.9.cloned.1.call-start = ((), (), s32[]{:S(2)}) async-start(), calls=%async_computation.24 | async-start | bytes 589824 | tf_op jit(solution)/shard_map/while/body/eval_jaxpr/psum | solution.py:31
  965.3 77.2 %all-reduce.9.cloned.1.call-start = ((), (), s32[]{:S(2)}) async-start(), calls=%async_computation.24 | async-start | bytes 589824 | tf_op jit(solution)/shard_map/while/body/eval_jaxpr/psum | solution.py:31
  1044.2 77.2 %all-reduce.9.cloned.1.call-start = ((), (), s32[]{:S(2)}) async-start(), calls=%async_computation.24 | async-start | bytes 589824 | tf_op jit(solution)/shard_map/while/body/eval_jaxpr/psum | solution.py:31
  1123.1 77.2 %all-reduce.9.cloned.1.call-start = ((), (), s32[]{:S(2)}) async-start(), calls=%async_computation.24 | async-start | bytes 589824 | tf_op jit(solution)/shard_map/while/body/eval_jaxpr/psum | solution.py:31
  1202.0 77.2 %all-reduce.9.cloned.1.call-start = ((), (), s32[]{:S(2)}) async-start(), calls=%async_computation.24 | async-start | bytes 589824 | tf_op jit(solution)/shard_map/while/body/eval_jaxpr/psum | solution.py:31
  1280.9 77.2 %all-reduce.9.cloned.1.call-start = ((), (), s32[]{:S(2)}) async-start(), calls=%async_computation.24 | async-start | bytes 589824 | tf_op jit(solution)/shard_map/while/body/eval_jaxpr/psum | solution.py:31
  1359.8 77.2 %all-reduce.9.cloned.1.call-start = ((), (), s32[]{:S(2)}) async-start(), calls=%async_computation.24 | async-start | bytes 589824 | tf_op jit(solution)/shard_map/while/body/eval_jaxpr/psum | solution.py:31
  1438.6 77.2 %all-reduce.9.cloned.1.call-start = ((), (), s32[]{:S(2)}) async-start(), calls=%async_computation.24 | async-start | bytes 589824 | tf_op jit(solution)/shard_map/while/body/eval_jaxpr/psum | solution.py:31
  1517.5 77.2 %all-reduce.9.cloned.1.call-start = ((), (), s32[]{:S(2)}) async-start(), calls=%async_computation.24 | async-start | bytes 589824 | tf_op jit(solution)/shard_map/while/body/eval_jaxpr/psum | solution.py:31
  1596.4 77.2 %all-reduce.9.cloned.1.call-start = ((), (), s32[]{:S(2)}) async-start(), calls=%async_computation.24 | async-start | bytes 589824 | tf_op jit(solution)/shard_map/while/body/eval_jaxpr/psum | solution.py:31
  1675.2 77.2 %all-reduce.9.cloned.1.call-start = ((), (), s32[]{:S(2)}) async-start(), calls=%async_computation.24 | async-start | bytes 589824 | tf_op jit(solution)/shard_map/while/body/eval_jaxpr/psum | solution.py:31
  1754.1 77.2 %all-reduce.9.cloned.1.call-start = ((), (), s32[]{:S(2)}) async-start(), calls=%async_computation.24 | async-start | bytes 589824 | tf_op jit(solution)/shard_map/while/body/eval_jaxpr/psum | solution.py:31
  1833.0 77.2 %all-reduce.9.cloned.1.call-start = ((), (), s32[]{:S(2)}) async-start(), calls=%async_computation.24 | async-start | bytes 589824 | tf_op jit(solution)/shard_map/while/body/eval_jaxpr/psum | solution.py:31
  1911.9 77.2 %all-reduce.9.cloned.1.call-start = ((), (), s32[]{:S(2)}) async-start(), calls=%async_computation.24 | async-start | bytes 589824 | tf_op jit(solution)/shard_map/while/body/eval_jaxpr/psum | solution.py:31
  1990.7 77.2 %all-reduce.9.cloned.1.call-start = ((), (), s32[]{:S(2)}) async-start(), calls=%async_computation.24 | async-start | bytes 589824 | tf_op jit(solution)/shard_map/while/body/eval_jaxpr/psum | solution.py:31
  2069.6 51.7 %all-gather.8.cloned.1.call-start = ((), (), s32[]{:S(2)}) async-start(), calls=%async_computation.8 | async-start | bytes 2949120 | tf_op jit(solution)/shard_map/all_gather | solution.py:130
  2097.6 74.1 %reduce-scatter.13.cloned.1.call-start = ((), (), s32[]{:S(2)}) async-start(), calls=%async_computation.9 | async-start | bytes 2949120 | tf_op jit(solution)/shard_map/reduce_scatter | solution.py:134
  2138.7 59.7 %all-gather.10.cloned.1.call-start = ((), (), s32[]{:S(2)}) async-start(), calls=%async_computation.10 | async-start | bytes 2949120 | tf_op jit(solution)/shard_map/all_gather | solution.py:130
  2174.4 69.9 %reduce-scatter.15.cloned.1.call-start = ((), (), s32[]{:S(2)}) async-start(), calls=%async_computation.11 | async-start | bytes 2949120 | tf_op jit(solution)/shard_map/reduce_scatter | solution.py:134
  2211.3 60.9 %all-gather.12.cloned.1.call-start = ((), (), s32[]{:S(2)}) async-start(), calls=%async_computation.12 | async-start | bytes 2949120 | tf_op jit(solution)/shard_map/all_gather | solution.py:130
  2248.2 67.2 %reduce-scatter.17.cloned.1.call-start = ((), (), s32[]{:S(2)}) async-start(), calls=%async_computation.13 | async-start | bytes 2949120 | tf_op jit(solution)/shard_map/reduce_scatter | solution.py:134
  2282.3 66.3 %all-gather.14.cloned.1.call-start = ((), (), s32[]{:S(2)}) async-start(), calls=%async_computation.14 | async-start | bytes 2949120 | tf_op jit(solution)/shard_map/all_gather | solution.py:130
  2324.6 69.2 %reduce-scatter.19.cloned.1.call-start = ((), (), s32[]{:S(2)}) async-start(), calls=%async_computation.15 | async-start | bytes 2949120 | tf_op jit(solution)/shard_map/reduce_scatter | solution.py:134
  2360.7 64.5 %all-gather.16.cloned.1.call-start = ((), (), s32[]{:S(2)}) async-start(), calls=%async_computation.16 | async-start | bytes 2949120 | tf_op jit(solution)/shard_map/all_gather | solution.py:130
  2401.1 79.5 %reduce-scatter.21.cloned.1.call-start = ((), (), s32[]{:S(2)}) async-start(), calls=%async_computation.17 | async-start | bytes 2949120 | tf_op jit(solution)/shard_map/reduce_scatter | solution.py:134
  2447.5 65.3 %all-gather.18.cloned.1.call-start = ((), (), s32[]{:S(2)}) async-start(), calls=%async_computation.18 | async-start | bytes 2949120 | tf_op jit(solution)/shard_map/all_gather | solution.py:130
  2488.8 97.3 %reduce-scatter.23.cloned.1.call-start = ((), (), s32[]{:S(2)}) async-start(), calls=%async_computation.19 | async-start | bytes 2949120 | tf_op jit(solution)/shard_map/reduce_scatter | solution.py:134
  2553.0 61.3 %reduce-scatter.25.cloned.1.call-start = ((), (), s32[]{:S(2)}) async-start(), calls=%async_computation.22 | async-start | bytes 245760
  2594.5 44.9 %reduce-scatter.27.cloned.1.call-start = ((), (), s32[]{:S(2)}) async-start(), calls=%async_computation.23 | async-start | bytes 491520
  2618.6 149.9 %all-reduce.7.cloned.1.call-start = ((), (), s32[]{:S(2)}) async-start(), calls=%async_computation.21 | async-start | bytes 294912 | tf_op jit(solution)/shard_map/psum | solution.py:309
  2619.4 717.4 %all-reduce.5.cloned.1.call-start = ((), (), s32[]{:S(2)}) async-start(), calls=%async_computation.20 | async-start | bytes 37748736 | tf_op jit(solution)/shard_map/psum | solution.py:307
  (131 other events, 3364.5 us)
Sparse Core Ops, SparseCore 0:
  24.7 71.3 all-reduce.8
  104.9 69.9 all-reduce.8
  183.8 69.9 all-reduce.8
  262.7 69.9 all-reduce.8
  341.5 69.9 all-reduce.8
  420.4 69.9 all-reduce.8
  499.3 69.9 all-reduce.8
  578.2 69.9 all-reduce.8
  657.0 69.9 all-reduce.8
  735.9 69.9 all-reduce.8
  814.8 69.9 all-reduce.8
  893.7 69.9 all-reduce.8
  972.5 69.9 all-reduce.8
  1051.4 69.9 all-reduce.8
  1130.3 69.9 all-reduce.8
  1209.1 69.9 all-reduce.8
  1288.0 69.9 all-reduce.8
  1366.9 69.9 all-reduce.8
  1445.8 69.9 all-reduce.8
  1524.7 69.9 all-reduce.8
  1603.5 69.9 all-reduce.8
  1682.4 69.9 all-reduce.8
  1761.3 69.9 all-reduce.8
  1840.2 69.9 all-reduce.8
  1919.0 69.9 all-reduce.8
  1997.9 69.9 all-reduce.8
Sparse Core Ops, SparseCore 1:
  2097.7 23.6 all-gather.7
  2138.8 32.9 reduce-scatter.12
  2174.5 23.9 all-gather.9
  2211.4 32.9 reduce-scatter.14
  2248.3 23.9 all-gather.11
  2282.4 33.0 reduce-scatter.16
  2324.7 23.9 all-gather.13
  2360.8 32.9 reduce-scatter.18
  2401.2 23.9 all-gather.15
  2447.6 33.0 reduce-scatter.20
  2488.8 23.9 all-gather.17
  2553.1 32.9 reduce-scatter.22
  2594.6 19.7 reduce-scatter.24
  2618.7 20.7 reduce-scatter.26
  2645.0 123.4 all-reduce.6
  2772.6 564.1 all-reduce.4
where the time goes:
time: 3450 us; the launch traced here: 3430 us
  waiting for transfers between devices  2770 us (80%)
  local copies, waits for them, and re-layouts  219 us (6%)
  matrix products  128 us (4%)
  loops' own time  119 us (3%)
  other arithmetic  89.9 us (3%)
  blocking collectives  75.1 us (2%)
    psum x26, waiting for transfers between devices, broadcast(): return lax.psum(jnp.where(mine, array, jnp.zeros_like(array)), axis)  1820 us
    psum x1, waiting for transfers between devices, body(): summed = lax.psum(grads, 'dp')  567 us
    all_gather x6, waiting for transfers between devices, spread(): return lax.all_gather(values, 'mp', axis=1, tiled=True)  137 us
    reduce_scatter x6, waiting for transfers between devices, collect(): lax.psum_scatter(values.astype(jnp.bfloat16), 'mp', scatter_dimension=1,...  133 us
    another operation x1, loops' own time, body(): _, fetched = lax.scan(fetch_one, 0, jnp.arange(UNITS))  118 us
    dot_general x55, matrix products, matmul(): return jnp.einsum(form, left, right, preferred_element_type=single)  106 us
    psum x1, waiting for transfers between devices, body(): lax.psum((jnp.stack([grad_in_proj, grad_out_proj]), loss_local), ('dp', '...  76.2 us
  transfers between devices with their start and end apart: 42, of which 42 were waited for; matrix products, arithmetic and copies ran while one was open for 3% of the time, Pallas kernels for 0%

commit v1 on v0

v1 whole, which is shorter than its diff:
```python
import math

import jax
import jax.numpy as jnp
from jax import lax
from jax.experimental import pallas as pl
from jax.experimental.pallas import tpu as pltpu
from jax.sharding import Mesh
from jax.sharding import PartitionSpec as P

D = 768
HD = 64
C = 20
FRAMES = 768
NT = 1000
UNITS = 26
WIDE = 16

highest = lax.Precision.HIGHEST
beta_first = 0.9
beta_second = 0.999
adam_epsilon = 1e-08
learn_rate = 0.02
decay_rate = 0.1
clip_limit = 0.002
norm_epsilon = 1e-06
masked_score = -1e30
bfloat = jnp.bfloat16
single = jnp.float32


def swap(values, axis, bit=0):
    count = lax.axis_size(axis)
    return lax.ppermute(values, axis, [(i, i ^ (1 << bit)) for i in range(count)])


def dp_bits():
    return lax.axis_size("dp").bit_length() - 1


def step(values, which):
    return swap(values, "mx") if which == "x" else swap(values, "dp", which)


def gather_dp(values):
    values = values[None]
    for bit in range(dp_bits()):
        values = jnp.concatenate([values, swap(values, "dp", bit)], axis=0)
    return values


def flip(values, bit):
    shape = values.shape
    split = values.reshape((shape[0] >> (bit + 1), 2, 1 << bit) + shape[1:])
    return split[:, ::-1].reshape(shape)


def sum_dp(values, relative):
    for bit in range(dp_bits()):
        other = swap(values, "dp", bit)
        values = values + (flip(other, bit) if relative else other)
    return values


def scatter_sum_dp(values):
    for bit in reversed(range(dp_bits())):
        half = values.shape[0] // 2
        values = values[:half] + swap(values[half:], "dp", bit)
    return values[0]


def sum_mp(values):
    values = values + swap(values, "mc")
    return values + swap(values, "mx")


def pair(values, axis, name):
    other = swap(values, name)
    first = lax.axis_index(name) == 0
    return jnp.stack([jnp.where(first, values, other), jnp.where(first, other, values)], axis=axis)


def gather_units(chunk, order):
    pieces = chunk[None]
    for which in order:
        pieces = jnp.concatenate([pieces, step(pieces, which)], axis=0)
    bits = dp_bits()
    tail = chunk.shape
    pieces = pieces.reshape((2,) * (bits + 1) + tail)
    axis_of = {which: bits - i for i, which in enumerate(order)}
    perm = (
        [bits + 1, axis_of["x"], bits + 2]
        + [axis_of[bit] for bit in reversed(range(bits))]
        + [bits + 3, bits + 4]
    )
    return jnp.transpose(pieces, perm).reshape(tail[0], -1, tail[3])


def scatter_units(grads, order):
    bits = dp_bits()
    count, rows, depth = grads.shape
    small = rows // (6 << bits)
    pieces = grads.astype(bfloat).reshape((count, 2, 3) + (2,) * bits + (small, depth))
    axis_of = {bit: 3 + (bits - 1 - bit) for bit in range(bits)}
    axis_of["x"] = 1
    perm = [axis_of[which] for which in reversed(order)] + [0, 2, 3 + bits, 4 + bits]
    pieces = jnp.transpose(pieces, perm)
    for i, which in enumerate(reversed(order)):
        total = pieces[0].astype(single) + step(pieces[1], which).astype(single)
        pieces = total.astype(bfloat) if i < bits else total
    return pieces


def pick_kernel(ids, source, target):
    @pl.loop(0, target.shape[0])
    def _(i):
        target[i] = source[ids[i]]


def pick_blocks(source, ids):
    count = ids.shape[0]
    return pl.pallas_call(
        pick_kernel,
        out_shape=jax.ShapeDtypeStruct((count,) + source.shape[1:], source.dtype),
        grid_spec=pltpu.PrefetchScalarGridSpec(
            num_scalar_prefetch=1,
            grid=(),
            in_specs=[pl.BlockSpec(memory_space=pltpu.VMEM)],
            out_specs=pl.BlockSpec(memory_space=pltpu.VMEM),
        ),
        compiler_params=pltpu.CompilerParams(vmem_limit_bytes=40 << 20),
    )(ids.astype(jnp.int32), source)


def exchange_dp(blocks):
    count = lax.axis_size("dp")
    if count > 8:
        sent = jnp.stack([blocks(k) for k in range(count)])
        index = lax.axis_index("dp")
        ranked = pick_blocks(sent, jnp.arange(count) ^ index)
        got = lax.all_to_all(ranked, "dp", 0, 0, tiled=True)
        return pick_blocks(got, jnp.arange(count) ^ index)
    got = [blocks(0)] * count
    for k in reversed(range(1, count)):
        got[k] = lax.ppermute(blocks(k), "dp", [(i, i ^ k) for i in range(count)])
    return jnp.stack(got)


def normed(values):
    center = values - jnp.mean(values, axis=-1, keepdims=True)
    spread_sq = jnp.mean(center * center, axis=-1, keepdims=True)
    return center * lax.rsqrt(spread_sq + norm_epsilon)


def modulate(values, shift, scale):
    return normed(values) * (1.0 + scale[None, :]) + shift[None, :]


def modulate_back(values, shift, scale, grad):
    _, pullback = jax.vjp(modulate, values, shift, scale)
    return pullback(grad)


def adamw(weight, moment, square, grad, count):
    moment = beta_first * moment + (1.0 - beta_first) * grad
    square = beta_second * square + (1.0 - beta_second) * grad * grad
    first_fix = 1.0 - jnp.power(beta_first, count)
    second_fix = 1.0 - jnp.power(beta_second, count)
    update = (
        moment / first_fix / (jnp.sqrt(square / second_fix) + adam_epsilon) + decay_rate * weight
    )
    return (weight - learn_rate * update, moment, square)


def sinusoid(timestep):
    half_width = D // 2
    frequency = jnp.exp(-math.log(10000.0) * jnp.arange(half_width).astype(single) / half_width)
    angles = timestep.astype(single)[:, None] * frequency[None, :]
    return jnp.concatenate([jnp.cos(angles), jnp.sin(angles)], axis=1)


def matmul(form, left, right):
    return jnp.einsum(form, left, right, preferred_element_type=single)


def masked_scores(query, keys, mask):
    scores = matmul("fhk,ghk->hfg", query, keys) * HD ** (-0.5)
    if mask is None:
        return scores
    return jnp.where(mask[None, None, :], scores, masked_score)


def heads(values):
    return values.reshape(values.shape[0], -1, HD)


def merge(values):
    return values.reshape(values.shape[0], -1)


def attention(query, keys, values, mask):
    scores = masked_scores(heads(query), heads(keys), mask)
    row_max = jnp.max(scores, axis=-1, keepdims=True)
    shifted = jnp.exp(scores - row_max)
    row_total = jnp.sum(shifted, axis=-1, keepdims=True)
    probs = shifted / row_total
    output = matmul("hfg,ghk->fhk", probs.astype(bfloat), heads(values))
    return (merge(output.astype(bfloat)), (row_max + jnp.log(row_total))[..., 0])


def attention_back(query, keys, values, mask, grad_out, log_total):
    query, keys, values, grad_out = (heads(item) for item in (query, keys, values, grad_out))
    probs = jnp.exp(masked_scores(query, keys, mask) - log_total[..., None])
    grad_probs = matmul("fhk,ghk->hfg", grad_out, values)
    inner = jnp.sum(probs * grad_probs, axis=-1, keepdims=True)
    grad_scores = (probs * (grad_probs - inner)).astype(bfloat)
    grad_query = matmul("hfg,ghk->fhk", grad_scores, keys) * HD ** (-0.5)
    grad_keys = matmul("hfg,fhk->ghk", grad_scores, query) * HD ** (-0.5)
    grad_values = matmul("hfg,fhk->ghk", probs.astype(bfloat), grad_out)
    return tuple(merge(item.astype(bfloat)) for item in (grad_query, grad_keys, grad_values))


def spread(values):
    return jnp.concatenate([values, swap(values, "mc")], axis=0)


def collect(left, right):
    own = left.shape[0] // 2
    other = matmul("fk,kd->fd", left[own:], right).astype(bfloat)
    got = swap(other, "mc")
    return matmul("fk,kd->fd", left[:own], right) + got.astype(single)


def body(
    clean_latent,
    noise_draw,
    captions,
    caption_len,
    timestep,
    step_weight,
    step_count,
    unit_slot,
    master,
    first_moment,
    second_moment,
    latent_master,
    latent_first,
    latent_second,
):
    slots = master.shape[0]
    width = master.shape[1]
    n_dp = lax.axis_size("dp")
    index = lax.axis_index("dp")
    column = 2 * lax.axis_index("mx") + lax.axis_index("mc")
    clip = lax.axis_index("mx")
    clips = captions.shape[0]
    owner = unit_slot // slots
    place = unit_slot % slots
    local_ids = index * slots + jnp.arange(slots)
    pick = unit_slot[None, :] == local_ids[:, None]
    live_slot = jnp.any(pick, axis=1)

    master_low = master.astype(bfloat)
    split = master_low.reshape(slots, 3, n_dp, width // (3 * n_dp), D)

    def rows_of(k):
        return lax.dynamic_index_in_dim(split, index ^ k, 2, keepdims=False)

    got = exchange_dp(rows_of)
    got = got.reshape((n_dp * slots,) + got.shape[2:])
    where_at = (owner ^ index) * slots + place
    chunks = pick_blocks(got, where_at[:WIDE])
    z_bits = list(range(1, dp_bits()))
    order_y = z_bits + ["x", 0]
    order_x = z_bits + [0, "x"]
    orders = [order_y, order_x]
    halves = [(0, 1), (2, 3), (4, 5), (6, 7)]
    weights = [None] * WIDE
    for i, group in enumerate(halves):
        whole = gather_units(chunks[group[0] : group[-1] + 1], orders[i % 2])
        for j, u in enumerate(group):
            weights[u] = whole[j]

    far = lax.all_gather(chunks[8:], ("dp", "mx"))
    w_up = far[:, :4].reshape(8 * width, D)
    w_down = far[:, 4:].reshape(8 * width, D)

    table = jnp.arange(step_weight.shape[0])
    clip_weight = jnp.sum(
        jnp.where(timestep[:, None] == table[None, :], step_weight[None, :], 0.0), axis=1
    )
    cap_mask = jnp.arange(captions.shape[1])[None, :] < caption_len[:, None]
    pooled = (
        jnp.sum(jnp.where(cap_mask[:, :, None], captions.astype(single), 0.0), axis=1)
        / caption_len.astype(single)[:, None]
    )
    packed = jnp.concatenate(
        [sinusoid(timestep), pooled, jnp.broadcast_to(clip_weight[:, None], (clips, 128))], axis=1
    )
    packed = gather_dp(packed).reshape(n_dp * clips, -1)
    sinus_low = packed[:, :D].astype(bfloat)
    pooled_low = packed[:, D : 2 * D].astype(bfloat)
    weight_total = jnp.sum(packed[:, 2 * D])

    def held(u):
        return lax.dynamic_index_in_dim(master_low, place[u], 0, keepdims=False)

    zero = jnp.zeros((), bfloat)
    cond_part = matmul(
        "bd,ed->be", jnp.where(owner[24] == index, sinus_low, zero), held(24)
    ) + matmul("bd,ed->be", jnp.where(owner[25] == index, pooled_low, zero), held(25))
    cond_part = sum_dp(cond_part.reshape(n_dp, clips, width), True)
    cond = pair(pair(cond_part, 2, "mc"), 2, "mx").reshape(n_dp * clips, D)
    active = jax.nn.silu(cond).astype(bfloat)
    all_rows = matmul("bd,sed->bse", active, master_low)
    ada = pick[:, 16:24]
    rows = jnp.einsum("sj,bse->bje", ada.astype(single), all_rows, precision=highest)
    rows = scatter_sum_dp(rows.reshape(n_dp, clips, 8, width))
    mine = lax.dynamic_index_in_dim(rows, clip, 0, keepdims=False)
    theirs = swap(lax.dynamic_index_in_dim(rows, 1 - clip, 0, keepdims=False), "mx")
    by_x = jnp.stack(
        [jnp.where(clip == 0, mine, theirs), jnp.where(clip == 0, theirs, mine)], axis=1
    )
    modulation = pair(by_x, 2, "mc").reshape(8, D)

    text = lax.dynamic_index_in_dim(captions, clip, 0, keepdims=False)
    text_mask = lax.dynamic_index_in_dim(cap_mask, clip, 0, keepdims=False)
    my_step = lax.dynamic_index_in_dim(timestep, clip, 0, keepdims=False)
    my_weight = lax.dynamic_index_in_dim(clip_weight, clip, 0, keepdims=False)
    latents = jnp.stack([clean_latent, noise_draw], axis=1)
    away = swap(lax.dynamic_index_in_dim(latents, 1 - clip, 0, keepdims=False), "mx")
    latents = jnp.concatenate(
        [lax.dynamic_index_in_dim(latents, clip, 0, keepdims=False), away], axis=1
    )
    level = (my_step.astype(single) + 0.5) / NT
    noisy = (1.0 - level) * latents[0] + level * latents[1]
    target = latents[1] - latents[0]

    hidden_zero = jnp.einsum("fc,cd->fd", noisy, latent_master[0], precision=highest)
    first_in = spread(modulate(hidden_zero, modulation[0], modulation[1]).astype(bfloat))
    self_query, self_keys, self_values = (
        matmul("fd,ed->fe", first_in, weights[u]).astype(bfloat) for u in range(3)
    )
    self_flat, self_total = attention(self_query, self_keys, self_values, None)
    self_branch = collect(self_flat, weights[3])
    hidden_one = hidden_zero + modulation[2] * self_branch
    second_in = spread(normed(hidden_one).astype(bfloat))
    cross_query = matmul("fd,ed->fe", second_in, weights[4]).astype(bfloat)
    cross_keys = matmul("ld,ed->le", text, weights[5]).astype(bfloat)
    cross_values = matmul("ld,ed->le", text, weights[6]).astype(bfloat)
    cross_flat, cross_total = attention(cross_query, cross_keys, cross_values, text_mask)
    cross_branch = collect(cross_flat, weights[7])
    hidden_two = hidden_one + cross_branch
    third_in = spread(modulate(hidden_two, modulation[3], modulation[4]).astype(bfloat))
    upper = matmul("fd,kd->fk", third_in, w_up).astype(bfloat)
    upper_wide = upper.astype(single)
    activated = jax.nn.gelu(upper_wide, approximate=True).astype(bfloat)
    mlp_branch = collect(activated, w_down)
    hidden_three = hidden_two + modulation[5] * mlp_branch
    final_wide = modulate(hidden_three, modulation[6], modulation[7]).astype(bfloat).astype(single)
    predicted = jnp.einsum("fd,cd->fc", final_wide, latent_master[1], precision=highest)
    error = predicted - target
    loss_local = jnp.sum(my_weight * error * error)

    grad_pred = 2.0 / (C * FRAMES) * my_weight * error / weight_total
    grad_out_proj = jnp.einsum("fc,fd->cd", grad_pred, final_wide, precision=highest)
    grad_final = jnp.einsum("fc,cd->fd", grad_pred, latent_master[1], precision=highest)
    grad_three, shift_f, scale_f = modulate_back(
        hidden_three, modulation[6], modulation[7], grad_final
    )
    gate_m_grad = jnp.sum(grad_three * mlp_branch, axis=0)
    grad_mlp = spread((modulation[5] * grad_three).astype(bfloat))
    grad_act = matmul("fd,kd->fk", grad_mlp, w_down)
    _, gelu_back = jax.vjp(lambda inner_in: jax.nn.gelu(inner_in, approximate=True), upper_wide)
    grad_upper = gelu_back(grad_act)[0].astype(bfloat)
    sums = [None] * WIDE

    def reduce_pairs(first, grads):
        grads = grads.reshape(-1, 2 * width, D)
        for j in range(0, grads.shape[0], 2):
            done = scatter_units(grads[j : j + 2], orders[((first + j) // 2) % 2])
            sums[first + j], sums[first + j + 1] = done[0], done[1]

    grad_far = jnp.concatenate(
        [
            item.astype(bfloat).reshape((2 * n_dp, 4) + chunks.shape[1:])
            for item in (
                matmul("fk,fd->kd", grad_upper, third_in),
                matmul("fk,fd->kd", activated, grad_mlp),
            )
        ],
        axis=1,
    )
    far_sum = lax.psum_scatter(grad_far, ("dp", "mx"), scatter_dimension=0).astype(single)
    for u in range(8):
        sums[8 + u] = far_sum[u]
    grad_third = collect(grad_upper, w_up)
    grad_two, shift_m, scale_m = modulate_back(hidden_two, modulation[3], modulation[4], grad_third)
    grad_two = grad_two + grad_three
    grad_cross = spread(grad_two.astype(bfloat))
    grad_cross_flat = matmul("fd,kd->fk", grad_cross, weights[7]).astype(bfloat)
    grad_w_cross_out = matmul("fk,fd->kd", cross_flat, grad_cross)
    cq_grad, ck_grad, cv_grad = attention_back(
        cross_query, cross_keys, cross_values, text_mask, grad_cross_flat, cross_total
    )
    grad_w_cq = matmul("fk,fd->kd", cq_grad, second_in)
    grad_w_ck = matmul("lk,ld->kd", ck_grad, text)
    grad_w_cv = matmul("lk,ld->kd", cv_grad, text)
    reduce_pairs(4, jnp.concatenate([grad_w_cq, grad_w_ck, grad_w_cv, grad_w_cross_out], axis=0))
    grad_second = collect(cq_grad, weights[4])
    _, norm_back = jax.vjp(normed, hidden_one)
    grad_one = grad_two + norm_back(grad_second)[0]
    gate_a_grad = jnp.sum(grad_one * self_branch, axis=0)
    grad_self = spread((modulation[2] * grad_one).astype(bfloat))
    grad_self_flat = matmul("fd,kd->fk", grad_self, weights[3]).astype(bfloat)
    grad_w_self_out = matmul("fk,fd->kd", self_flat, grad_self)
    sq_grad, sk_grad, sv_grad = attention_back(
        self_query, self_keys, self_values, None, grad_self_flat, self_total
    )
    grad_proj = jnp.concatenate([sq_grad, sk_grad, sv_grad], axis=1)
    grad_w_attn = matmul("fk,fd->kd", grad_proj, first_in)
    reduce_pairs(0, jnp.concatenate([grad_w_attn, grad_w_self_out], axis=0))
    grad_first = collect(grad_proj, jnp.concatenate(weights[0:3], axis=0))
    grad_zero, shift_a, scale_a = modulate_back(
        hidden_zero, modulation[0], modulation[1], grad_first
    )
    grad_zero = grad_zero + grad_one
    grad_in_proj = jnp.einsum("fc,fd->cd", noisy, grad_zero, precision=highest)

    grad_mod = jnp.stack(
        [shift_a, scale_a, gate_a_grad, shift_m, scale_m, gate_m_grad, shift_f, scale_f], axis=0
    )
    grad_mod = (grad_mod + swap(grad_mod, "mc")).astype(bfloat)
    grad_mod = gather_dp(pair(grad_mod, 0, "mx")).reshape(n_dp * clips, 8, D)
    mod_cols = lax.dynamic_index_in_dim(
        grad_mod.reshape(n_dp * clips, 8, D // width, width), column, 2, keepdims=False
    )
    slot_mod = matmul("sj,bje->sbe", ada.astype(bfloat), mod_cols).astype(bfloat)
    grad_active = matmul("sbe,sed->bd", slot_mod, master_low).reshape(n_dp, clips, D)
    grad_active = sum_mp(sum_dp(grad_active, True)).reshape(n_dp * clips, D)
    _, silu_back = jax.vjp(jax.nn.silu, cond)
    grad_cond = silu_back(grad_active)[0].astype(bfloat)
    cond_cols = lax.dynamic_index_in_dim(
        grad_cond.reshape(n_dp * clips, D // width, width), column, 1, keepdims=False
    )
    is_time, is_pool = pick[:, 24], pick[:, 25]
    slot_out = jnp.where((is_time | is_pool)[:, None, None], cond_cols[None], slot_mod)
    slot_in = jnp.where(
        is_time[:, None, None],
        sinus_low[None],
        jnp.where(is_pool[:, None, None], pooled_low[None], active[None]),
    )
    slot_grad = matmul("sbe,sbd->sed", slot_out, slot_in)

    def gram(values):
        return matmul("bd,cd->bc", values, values)

    flat_mod = grad_mod.reshape(n_dp * clips, 8 * D)
    thin_square = jnp.sum(gram(active) * gram(flat_mod)) + jnp.sum(
        (gram(sinus_low) + gram(pooled_low)) * gram(grad_cond)
    )

    reduced = jnp.stack(sums)
    wide_square = jnp.sum(reduced * reduced)
    reduced_low = reduced.astype(bfloat)
    at_slot = jnp.argmax(
        unit_slot[None, :WIDE] == jnp.arange(n_dp * slots)[:, None], axis=1
    ).reshape(n_dp, slots)

    relative = jnp.arange(n_dp) ^ index
    routes = pick_blocks(reduced_low, at_slot[relative].reshape(-1))
    routes = routes.reshape((n_dp, slots) + routes.shape[1:])
    routed = exchange_dp(lambda k: routes[k])
    routed = pick_blocks(routed, relative)
    routed = jnp.transpose(routed, (1, 2, 0, 3, 4)).reshape(slots, width, D).astype(single)
    is_wide = jnp.any(pick[:, :WIDE], axis=1)
    owned = jnp.where(is_wide[:, None, None], routed, slot_grad)

    pad = jnp.zeros((2 * C, 128), single).at[0, 0].set(loss_local)
    small = jnp.concatenate(
        [jnp.concatenate([grad_in_proj, grad_out_proj], axis=0), pad], axis=1
    )
    small = sum_mp(sum_dp(small, False))
    latent_grad = small[:, :D].reshape(2, C, D)
    loss_sum = small[0, D]
    wide_total = sum_mp(sum_dp(jnp.broadcast_to(wide_square, (8, 128)), False))[0, 0]
    square_sum = wide_total + thin_square + jnp.sum(latent_grad * latent_grad)
    grad_norm = jnp.sqrt(square_sum)
    factor = clip_limit / jnp.maximum(grad_norm, clip_limit)
    count = step_count[0].astype(single)
    new_weight, new_moment, new_square = adamw(
        master, first_moment, second_moment, owned * factor, count
    )
    keep = live_slot[:, None, None]
    latent_weight, latent_moment, latent_square = adamw(
        latent_master, latent_first, latent_second, latent_grad * factor, count
    )
    loss_value = loss_sum / (C * FRAMES * weight_total)
    return (
        jnp.where(keep, new_weight, master),
        jnp.where(keep, new_moment, first_moment),
        jnp.where(keep, new_square, second_moment),
        latent_weight,
        latent_moment,
        latent_square,
        grad_norm,
        loss_value,
    )


def solution(mesh):
    n_dp, n_mp = mesh.shape["dp"], mesh.shape["mp"]
    fine = Mesh(mesh.devices.reshape(n_dp, n_mp // 2, 2), ("dp", "mx", "mc"))
    frames = P("dp", ("mx", "mc"), None)
    placed = (
        frames,
        frames,
        P("dp", None, None),
        P("dp"),
        P("dp"),
        P(),
        P(),
        P(),
        frames,
        frames,
        frames,
        P(),
        P(),
        P(),
    )
    return jax.shard_map(
        body,
        mesh=fine,
        in_specs=placed,
        out_specs=(frames, frames, frames, P(), P(), P(), P(), P()),
        check_vma=False,
    )
```

time: 3450 us -> 578 us (0.17)
  the two profiles are of different devices: /device:TPU:8 before, /device:TPU:0 now
where the time goes in v1:
time: 578 us; the launch traced here: 570 us
  waiting for transfers between devices  168 us (29%)
  matrix products  107 us (19%)
  starting transfers between devices  103 us (18%)
  local copies, waits for them, and re-layouts  84.4 us (15%)
  other arithmetic  75.1 us (13%)
  between operations  31 us (5%)
    ppermute x78, waiting for transfers between devices, swap(): return lax.ppermute(values, axis, [(i, i ^ 1 << bit) for i in range(count)])  141 us
    dot_general x53, matrix products, matmul(): return jnp.einsum(form, left, right, preferred_element_type=single)  98.7 us
    ppermute x78, starting transfers between devices, swap(): return lax.ppermute(values, axis, [(i, i ^ 1 << bit) for i in range(count)])  77.7 us
    unnamed x348, local copies, waits for them, and re-layouts  30.5 us
    ppermute x14, waiting for transfers between devices, exchange_dp(): got[k] = lax.ppermute(blocks(k), 'dp', [(i, i ^ k) for i in range(count)])  26.8 us
    ppermute x14, starting transfers between devices, exchange_dp(): got[k] = lax.ppermute(blocks(k), 'dp', [(i, i ^ k) for i in range(count)])  24.6 us
    concatenate x12, other arithmetic, gather_units(): pieces = jnp.concatenate([pieces, step(pieces, which)], axis=0)  15.9 us
  transfers between devices with their start and end apart: 94, of which 39 were waited for; matrix products, arithmetic and copies ran while one was open for 37% of the time, Pallas kernels for 0%

profile of v1, /device:TPU:0, one launch (start us, length us, event | category | flops | bytes accessed | tf_op | source)
XLA Modules:
  0.0 570.2 jit_solution(17803253495052320357)
XLA Ops:
  11.8 3.0 collective-permute-start.1
  20.4 3.5 collective-permute-start.21
  29.4 3.4 collective-permute-start.2
  32.9 3.0 collective-permute-done.2
  44.9 4.3 collective-permute-done.3
  55.7 3.1 collective-permute-start.5
  62.5 2.7 collective-permute-done.6
  67.2 3.4 collective-permute-done.8
  79.6 2.8 collective-permute-done.16
  82.3 3.3 collective-permute-start.17
  85.7 4.2 collective-permute-done.17
  129.7 3.7 collective-permute-done.32
  154.2 6.7 %collective-permute-done.24 = bf16[4,2,3,8,768]{4,3,2,1,0:T(8,128)(2,1)S(1)} collective-permute-done((bf16[4,2,3,8,768]{4,3,2,1,0:T(8,128)(2,1)S(1)}, bf16[4,2,3,8,768]{4,3,2,1,0:T(8,128)(2,1)S(1)}, u32[]{:S(2)}, u32[]{:S(2)}) %collective-permute-start.24) | collective-permute-done | bytes 294944 | tf_op jit(solution)/shard_map/ppermute | solution.py:34
  163.5 30.4 %collective-permute-done.29 = bf16[8,2,3,8,768]{4,3,2,1,0:T(8,128)(2,1)S(1)} collective-permute-done((bf16[8,2,3,8,768]{4,3,2,1,0:T(8,128)(2,1)S(1)}, bf16[8,2,3,8,768]{4,3,2,1,0:T(8,128)(2,1)S(1)}, u32[]{:S(2)}, u32[]{:S(2)}) %collective-permute-start.29) | collective-permute-done | bytes 589856 | tf_op jit(solution)/shard_map/ppermute | solution.py:34
  202.6 3.4 convolution_convert_fusion.18
  206.0 3.6 fusion.32
  215.0 2.8 fusion.186
  247.0 2.7 fusion.187
  249.7 6.3 %fusion.12 = (bf16[768,1536]{1,0:T(8,128)(2,1)S(1)}, bf16[768,1536]{1,0:T(8,128)(2,1)}) fusion(bf16[1536,768]{1,0:T(8,128)(2,1)S(1)} %bitcast.527, bf16[384,768]{1,0:T(8,128)(2,1)} %collective-permute-done.41, bf16[384,768]{1,0:T(8,128)(2,1)} %add_convert_fusion.1), kind=kOutput, calls=%fused_computation.23 | convolution fusion | flops 1827274752 | bytes 8257536 | tf_op jit(solution)/shard_map/fd,kd->fk/dot_general | solution.py:183
  271.7 3.5 fusion.184
  285.8 5.1 fusion.8
  292.1 3.0 convolution_convert_fusion
  300.6 3.3 convolution_convert_fusion.1
  312.1 3.5 fusion.47
  315.7 3.4 multiply_reduce_fusion.2
  329.7 13.8 %collective-permute-done.60 = bf16[2,2,2,2,3,8,768]{6,5,4,3,2,1,0:T(8,128)(2,1)S(1)} collective-permute-done((bf16[2,2,2,2,3,8,768]{6,5,4,3,2,1,0:T(8,128)(2,1)S(1)}, bf16[2,2,2,2,3,8,768]{6,5,4,3,2,1,0:T(8,128)(2,1)S(1)}, u32[]{:S(2)}, u32[]{:S(2)}) %collective-permute-start.60) | collective-permute-done | bytes 589856 | tf_op jit(solution)/shard_map/ppermute | solution.py:34
  351.5 3.1 collective-permute-done.61
  357.9 9.5 %collective-permute-done.62 = bf16[2,2,3,8,768]{4,3,2,1,0:T(8,128)(2,1)S(1)} collective-permute-done((bf16[2,2,3,8,768]{4,3,2,1,0:T(8,128)(2,1)S(1)}, bf16[2,2,3,8,768]{4,3,2,1,0:T(8,128)(2,1)S(1)}, u32[]{:S(2)}, u32[]{:S(2)}) %collective-permute-start.62) | collective-permute-done | bytes 147488 | tf_op jit(solution)/shard_map/ppermute | solution.py:34
  372.1 2.7 fusion.29
  374.8 6.7 %multiply_reduce_fusion = (f32[6,768]{1,0:T(8,128)S(1)}, f32[6,768,768]{1,2,0:T(8,128)}) fusion(f32[6,768,768]{1,2,0:T(8,128)S(1)} %bitcast.480, f32[6,768]{1,0:T(8,128)S(1)} %copy-done.87, bf16[768,6,64]{0,2,1:T(8,128)(2,1)S(1)} %bitcast.538, bf16[768,6,64]{0,2,1:T(8,128)(2,1)S(1)} %bitcast.571), kind=kOutput, calls=%fused_computation.2 | convolution fusion | flops 467136000 | bytes 29528064 | tf_op jit(solution)/shard_map/fhk,ghk->hfg/dot_general | solution.py:183
  381.5 7.4 %multiply_convert_fusion = bf16[6,768,768]{1,2,0:T(8,128)(2,1)S(1)} fusion(f32[6,768,768]{1,2,0:T(8,128)} %get-tuple-element.203, f32[6,768,768]{1,2,0:T(8,128)S(1)} %bitcast.480, f32[6,768]{1,0:T(8,128)S(1)} %get-tuple-element.202, f32[6,768]{1,0:T(8,128)S(1)} %copy-done.87), kind=kLoop, calls=%fused_computation.1 | loop fusion | flops 17694720 | bytes 35426304 | tf_op jit(solution)/shard_map/convert_element_type | solution.py:216
  402.3 2.8 multiply_reduce_fusion.3
  411.8 7.1 %collective-permute-done.52 = bf16[2,2,2,2,3,8,768]{6,5,4,3,2,1,0:T(8,128)(2,1)} collective-permute-done((bf16[2,2,2,2,3,8,768]{6,5,4,3,2,1,0:T(8,128)(2,1)}, bf16[2,2,2,2,3,8,768]{6,5,4,3,2,1,0:T(8,128)(2,1)}, u32[]{:S(2)}, u32[]{:S(2)}) %collective-permute-start.52) | collective-permute-done | bytes 589856 | tf_op jit(solution)/shard_map/ppermute | solution.py:34
  420.1 2.5 collective-permute-start.73
  427.7 8.2 %collective-permute-done.74 = bf16[1,2,8,768]{3,2,1,0:T(8,128)(2,1)S(1)} collective-permute-done((bf16[1,2,8,768]{3,2,1,0:T(8,128)(2,1)S(1)}, bf16[1,2,8,768]{3,2,1,0:T(8,128)(2,1)S(1)}, u32[]{:S(2)}, u32[]{:S(2)}) %collective-permute-start.74) | collective-permute-done | bytes 24608 | tf_op jit(solution)/shard_map/ppermute | solution.py:34
  440.4 2.6 collective-permute-start.76
  443.7 3.0 collective-permute-done.76
  454.5 3.8 collective-permute-done.88
  459.3 3.6 collective-permute-start.89
  467.2 8.3 %collective-permute-done.79 = f32[8,2,768]{2,0,1:T(8,128)S(1)} collective-permute-done((f32[8,2,768]{2,0,1:T(8,128)S(1)}, f32[8,2,768]{2,0,1:T(8,128)S(1)}, u32[]{:S(2)}, u32[]{:S(2)}) %collective-permute-start.79) | collective-permute-done | bytes 49184 | tf_op jit(solution)/shard_map/ppermute | solution.py:34
  478.7 7.4 %collective-permute-done.50 = bf16[2,2,3,8,768]{4,3,2,1,0:T(8,128)(2,1)S(1)} collective-permute-done((bf16[2,2,3,8,768]{4,3,2,1,0:T(8,128)(2,1)S(1)}, bf16[2,2,3,8,768]{4,3,2,1,0:T(8,128)(2,1)S(1)}, u32[]{:S(2)}, u32[]{:S(2)}) %collective-permute-start.50) | collective-permute-done | bytes 147488 | tf_op jit(solution)/shard_map/ppermute | solution.py:34
  489.3 2.7 collective-permute-done.51
  512.1 2.7 collective-permute-start.70
  516.6 3.2 collective-permute-start.67
  527.2 7.4 %collective-permute-done.65 = bf16[5,3,8,768]{3,2,1,0:T(8,128)(2,1)S(1)} collective-permute-done((bf16[5,3,8,768]{3,2,1,0:T(8,128)(2,1)S(1)}, bf16[5,3,8,768]{3,2,1,0:T(8,128)(2,1)S(1)}, u32[]{:S(2)}, u32[]{:S(2)}) %collective-permute-start.65) | collective-permute-done | bytes 184352 | tf_op jit(solution)/shard_map/ppermute | solution.py:145
  534.6 3.0 collective-permute-start.66
  537.6 11.8 %collective-permute-done.66 = bf16[5,3,8,768]{3,2,1,0:T(8,128)(2,1)S(1)} collective-permute-done((bf16[5,3,8,768]{3,2,1,0:T(8,128)(2,1)S(1)}, bf16[5,3,8,768]{3,2,1,0:T(8,128)(2,1)S(1)}, u32[]{:S(2)}, u32[]{:S(2)}) %collective-permute-start.66) | collective-permute-done | bytes 184352 | tf_op jit(solution)/shard_map/ppermute | solution.py:145
  554.8 6.0 %fusion.24 = (f32[5,192,768]{2,1,0:T(8,128)}, f32[5,192,768]{2,1,0:T(8,128)}, f32[5,192,768]{2,1,0:T(8,128)}) fusion(f32[5,192,768]{2,1,0:T(8,128)S(1)} %copy-done.146, pred[5]{0:T(512)(128)(4,1)S(1)} %copy-done.145, f32[5,192,768]{2,1,0:T(8,128)S(1)} %copy-done.22, f32[]{:T(128)} %bitcast.173, f32[]{:T(128)} %bitcast.172, ...), kind=kOutput, calls=%fused_computation.50 | convolution fusion | flops 38461440 | bytes 20748320 | tf_op jit(solution)/shard_map/sbe,sbd->sed/dot_general | solution.py:183
  (814 shorter events, 291.5 us)
Async XLA Ops:
  7.2 239.8 %all-gather.3.cloned.1.call-start = ((), (), s32[]{:S(2)}) async-start(), calls=%async_computation.2 | async-start | bytes 5013504 | tf_op jit(solution)/shard_map/all_gather | solution.py:284
  11.8 17.6 %collective-permute-start.1 = (f32[1,2,1664]{2,1,0:T(2,128)S(1)}, f32[1,2,1664]{2,1,0:T(2,128)S(1)}, u32[]{:S(2)}, u32[]{:S(2)}) collective-permute-start(f32[1,2,1664]{2,1,0:T(2,128)S(1)} %maximum_bitcast_fusion.1), channel_id=1, source_target_pairs={{0,4},{4,0},{8,12},{12,8},{16,20},{20,16},{24,28},{28,24},{1,5},{5... | collective-permute-start | bytes 39944 | tf_op jit(solution)/shard_map/ppermute | solution.py:34
  15.8 36.0 %collective-permute-start = (f32[2,192,20]{1,2,0:T(8,128)S(1)}, f32[2,192,20]{1,2,0:T(8,128)S(1)}, u32[]{:S(2)}, u32[]{:S(2)}) collective-permute-start(f32[2,192,20]{1,2,0:T(8,128)S(1)} %copy.324), channel_id=1, source_target_pairs={{0,2},{2,0},{1,3},{3,1},{4,6},{6,4},{5,7},{7,5},{8,10},{10,8},{9,1... | collective-permute-start | bytes 92168 | tf_op jit(solution)/shard_map/ppermute | solution.py:34
  20.4 73.0 %collective-permute-start.21 = (bf16[5,3,8,768]{3,2,1,0:T(8,128)(2,1)S(1)}, bf16[5,3,8,768]{3,2,1,0:T(8,128)(2,1)}, u32[]{:S(2)}, u32[]{:S(2)}) collective-permute-start(bf16[5,3,8,768]{3,2,1,0:T(8,128)(2,1)S(1)} %get-tuple-element.117), channel_id=1, source_target_pairs={{0,28},{4,24},{8,20},{12,16},{16,12},{20,8},{24,4},{28,0},{1,29},{... | collective-permute-start | bytes 552968 | tf_op jit(solution)/shard_map/ppermute | solution.py:145
  24.0 68.5 %collective-permute-start.20 = (bf16[5,3,8,768]{3,2,1,0:T(8,128)(2,1)S(1)}, bf16[5,3,8,768]{3,2,1,0:T(8,128)(2,1)}, u32[]{:S(2)}, u32[]{:S(2)}) collective-permute-start(bf16[5,3,8,768]{3,2,1,0:T(8,128)(2,1)S(1)} %get-tuple-element.118), channel_id=1, source_target_pairs={{0,24},{4,28},{8,16},{12,20},{16,8},{20,12},{24,0},{28,4},{1,25},{... | collective-permute-start | bytes 552968 | tf_op jit(solution)/shard_map/ppermute | solution.py:145
  24.2 67.3 %collective-permute-start.19 = (bf16[5,3,8,768]{3,2,1,0:T(8,128)(2,1)}, bf16[5,3,8,768]{3,2,1,0:T(8,128)(2,1)}, u32[]{:S(2)}, u32[]{:S(2)}) collective-permute-start(bf16[5,3,8,768]{3,2,1,0:T(8,128)(2,1)} %get-tuple-element.119), channel_id=1, source_target_pairs={{0,20},{4,16},{8,28},{12,24},{16,4},{20,0},{24,12},{28,8},{1,21},{... | collective-permute-start | bytes 552968 | tf_op jit(solution)/shard_map/ppermute | solution.py:145
  35.9 13.4 %collective-permute-start.3 = (f32[4,2,1664]{2,1,0:T(2,128)S(1)}, f32[4,2,1664]{2,1,0:T(2,128)S(1)}, u32[]{:S(2)}, u32[]{:S(2)}) collective-permute-start(f32[4,2,1664]{2,1,0:T(2,128)S(1)} %pad_maximum_fusion.42), channel_id=1, source_target_pairs={{0,16},{4,20},{8,24},{12,28},{16,0},{20,4},{24,8},{28,12},{1,17},{... | collective-permute-start | bytes 159752 | tf_op jit(solution)/shard_map/ppermute | solution.py:34
  49.2 41.3 %collective-permute-start.18 = (bf16[5,3,8,768]{3,2,1,0:T(8,128)(2,1)}, bf16[5,3,8,768]{3,2,1,0:T(8,128)(2,1)}, u32[]{:S(2)}, u32[]{:S(2)}) collective-permute-start(bf16[5,3,8,768]{3,2,1,0:T(8,128)(2,1)} %get-tuple-element.120), channel_id=1, source_target_pairs={{0,16},{4,20},{8,24},{12,28},{16,0},{20,4},{24,8},{28,12},{1,17},{... | collective-permute-start | bytes 552968 | tf_op jit(solution)/shard_map/ppermute | solution.py:145
  103.6 390.3 %reduce-scatter.2.cloned.1.call-start = ((), (), s32[]{:S(2)}) async-start(), calls=%async_computation.1 | async-start | bytes 5013504 | tf_op jit(solution)/shard_map/reduce_scatter | solution.py:394
  107.2 11.4 %collective-permute-start.22 = (bf16[1,2,3,8,768]{4,3,2,1,0:T(8,128)(2,1)}, bf16[1,2,3,8,768]{4,3,2,1,0:T(8,128)(2,1)S(1)}, u32[]{:S(2)}, u32[]{:S(2)}) collective-permute-start(bf16[1,2,3,8,768]{4,3,2,1,0:T(8,128)(2,1)} %get-tuple-element.143), channel_id=1, source_target_pairs={{0,8},{4,12},{8,0},{12,4},{16,24},{20,28},{24,16},{28,20},{1,9},{5... | collective-permute-start | bytes 221192 | tf_op jit(solution)/shard_map/ppermute | solution.py:34
  108.7 14.1 %collective-permute-start.12 = (f32[8,192]{1,0:T(8,128)S(1)}, f32[8,192]{1,0:T(8,128)S(1)}, u32[]{:S(2)}, u32[]{:S(2)}) collective-permute-start(f32[8,192]{1,0:T(8,128)S(1)} %dynamic-slice_bitcast_fusion.7), channel_id=1, source_target_pairs={{0,2},{2,0},{1,3},{3,1},{4,6},{6,4},{5,7},{7,5},{8,10},{10,8},{9,1... | collective-permute-start | bytes 18440 | tf_op jit(solution)/shard_map/ppermute | solution.py:34
  110.9 22.6 %collective-permute-start.32 = (bf16[2,2,3,8,768]{4,3,2,1,0:T(8,128)(2,1)}, bf16[2,2,3,8,768]{4,3,2,1,0:T(8,128)(2,1)}, u32[]{:S(2)}, u32[]{:S(2)}) collective-permute-start(bf16[2,2,3,8,768]{4,3,2,1,0:T(8,128)(2,1)} %pad_maximum_fusion.37), channel_id=1, source_target_pairs={{0,16},{4,20},{8,24},{12,28},{16,0},{20,4},{24,8},{28,12},{1,17},{... | collective-permute-start | bytes 442376 | tf_op jit(solution)/shard_map/ppermute | solution.py:34
  114.1 21.0 %collective-permute-start.37 = (bf16[2,2,3,8,768]{4,3,2,1,0:T(8,128)(2,1)}, bf16[2,2,3,8,768]{4,3,2,1,0:T(8,128)(2,1)}, u32[]{:S(2)}, u32[]{:S(2)}) collective-permute-start(bf16[2,2,3,8,768]{4,3,2,1,0:T(8,128)(2,1)} %pad_maximum_fusion.38), channel_id=1, source_target_pairs={{0,16},{4,20},{8,24},{12,28},{16,0},{20,4},{24,8},{28,12},{1,17},{... | collective-permute-start | bytes 442376 | tf_op jit(solution)/shard_map/ppermute | solution.py:34
  117.0 20.7 %collective-permute-start.27 = (bf16[2,2,3,8,768]{4,3,2,1,0:T(8,128)(2,1)}, bf16[2,2,3,8,768]{4,3,2,1,0:T(8,128)(2,1)}, u32[]{:S(2)}, u32[]{:S(2)}) collective-permute-start(bf16[2,2,3,8,768]{4,3,2,1,0:T(8,128)(2,1)} %pad_maximum_fusion.36), channel_id=1, source_target_pairs={{0,16},{4,20},{8,24},{12,28},{16,0},{20,4},{24,8},{28,12},{1,17},{... | collective-permute-start | bytes 442376 | tf_op jit(solution)/shard_map/ppermute | solution.py:34
  120.3 19.4 %collective-permute-start.23 = (bf16[2,2,3,8,768]{4,3,2,1,0:T(8,128)(2,1)}, bf16[2,2,3,8,768]{4,3,2,1,0:T(8,128)(2,1)}, u32[]{:S(2)}, u32[]{:S(2)}) collective-permute-start(bf16[2,2,3,8,768]{4,3,2,1,0:T(8,128)(2,1)} %pad_maximum_fusion.35), channel_id=1, source_target_pairs={{0,16},{4,20},{8,24},{12,28},{16,0},{20,4},{24,8},{28,12},{1,17},{... | collective-permute-start | bytes 442376 | tf_op jit(solution)/shard_map/ppermute | solution.py:34
  129.5 66.0 %collective-permute-start.14 = (bf16[384,768]{1,0:T(8,128)(2,1)}, bf16[384,768]{1,0:T(8,128)(2,1)S(1)}, u32[]{:S(2)}, u32[]{:S(2)}) collective-permute-start(bf16[384,768]{1,0:T(8,128)(2,1)} %add_convert_fusion.2), channel_id=1, source_target_pairs={{0,1},{1,0},{2,3},{3,2},{4,5},{5,4},{6,7},{7,6},{8,9},{9,8},{10,11... | collective-permute-start | bytes 1769480 | tf_op jit(solution)/shard_map/ppermute | solution.py:34
  134.5 12.4 %collective-permute-start.33 = (bf16[4,2,3,8,768]{4,3,2,1,0:T(8,128)(2,1)S(1)}, bf16[4,2,3,8,768]{4,3,2,1,0:T(8,128)(2,1)S(1)}, u32[]{:S(2)}, u32[]{:S(2)}) collective-permute-start(bf16[4,2,3,8,768]{4,3,2,1,0:T(8,128)(2,1)S(1)} %pad_maximum_fusion.32), channel_id=1, source_target_pairs={{0,4},{4,0},{8,12},{12,8},{16,20},{20,16},{24,28},{28,24},{1,5},{5... | collective-permute-start | bytes 884744 | tf_op jit(solution)/shard_map/ppermute | solution.py:34
  136.2 13.5 %collective-permute-start.38 = (bf16[4,2,3,8,768]{4,3,2,1,0:T(8,128)(2,1)S(1)}, bf16[4,2,3,8,768]{4,3,2,1,0:T(8,128)(2,1)S(1)}, u32[]{:S(2)}, u32[]{:S(2)}) collective-permute-start(bf16[4,2,3,8,768]{4,3,2,1,0:T(8,128)(2,1)S(1)} %pad_maximum_fusion.33), channel_id=1, source_target_pairs={{0,2},{2,0},{1,3},{3,1},{4,6},{6,4},{5,7},{7,5},{8,10},{10,8},{9,1... | collective-permute-start | bytes 884744 | tf_op jit(solution)/shard_map/ppermute | solution.py:34
  138.7 13.8 %collective-permute-start.28 = (bf16[4,2,3,8,768]{4,3,2,1,0:T(8,128)(2,1)S(1)}, bf16[4,2,3,8,768]{4,3,2,1,0:T(8,128)(2,1)S(1)}, u32[]{:S(2)}, u32[]{:S(2)}) collective-permute-start(bf16[4,2,3,8,768]{4,3,2,1,0:T(8,128)(2,1)S(1)} %pad_maximum_fusion.31), channel_id=1, source_target_pairs={{0,4},{4,0},{8,12},{12,8},{16,20},{20,16},{24,28},{28,24},{1,5},{5... | collective-permute-start | bytes 884744 | tf_op jit(solution)/shard_map/ppermute | solution.py:34
  140.7 20.2 %collective-permute-start.24 = (bf16[4,2,3,8,768]{4,3,2,1,0:T(8,128)(2,1)S(1)}, bf16[4,2,3,8,768]{4,3,2,1,0:T(8,128)(2,1)S(1)}, u32[]{:S(2)}, u32[]{:S(2)}) collective-permute-start(bf16[4,2,3,8,768]{4,3,2,1,0:T(8,128)(2,1)S(1)} %pad_maximum_fusion.30), channel_id=1, source_target_pairs={{0,2},{2,0},{1,3},{3,1},{4,6},{6,4},{5,7},{7,5},{8,10},{10,8},{9,1... | collective-permute-start | bytes 884744 | tf_op jit(solution)/shard_map/ppermute | solution.py:34
  148.7 62.5 %collective-permute-start.34 = (bf16[8,2,3,8,768]{4,3,2,1,0:T(8,128)(2,1)}, bf16[8,2,3,8,768]{4,3,2,1,0:T(8,128)(2,1)}, u32[]{:S(2)}, u32[]{:S(2)}) collective-permute-start(bf16[8,2,3,8,768]{4,3,2,1,0:T(8,128)(2,1)} %pad_maximum_fusion.28), channel_id=1, source_target_pairs={{0,2},{2,0},{1,3},{3,1},{4,6},{6,4},{5,7},{7,5},{8,10},{10,8},{9,1... | collective-permute-start | bytes 1769480 | tf_op jit(solution)/shard_map/ppermute | solution.py:34
  151.4 68.2 %collective-permute-start.39 = (bf16[8,2,3,8,768]{4,3,2,1,0:T(8,128)(2,1)}, bf16[8,2,3,8,768]{4,3,2,1,0:T(8,128)(2,1)}, u32[]{:S(2)}, u32[]{:S(2)}) collective-permute-start(bf16[8,2,3,8,768]{4,3,2,1,0:T(8,128)(2,1)} %pad_maximum_fusion.29), channel_id=1, source_target_pairs={{0,4},{4,0},{8,12},{12,8},{16,20},{20,16},{24,28},{28,24},{1,5},{5... | collective-permute-start | bytes 1769480 | tf_op jit(solution)/shard_map/ppermute | solution.py:34
  153.5 40.4 %collective-permute-start.29 = (bf16[8,2,3,8,768]{4,3,2,1,0:T(8,128)(2,1)S(1)}, bf16[8,2,3,8,768]{4,3,2,1,0:T(8,128)(2,1)S(1)}, u32[]{:S(2)}, u32[]{:S(2)}) collective-permute-start(bf16[8,2,3,8,768]{4,3,2,1,0:T(8,128)(2,1)S(1)} %pad_maximum_fusion.27), channel_id=1, source_target_pairs={{0,2},{2,0},{1,3},{3,1},{4,6},{6,4},{5,7},{7,5},{8,10},{10,8},{9,1... | collective-permute-start | bytes 1769480 | tf_op jit(solution)/shard_map/ppermute | solution.py:34
  161.8 32.1 %collective-permute-start.25 = (bf16[8,2,3,8,768]{4,3,2,1,0:T(8,128)(2,1)S(1)}, bf16[8,2,3,8,768]{4,3,2,1,0:T(8,128)(2,1)S(1)}, u32[]{:S(2)}, u32[]{:S(2)}) collective-permute-start(bf16[8,2,3,8,768]{4,3,2,1,0:T(8,128)(2,1)S(1)} %pad_maximum_fusion.26), channel_id=1, source_target_pairs={{0,4},{4,0},{8,12},{12,8},{16,20},{20,16},{24,28},{28,24},{1,5},{5... | collective-permute-start | bytes 1769480 | tf_op jit(solution)/shard_map/ppermute | solution.py:34
  258.0 13.7 %collective-permute-start.42 = (bf16[384,768]{1,0:T(8,128)(2,1)}, bf16[384,768]{1,0:T(8,128)(2,1)}, u32[]{:S(2)}, u32[]{:S(2)}) collective-permute-start(bf16[384,768]{1,0:T(8,128)(2,1)} %convolution_convert_fusion.5), channel_id=1, source_target_pairs={{0,1},{1,0},{2,3},{3,2},{4,5},{5,4},{6,7},{7,6},{8,9},{9,8},{10,11... | collective-permute-start | bytes 1769480 | tf_op jit(solution)/shard_map/ppermute | solution.py:34
  324.5 19.0 %collective-permute-start.60 = (bf16[2,2,2,2,3,8,768]{6,5,4,3,2,1,0:T(8,128)(2,1)S(1)}, bf16[2,2,2,2,3,8,768]{6,5,4,3,2,1,0:T(8,128)(2,1)S(1)}, u32[]{:S(2)}, u32[]{:S(2)}) collective-permute-start(bf16[2,2,2,2,3,8,768]{6,5,4,3,2,1,0:T(8,128)(2,1)S(1)} %slice_bitcast_fusion), channel_id=1, source_target_pairs={{0,2},{2,0},{1,3},{3,1},{4,6},{6,4},{5,7},{7,5},{8,10},{10,8},{9,1... | collective-permute-start | bytes 1769480 | tf_op jit(solution)/shard_map/ppermute | solution.py:34
  328.2 17.2 %collective-permute-start.56 = (bf16[2,2,2,2,3,8,768]{6,5,4,3,2,1,0:T(8,128)(2,1)S(1)}, bf16[2,2,2,2,3,8,768]{6,5,4,3,2,1,0:T(8,128)(2,1)S(1)}, u32[]{:S(2)}, u32[]{:S(2)}) collective-permute-start(bf16[2,2,2,2,3,8,768]{6,5,4,3,2,1,0:T(8,128)(2,1)S(1)} %slice_bitcast_fusion.2), channel_id=1, source_target_pairs={{0,4},{4,0},{8,12},{12,8},{16,20},{20,16},{24,28},{28,24},{1,5},{5... | collective-permute-start | bytes 1769480 | tf_op jit(solution)/shard_map/ppermute | solution.py:34
  329.7 17.1 %collective-permute-start.46 = (bf16[384,768]{1,0:T(8,128)(2,1)S(1)}, bf16[384,768]{1,0:T(8,128)(2,1)S(1)}, u32[]{:S(2)}, u32[]{:S(2)}) collective-permute-start(bf16[384,768]{1,0:T(8,128)(2,1)S(1)} %convolution_convert_fusion.13), channel_id=1, source_target_pairs={{0,1},{1,0},{2,3},{3,2},{4,5},{5,4},{6,7},{7,6},{8,9},{9,8},{10,11... | collective-permute-start | bytes 1769480 | tf_op jit(solution)/shard_map/ppermute | solution.py:34
  343.7 10.9 %collective-permute-start.61 = (bf16[2,2,2,3,8,768]{5,4,3,2,1,0:T(8,128)(2,1)S(1)}, bf16[2,2,2,3,8,768]{5,4,3,2,1,0:T(8,128)(2,1)S(1)}, u32[]{:S(2)}, u32[]{:S(2)}) collective-permute-start(bf16[2,2,2,3,8,768]{5,4,3,2,1,0:T(8,128)(2,1)S(1)} %slice_bitcast_fusion.8), channel_id=1, source_target_pairs={{0,4},{4,0},{8,12},{12,8},{16,20},{20,16},{24,28},{28,24},{1,5},{5... | collective-permute-start | bytes 884744 | tf_op jit(solution)/shard_map/ppermute | solution.py:34
  351.4 19.9 %collective-permute-start.47 = (bf16[384,768]{1,0:T(8,128)(2,1)S(1)}, bf16[384,768]{1,0:T(8,128)(2,1)S(1)}, u32[]{:S(2)}, u32[]{:S(2)}) collective-permute-start(bf16[384,768]{1,0:T(8,128)(2,1)S(1)} %multiply_convert_fusion.2), channel_id=1, source_target_pairs={{0,1},{1,0},{2,3},{3,2},{4,5},{5,4},{6,7},{7,6},{8,9},{9,8},{10,11... | collective-permute-start | bytes 1769480 | tf_op jit(solution)/shard_map/ppermute | solution.py:34
  354.7 12.6 %collective-permute-start.62 = (bf16[2,2,3,8,768]{4,3,2,1,0:T(8,128)(2,1)S(1)}, bf16[2,2,3,8,768]{4,3,2,1,0:T(8,128)(2,1)S(1)}, u32[]{:S(2)}, u32[]{:S(2)}) collective-permute-start(bf16[2,2,3,8,768]{4,3,2,1,0:T(8,128)(2,1)S(1)} %slice_bitcast_fusion.17), channel_id=1, source_target_pairs={{0,16},{4,20},{8,24},{12,28},{16,0},{20,4},{24,8},{28,12},{1,17},{... | collective-permute-start | bytes 442376 | tf_op jit(solution)/shard_map/ppermute | solution.py:34
  355.4 15.1 %collective-permute-start.58 = (bf16[2,2,3,8,768]{4,3,2,1,0:T(8,128)(2,1)S(1)}, bf16[2,2,3,8,768]{4,3,2,1,0:T(8,128)(2,1)S(1)}, u32[]{:S(2)}, u32[]{:S(2)}) collective-permute-start(bf16[2,2,3,8,768]{4,3,2,1,0:T(8,128)(2,1)S(1)} %slice_bitcast_fusion.19), channel_id=1, source_target_pairs={{0,16},{4,20},{8,24},{12,28},{16,0},{20,4},{24,8},{28,12},{1,17},{... | collective-permute-start | bytes 442376 | tf_op jit(solution)/shard_map/ppermute | solution.py:34
  368.1 124.8 %collective-permute-start.63 = (bf16[2,3,8,768]{3,2,1,0:T(8,128)(2,1)}, bf16[2,3,8,768]{3,2,1,0:T(8,128)(2,1)}, u32[]{:S(2)}, u32[]{:S(2)}) collective-permute-start(bf16[2,3,8,768]{3,2,1,0:T(8,128)(2,1)} %slice_bitcast_fusion.25), channel_id=1, source_target_pairs={{0,8},{4,12},{8,0},{12,4},{16,24},{20,28},{24,16},{28,20},{1,9},{5... | collective-permute-start | bytes 221192 | tf_op jit(solution)/shard_map/ppermute | solution.py:34
  371.3 120.7 %collective-permute-start.59 = (bf16[2,3,8,768]{3,2,1,0:T(8,128)(2,1)}, bf16[2,3,8,768]{3,2,1,0:T(8,128)(2,1)}, u32[]{:S(2)}, u32[]{:S(2)}) collective-permute-start(bf16[2,3,8,768]{3,2,1,0:T(8,128)(2,1)} %slice_bitcast_fusion.27), channel_id=1, source_target_pairs={{0,8},{4,12},{8,0},{12,4},{16,24},{20,28},{24,16},{28,20},{1,9},{5... | collective-permute-start | bytes 221192 | tf_op jit(solution)/shard_map/ppermute | solution.py:34
  399.3 19.5 %collective-permute-start.52 = (bf16[2,2,2,2,3,8,768]{6,5,4,3,2,1,0:T(8,128)(2,1)}, bf16[2,2,2,2,3,8,768]{6,5,4,3,2,1,0:T(8,128)(2,1)}, u32[]{:S(2)}, u32[]{:S(2)}) collective-permute-start(bf16[2,2,2,2,3,8,768]{6,5,4,3,2,1,0:T(8,128)(2,1)} %slice_bitcast_fusion.4), channel_id=1, source_target_pairs={{0,2},{2,0},{1,3},{3,1},{4,6},{6,4},{5,7},{7,5},{8,10},{10,8},{9,1... | collective-permute-start | bytes 1769480 | tf_op jit(solution)/shard_map/ppermute | solution.py:34
  402.0 24.4 %collective-permute-start.48 = (bf16[2,2,2,2,3,8,768]{6,5,4,3,2,1,0:T(8,128)(2,1)}, bf16[2,2,2,2,3,8,768]{6,5,4,3,2,1,0:T(8,128)(2,1)}, u32[]{:S(2)}, u32[]{:S(2)}) collective-permute-start(bf16[2,2,2,2,3,8,768]{6,5,4,3,2,1,0:T(8,128)(2,1)} %slice_bitcast_fusion.6), channel_id=1, source_target_pairs={{0,4},{4,0},{8,12},{12,8},{16,20},{20,16},{24,28},{28,24},{1,5},{5... | collective-permute-start | bytes 1769480 | tf_op jit(solution)/shard_map/ppermute | solution.py:34
  407.7 12.4 %collective-permute-start.72 = (f32[8,768]{1,0:T(8,128)}, f32[8,768]{1,0:T(8,128)S(1)}, u32[]{:S(2)}, u32[]{:S(2)}) collective-permute-start(f32[8,768]{1,0:T(8,128)} %stack.159), channel_id=1, source_target_pairs={{0,1},{1,0},{2,3},{3,2},{4,5},{5,4},{6,7},{7,6},{8,9},{9,8},{10,11... | collective-permute-start | bytes 73736 | tf_op jit(solution)/shard_map/ppermute | solution.py:34
  418.9 21.5 %collective-permute-start.87 = (f32[40,896]{1,0:T(8,128)S(1)}, f32[40,896]{1,0:T(8,128)S(1)}, u32[]{:S(2)}, u32[]{:S(2)}) collective-permute-start(f32[40,896]{1,0:T(8,128)S(1)} %select_maximum_fusion), channel_id=1, source_target_pairs={{0,4},{4,0},{8,12},{12,8},{16,20},{20,16},{24,28},{28,24},{1,5},{5... | collective-permute-start | bytes 430088 | tf_op jit(solution)/shard_map/ppermute | solution.py:34
  424.4 34.9 %collective-permute-start.53 = (bf16[2,2,2,3,8,768]{5,4,3,2,1,0:T(8,128)(2,1)}, bf16[2,2,2,3,8,768]{5,4,3,2,1,0:T(8,128)(2,1)}, u32[]{:S(2)}, u32[]{:S(2)}) collective-permute-start(bf16[2,2,2,3,8,768]{5,4,3,2,1,0:T(8,128)(2,1)} %slice_bitcast_fusion.12), channel_id=1, source_target_pairs={{0,4},{4,0},{8,12},{12,8},{16,20},{20,16},{24,28},{28,24},{1,5},{5... | collective-permute-start | bytes 884744 | tf_op jit(solution)/shard_map/ppermute | solution.py:34
  440.1 25.9 %collective-permute-start.49 = (bf16[2,2,2,3,8,768]{5,4,3,2,1,0:T(8,128)(2,1)S(1)}, bf16[2,2,2,3,8,768]{5,4,3,2,1,0:T(8,128)(2,1)S(1)}, u32[]{:S(2)}, u32[]{:S(2)}) collective-permute-start(bf16[2,2,2,3,8,768]{5,4,3,2,1,0:T(8,128)(2,1)S(1)} %slice_bitcast_fusion.14), channel_id=1, source_target_pairs={{0,2},{2,0},{1,3},{3,1},{4,6},{6,4},{5,7},{7,5},{8,10},{10,8},{9,1... | collective-permute-start | bytes 884744 | tf_op jit(solution)/shard_map/ppermute | solution.py:34
  459.3 17.6 %collective-permute-start.89 = (f32[40,896]{1,0:T(8,128)S(1)}, f32[40,896]{1,0:T(8,128)S(1)}, u32[]{:S(2)}, u32[]{:S(2)}) collective-permute-start(f32[40,896]{1,0:T(8,128)S(1)} %add.566), channel_id=1, source_target_pairs={{0,16},{4,20},{8,24},{12,28},{16,0},{20,4},{24,8},{28,12},{1,17},{... | collective-permute-start | bytes 430088 | tf_op jit(solution)/shard_map/ppermute | solution.py:34
  463.9 14.6 %collective-permute-start.54 = (bf16[2,2,3,8,768]{4,3,2,1,0:T(8,128)(2,1)S(1)}, bf16[2,2,3,8,768]{4,3,2,1,0:T(8,128)(2,1)S(1)}, u32[]{:S(2)}, u32[]{:S(2)}) collective-permute-start(bf16[2,2,3,8,768]{4,3,2,1,0:T(8,128)(2,1)S(1)} %slice_bitcast_fusion.21), channel_id=1, source_target_pairs={{0,16},{4,20},{8,24},{12,28},{16,0},{20,4},{24,8},{28,12},{1,17},{... | collective-permute-start | bytes 442376 | tf_op jit(solution)/shard_map/ppermute | solution.py:34
  478.6 19.3 %collective-permute-start.90 = (f32[40,896]{1,0:T(8,128)S(1)}, f32[40,896]{1,0:T(8,128)S(1)}, u32[]{:S(2)}, u32[]{:S(2)}) collective-permute-start(f32[40,896]{1,0:T(8,128)S(1)} %add.567), channel_id=1, source_target_pairs={{0,1},{1,0},{2,3},{3,2},{4,5},{5,4},{6,7},{7,6},{8,9},{9,8},{10,11... | collective-permute-start | bytes 430088 | tf_op jit(solution)/shard_map/ppermute | solution.py:34
  512.1 38.3 %collective-permute-start.70 = (bf16[5,3,8,768]{3,2,1,0:T(8,128)(2,1)S(1)}, bf16[5,3,8,768]{3,2,1,0:T(8,128)(2,1)S(1)}, u32[]{:S(2)}, u32[]{:S(2)}) collective-permute-start(bf16[5,3,8,768]{3,2,1,0:T(8,128)(2,1)S(1)} %get-tuple-element.110), channel_id=1, source_target_pairs={{0,28},{4,24},{8,20},{12,16},{16,12},{20,8},{24,4},{28,0},{1,29},{... | collective-permute-start | bytes 552968 | tf_op jit(solution)/shard_map/ppermute | solution.py:145
  514.8 35.6 %collective-permute-start.69 = (bf16[5,3,8,768]{3,2,1,0:T(8,128)(2,1)S(1)}, bf16[5,3,8,768]{3,2,1,0:T(8,128)(2,1)S(1)}, u32[]{:S(2)}, u32[]{:S(2)}) collective-permute-start(bf16[5,3,8,768]{3,2,1,0:T(8,128)(2,1)S(1)} %get-tuple-element.111), channel_id=1, source_target_pairs={{0,24},{4,28},{8,16},{12,20},{16,8},{20,12},{24,0},{28,4},{1,25},{... | collective-permute-start | bytes 552968 | tf_op jit(solution)/shard_map/ppermute | solution.py:145
  516.4 33.9 %collective-permute-start.68 = (bf16[5,3,8,768]{3,2,1,0:T(8,128)(2,1)S(1)}, bf16[5,3,8,768]{3,2,1,0:T(8,128)(2,1)S(1)}, u32[]{:S(2)}, u32[]{:S(2)}) collective-permute-start(bf16[5,3,8,768]{3,2,1,0:T(8,128)(2,1)S(1)} %get-tuple-element.112), channel_id=1, source_target_pairs={{0,20},{4,16},{8,28},{12,24},{16,4},{20,0},{24,12},{28,8},{1,21},{... | collective-permute-start | bytes 552968 | tf_op jit(solution)/shard_map/ppermute | solution.py:145
  516.6 32.8 %collective-permute-start.67 = (bf16[5,3,8,768]{3,2,1,0:T(8,128)(2,1)S(1)}, bf16[5,3,8,768]{3,2,1,0:T(8,128)(2,1)}, u32[]{:S(2)}, u32[]{:S(2)}) collective-permute-start(bf16[5,3,8,768]{3,2,1,0:T(8,128)(2,1)S(1)} %get-tuple-element.113), channel_id=1, source_target_pairs={{0,16},{4,20},{8,24},{12,28},{16,0},{20,4},{24,8},{28,12},{1,17},{... | collective-permute-start | bytes 552968 | tf_op jit(solution)/shard_map/ppermute | solution.py:145
  534.6 14.8 %collective-permute-start.66 = (bf16[5,3,8,768]{3,2,1,0:T(8,128)(2,1)S(1)}, bf16[5,3,8,768]{3,2,1,0:T(8,128)(2,1)S(1)}, u32[]{:S(2)}, u32[]{:S(2)}) collective-permute-start(bf16[5,3,8,768]{3,2,1,0:T(8,128)(2,1)S(1)} %get-tuple-element.114), channel_id=1, source_target_pairs={{0,12},{4,8},{8,4},{12,0},{16,28},{20,24},{24,20},{28,16},{1,13},{... | collective-permute-start | bytes 552968 | tf_op jit(solution)/shard_map/ppermute | solution.py:145
  (204 other events, 1630.3 us)
Sparse Core Ops, SparseCore 0:
  103.7 106.3 all-gather.2
  306.6 151.8 reduce-scatter.1

commit v2 on v1

v2 whole, which is shorter than its diff:
```python
import functools
import math

import jax
import jax.numpy as jnp
from jax import lax
from jax.experimental import pallas as pl
from jax.experimental.pallas import tpu as pltpu
from jax.sharding import Mesh
from jax.sharding import PartitionSpec as P

D = 768
HD = 64
C = 20
FRAMES = 768
NT = 1000
UNITS = 26
WIDE = 16

highest = lax.Precision.HIGHEST
beta_first = 0.9
beta_second = 0.999
adam_epsilon = 1e-08
learn_rate = 0.02
decay_rate = 0.1
clip_limit = 0.002
norm_epsilon = 1e-06
masked_score = -1e30
bfloat = jnp.bfloat16
single = jnp.float32


def swap(values, axis, bit=0):
    count = lax.axis_size(axis)
    return lax.ppermute(values, axis, [(i, i ^ (1 << bit)) for i in range(count)])


def dp_bits():
    return lax.axis_size("dp").bit_length() - 1


def step(values, which):
    return swap(values, "mx") if which == "x" else swap(values, "dp", which)


def gather_dp(values):
    values = values[None]
    for bit in range(dp_bits()):
        values = jnp.concatenate([values, swap(values, "dp", bit)], axis=0)
    return values


def sum_dp(values):
    for bit in range(dp_bits()):
        values = values + swap(values, "dp", bit)
    return values


def sum_mp(values):
    values = values + swap(values, "mc")
    return values + swap(values, "mx")


def pair(values, axis, name):
    other = swap(values, name)
    first = lax.axis_index(name) == 0
    return jnp.stack([jnp.where(first, values, other), jnp.where(first, other, values)], axis=axis)


def tie(*values):
    return lax.optimization_barrier(values)


def high():
    return lax.axis_size("dp") // 2


def shift(values, by):
    count = lax.axis_size("dp")
    return lax.ppermute(values, "dp", [(i, (i + 2 * by) % count) for i in range(count)])


class Gather:
    def __init__(self, chunk=None):
        self.ring, self.pieces, self.done, self.got = [chunk], None, [], None

    def send_ring(self):
        last = len(self.ring) == 3
        for _ in range(high() - 4 if last else 0):
            self.ring.append(shift(self.ring[-1], 1))
        self.got = shift(self.ring[-1], 1)

    def closed(self):
        return len(self.ring) == high()

    def send(self, which):
        self.done.append(which)
        self.got = step(self.pieces, which)

    def take(self, got):
        if self.pieces is not None:
            self.pieces = jnp.stack([self.pieces, got])
            return
        self.ring.append(got)
        if self.closed():
            self.pieces = jnp.stack(self.ring)

    def halves(self):
        units = self.pieces.shape[1] // 2
        parts = tie(self.pieces[:, :units], self.pieces[:, units:])
        both = Gather(), Gather()
        for part, pieces in zip(both, parts):
            part.pieces = pieces
        return both

    def laid(self):
        x, y = (0, 1) if self.done[-1] == "x" else (1, 0)
        pieces = jnp.transpose(self.pieces, [3, x, 4, 2, y, 5, 6])
        return pieces.reshape(pieces.shape[0], -1, D)


class Scatter:
    def __init__(self, pieces):
        self.pieces, self.got, self.steps = pieces, None, 0

    def send(self, which):
        self.got = step(self.pieces[1], which)

    def send_ring(self):
        if self.steps == 2:
            self.sum = self.pieces[1]
        last = self.steps == 4
        for _ in range(high() - 4 if last else 0):
            self.got = shift(self.sum, 1)
            self.add_ring(self.got)
        self.got = shift(self.sum, 1)

    def add_ring(self, got):
        self.steps += 1
        own = self.pieces[(self.steps - 1) % high()]
        self.sum = (own.astype(single) + got.astype(single)).astype(bfloat)

    def take(self, got):
        if self.steps < 2:
            self.steps += 1
            self.pieces = (self.pieces[0].astype(single) + got.astype(single)).astype(bfloat)
        else:
            self.add_ring(got)

    def join(self, other):
        both = Scatter(jnp.concatenate([self.pieces, other.pieces], axis=1))
        both.steps = 2
        return both


def cut_units(grads, x_first):
    count, rows, depth = grads.shape
    pieces = grads.astype(bfloat).reshape(count, 2, 3, high(), 2, -1, depth)
    perm = [1, 4, 3, 0, 2, 5, 6] if x_first else [4, 1, 3, 0, 2, 5, 6]
    return jnp.transpose(pieces, perm)


def cut_far(grads, tail, x_first):
    pieces = grads.astype(bfloat).reshape((2, 2, high(), 4) + tail)
    return pieces if x_first else pieces.swapaxes(0, 1)


def land(anchor, *streams):
    held = tie(anchor, *(stream.got for stream in streams))
    for stream, got in zip(streams, held[1:]):
        stream.take(got)
    return held[0]


WHOLE = pl.BlockSpec(memory_space=pltpu.VMEM)


def pick_kernel(ids, source, *targets):
    first = 0
    for target in targets:

        @pl.loop(0, target.shape[0])
        def _(i, first=first, target=target):
            target[i] = source[ids[first + i]]

        first += target.shape[0]


def pick_blocks(source, ids, counts):
    return pl.pallas_call(
        pick_kernel,
        out_shape=[
            jax.ShapeDtypeStruct((size,) + source.shape[1:], source.dtype) for size in counts
        ],
        grid_spec=pltpu.PrefetchScalarGridSpec(
            num_scalar_prefetch=1,
            grid=(),
            in_specs=[WHOLE],
            out_specs=[WHOLE] * len(counts),
        ),
        compiler_params=pltpu.CompilerParams(vmem_limit_bytes=40 << 20),
    )(ids.astype(jnp.int32), source)


def place_kernel(n_in, sizes, to, *refs):
    first = 0
    for source in refs[:n_in]:

        @pl.loop(0, source.shape[0])
        def _(i, first=first, source=source):
            unit = to[first + i]
            start = 0
            for target, size in zip(refs[n_in:], sizes):

                @pl.when((unit >= start) & (unit < start + size))
                def _(start=start, target=target):
                    target[unit - start] = source[i]

                start += size

        first += source.shape[0]


def place_blocks(sources, to, sizes):
    tail = sources[0].shape[1:]
    return pl.pallas_call(
        functools.partial(place_kernel, len(sources), sizes),
        out_shape=[jax.ShapeDtypeStruct((size,) + tail, sources[0].dtype) for size in sizes],
        grid_spec=pltpu.PrefetchScalarGridSpec(
            num_scalar_prefetch=1,
            grid=(),
            in_specs=[WHOLE] * len(sources),
            out_specs=[WHOLE] * len(sizes),
        ),
        compiler_params=pltpu.CompilerParams(vmem_limit_bytes=40 << 20),
    )(to.astype(jnp.int32), *sources)


def route_kernel(count, slots, ids, source, square, *targets):
    lane = lax.broadcasted_iota(jnp.int32, targets[0].shape[1:], 1)
    rest = square[0:1, 0:1]
    parts = []
    for _ in range(3):
        parts.append(rest.astype(bfloat).astype(single))
        rest = rest - parts[-1]
    told = jnp.where(lane < 128, parts[0], jnp.where(lane < 256, parts[1], parts[2]))
    for k, target in enumerate(targets):
        for s in range(slots):
            for h in range(3):
                target[3 * s + h] = source[ids[k * slots + s], h]
        target[3 * slots] = told.astype(bfloat)


def route_blocks(source, ids, square, count):
    slots = ids.shape[0] // count
    shape = (3 * slots + 1,) + source.shape[2:]
    return pl.pallas_call(
        functools.partial(route_kernel, count, slots),
        out_shape=[jax.ShapeDtypeStruct(shape, source.dtype)] * count,
        grid_spec=pltpu.PrefetchScalarGridSpec(
            num_scalar_prefetch=1,
            grid=(),
            in_specs=[WHOLE, WHOLE],
            out_specs=[WHOLE] * count,
        ),
        compiler_params=pltpu.CompilerParams(vmem_limit_bytes=40 << 20),
    )(ids.astype(jnp.int32), source, square)


def exchange_dp(blocks):
    count = lax.axis_size("dp")
    if count != 8:
        relative = jnp.arange(count) ^ lax.axis_index("dp")
        ranked = pick_blocks(jnp.stack(blocks), relative, (count,))[0]
        got = lax.all_to_all(ranked, "dp", 0, 0, tiled=True)
        got = pick_blocks(got, relative, (count,))[0]
        return [got.reshape((-1,) + got.shape[2:])]
    got = [blocks[0]] * count
    for k in (7, 6, 5, 4, 1, 2, 3):
        got[k] = lax.ppermute(blocks[k], "dp", [(i, i ^ k) for i in range(count)])
    return got


def adamw(weight, moment, square, grad, first_fix, second_fix):
    moment = beta_first * moment + (1.0 - beta_first) * grad
    square = beta_second * square + (1.0 - beta_second) * grad * grad
    update = (moment / first_fix) / (
        jnp.sqrt(square / second_fix) + adam_epsilon
    ) + decay_rate * weight
    return (weight - learn_rate * update, moment, square)


def adam_kernel(n_src, me, kind, scalars, *refs):
    routed, told, refs = refs[:n_src], refs[n_src : 2 * n_src], refs[2 * n_src :]
    slot_out, slot_in, weight, moment, square, latent_grad, *refs = refs
    latents, (new_weight, new_moment, new_square), refs = refs[:3], refs[3:6], refs[6:]
    new_latents, norm_out, grads = refs[:3], refs[3], refs[4]
    per, rows = routed[0].shape[0], routed[0].shape[2]
    squares = []
    for item in told:
        for j in range(per):
            parts = [item[j, 0, 0:1, 128 * i : 128 * i + 1].astype(single) for i in range(3)]
            squares.append(parts[0] + parts[1] + parts[2])
    while len(squares) > 1:
        squares = [squares[i] + squares[i + 1] for i in range(0, len(squares), 2)]
    norm = jnp.sqrt(squares[0] + scalars[0])
    factor = clip_limit / jnp.maximum(norm, clip_limit)

    @pl.when(pl.program_id(0) == 0)
    def _():
        norm_out[...] = jnp.broadcast_to(norm, norm_out.shape)
        held = [item[...] for item in latents]
        fresh = adamw(*held, latent_grad[...] * factor[None], scalars[1], scalars[2])
        for target, item in zip(new_latents, fresh):
            target[...] = item

    for i in range(n_src):
        for j in range(per):
            at = pl.multiple_of(((i * per + j) ^ me[0]) * rows, rows)
            for h in range(3):
                grads[h, pl.ds(at, rows), :] = routed[i][j, h].astype(single)
    sort = kind[pl.program_id(0)]
    for h in range(3):
        thin = lax.dot_general(
            slot_out[0, h], slot_in[0], (((0,), (0,)), ((), ())), preferred_element_type=single
        )
        grad = jnp.where(sort == 1, grads[h], thin) * factor
        w, m, v = weight[0, h], moment[0, h], square[0, h]
        fresh_w, fresh_m, fresh_v = adamw(w, m, v, grad, scalars[1], scalars[2])
        new_weight[0, h] = jnp.where(sort == 0, w, fresh_w)
        new_moment[0, h] = jnp.where(sort == 0, m, fresh_m)
        new_square[0, h] = jnp.where(sort == 0, v, fresh_v)


def adam_places(me, kind, scalars, routed, slot_out, slot_in, held, latent_grad, latents):
    slots, width, depth = held[0].shape
    head = width // 3
    clips = slot_in.shape[1]
    rows = routed[0].shape[1]
    routed = [item.reshape((-1, 3 * slots + 1, rows, depth)) for item in routed]
    per = routed[0].shape[0]
    big = pl.BlockSpec((1, 3, head, depth), lambda s, *_: (s, 0, 0, 0))
    small = pl.BlockSpec(latent_grad.shape, lambda s, *_: (0, 0, 0))
    out = pl.pallas_call(
        functools.partial(adam_kernel, len(routed)),
        out_shape=[jax.ShapeDtypeStruct((slots, 3, head, depth), single)] * 3
        + [jax.ShapeDtypeStruct(item.shape, single) for item in latents]
        + [jax.ShapeDtypeStruct((8, 128), single)],
        grid_spec=pltpu.PrefetchScalarGridSpec(
            num_scalar_prefetch=3,
            grid=(slots,),
            in_specs=[pl.BlockSpec((per, 3, rows, depth), lambda s, *_: (0, s, 0, 0))]
            * len(routed)
            + [pl.BlockSpec((per, 1, rows, depth), lambda s, *_: (0, 3 * slots, 0, 0))]
            * len(routed)
            + [
                pl.BlockSpec((1, 3, clips, head), lambda s, *_: (s, 0, 0, 0)),
                pl.BlockSpec((1, clips, depth), lambda s, *_: (s, 0, 0)),
                big,
                big,
                big,
            ]
            + [small] * 4,
            out_specs=[big] * 3 + [small] * 3 + [pl.BlockSpec((8, 128), lambda s, *_: (0, 0))],
            scratch_shapes=[pltpu.VMEM((3, head, depth), single)],
        ),
        compiler_params=pltpu.CompilerParams(vmem_limit_bytes=40 << 20),
    )(
        me,
        kind,
        scalars,
        *routed,
        *routed,
        slot_out.reshape(slots, clips, 3, head).swapaxes(1, 2),
        slot_in,
        *(item.reshape(slots, 3, head, depth) for item in held),
        latent_grad,
        *latents,
    )
    places = [item.reshape(slots, width, depth) for item in out[:3]]
    return places + list(out[3:6]) + [out[6][0, 0]]


def normed(values):
    center = values - jnp.mean(values, axis=-1, keepdims=True)
    spread_sq = jnp.mean(center * center, axis=-1, keepdims=True)
    return center * lax.rsqrt(spread_sq + norm_epsilon)


def modulate(values, shift, scale):
    return normed(values) * (1.0 + scale[None, :]) + shift[None, :]


def modulate_back(values, shift, scale, grad):
    _, pullback = jax.vjp(modulate, values, shift, scale)
    return pullback(grad)


def sinusoid(timestep):
    half_width = D // 2
    frequency = jnp.exp(-math.log(10000.0) * jnp.arange(half_width).astype(single) / half_width)
    angles = timestep.astype(single)[:, None] * frequency[None, :]
    return jnp.concatenate([jnp.cos(angles), jnp.sin(angles)], axis=1)


def matmul(form, left, right):
    return jnp.einsum(form, left, right, preferred_element_type=single)


NT_DIMS = (((1,), (1,)), ((), ()))
TN_DIMS = (((0,), (0,)), ((), ()))


def dot(left, right, dims=(((1,), (0,)), ((), ()))):
    return lax.dot_general(left, right, dims, preferred_element_type=single)


def scores_of(keys, query, length):
    scores = dot(keys, query, NT_DIMS) * HD ** (-0.5)
    if length is None:
        return scores
    row = lax.broadcasted_iota(jnp.int32, scores.shape, 0)
    return jnp.where(row < length, scores, masked_score)


def attend_kernel(masked, length, query, keys, values, output, totals):
    limit = length[0] if masked else None
    rows = []
    for h in range(2):
        at = slice(h * HD, (h + 1) * HD)
        scores = scores_of(keys[:, at], query[:, at], limit)
        top = jnp.max(scores, axis=0, keepdims=True)
        shifted = jnp.exp(scores - top)
        total = jnp.sum(shifted, axis=0, keepdims=True)
        probs = (shifted * (1.0 / total)).astype(bfloat)
        rows.append(dot(values[:, at], probs, TN_DIMS))
        totals[0, h : h + 1, :] = top + jnp.log(total)
    output[...] = jnp.concatenate(rows, axis=0).T.astype(bfloat)


def attend_back_kernel(masked, length, query, keys, values, grad_out, totals, dq, dk, dv):
    limit = length[0] if masked else None
    query_rows, key_cols, value_cols = [], [], []
    for h in range(2):
        at = slice(h * HD, (h + 1) * HD)
        q, k, v, do = query[:, at], keys[:, at], values[:, at], grad_out[:, at]
        probs = jnp.exp(scores_of(k, q, limit) - totals[0, h : h + 1, :])
        grad_probs = dot(v, do, NT_DIMS)
        inner = jnp.sum(probs * grad_probs, axis=0, keepdims=True)
        grad_scores = (probs * (grad_probs - inner)).astype(bfloat)
        query_rows.append(dot(k, grad_scores, TN_DIMS))
        key_cols.append(dot(grad_scores, q))
        value_cols.append(dot(probs.astype(bfloat), do))
    scale = HD ** (-0.5)
    dq[...] = (jnp.concatenate(query_rows, axis=0).T * scale).astype(bfloat)
    dk[...] = (jnp.concatenate(key_cols, axis=1) * scale).astype(bfloat)
    dv[...] = jnp.concatenate(value_cols, axis=1).astype(bfloat)


def pair_call(kernel, length, ins, outs, flops):
    def spec(shape):
        if len(shape) == 3:
            return pl.BlockSpec((1,) + shape[1:], lambda i, *_: (i, 0, 0))
        return pl.BlockSpec((shape[0], 2 * HD), lambda i, *_: (0, i))

    masked = length is not None
    length = jnp.zeros((1,), jnp.int32) if length is None else length.reshape(1)
    return pl.pallas_call(
        functools.partial(kernel, masked),
        out_shape=outs,
        grid_spec=pltpu.PrefetchScalarGridSpec(
            num_scalar_prefetch=1,
            grid=(ins[0].shape[1] // (2 * HD),),
            in_specs=[spec(item.shape) for item in ins],
            out_specs=[spec(item.shape) for item in outs],
        ),
        compiler_params=pltpu.CompilerParams(vmem_limit_bytes=48 << 20),
        cost_estimate=pl.CostEstimate(
            flops=flops, bytes_accessed=8 << 20, transcendentals=6 * FRAMES * FRAMES
        ),
    )(length, *ins)


def attention(query, keys, values, length):
    shape = query.shape
    outs = [
        jax.ShapeDtypeStruct(shape, bfloat),
        jax.ShapeDtypeStruct((shape[1] // (2 * HD), 2, shape[0]), single),
    ]
    flops = 16 * shape[0] * keys.shape[0] * shape[1]
    return pair_call(attend_kernel, length, (query, keys, values), outs, flops)


def attention_back(query, keys, values, length, grad_out, totals):
    outs = [jax.ShapeDtypeStruct(item.shape, bfloat) for item in (query, keys, values)]
    flops = 40 * query.shape[0] * keys.shape[0] * query.shape[1]
    ins = (query, keys, values, grad_out, totals)
    return pair_call(attend_back_kernel, length, ins, outs, flops)


def spread(values):
    return jnp.concatenate([values, swap(values, "mc")], axis=0)


def collect(left, right):
    own = left.shape[0] // 2
    other = matmul("fk,kd->fd", left[own:], right).astype(bfloat)
    got = swap(other, "mc")
    return matmul("fk,kd->fd", left[:own], right) + got.astype(single)


def body(
    clean_latent,
    noise_draw,
    captions,
    caption_len,
    timestep,
    step_weight,
    step_count,
    unit_slot,
    master,
    first_moment,
    second_moment,
    latent_master,
    latent_first,
    latent_second,
):
    slots = master.shape[0]
    width = master.shape[1]
    n_dp = lax.axis_size("dp")
    index = lax.axis_index("dp")
    column = 2 * lax.axis_index("mx") + lax.axis_index("mc")
    clip = lax.axis_index("mx")
    clips = captions.shape[0]
    owner = unit_slot // slots
    place = unit_slot % slots
    local_ids = index * slots + jnp.arange(slots)
    pick = unit_slot[None, :] == local_ids[:, None]
    live_slot = jnp.any(pick, axis=1)

    table = jnp.arange(step_weight.shape[0])
    clip_weight = jnp.sum(
        jnp.where(timestep[:, None] == table[None, :], step_weight[None, :], 0.0), axis=1
    )
    cap_mask = jnp.arange(captions.shape[1])[None, :] < caption_len[:, None]
    pooled = (
        jnp.sum(jnp.where(cap_mask[:, :, None], captions.astype(single), 0.0), axis=1)
        / caption_len.astype(single)[:, None]
    )
    packed = jnp.concatenate(
        [sinusoid(timestep), pooled, jnp.broadcast_to(clip_weight[:, None], (clips, 128))], axis=1
    )

    master_low = master.astype(bfloat)
    split = master_low.reshape(slots, 3, n_dp, width // (3 * n_dp), D)
    blocks = [
        lax.dynamic_index_in_dim(split, index ^ k, 2, keepdims=False) for k in range(n_dp)
    ]
    got = exchange_dp(blocks)
    unit_of = jnp.sum(
        jnp.where(
            unit_slot[None, :] == jnp.arange(n_dp * slots)[:, None],
            jnp.arange(UNITS)[None, :] + 1,
            0,
        ),
        axis=1,
    ) - 1
    table = jnp.stack(
        [
            unit_of.reshape(n_dp, slots)[jnp.array([d ^ k for k in range(n_dp)])]
            for d in range(n_dp)
        ]
    )
    unit_at = lax.dynamic_index_in_dim(table, index, 0, keepdims=False).reshape(-1)
    chunk_self, chunk_cross, chunk_far = place_blocks(got, unit_at, (4, 4, 8))
    unit_tail = chunk_far.shape[1:]
    chunk_self, packed = tie(chunk_self, packed)
    near, cross, far = Gather(chunk_self), Gather(chunk_cross), Gather(chunk_far)

    near.send_ring()
    packed = packed[None]
    for bit in range(dp_bits()):
        packed = jnp.concatenate([packed, swap(packed, "dp", bit)], axis=0)
        if bit < 3:
            packed = land(packed, near)
            if bit < 2:
                near.send_ring()
    near_a, near_b = near.halves()
    near_a.pieces, near_b.pieces, cross.ring[0] = tie(
        near_a.pieces, near_b.pieces, cross.ring[0]
    )
    near_a.send(0)
    near_b.send("x")
    cross.send_ring()
    packed = packed.reshape(n_dp * clips, -1)
    sinus_low = packed[:, :D].astype(bfloat)
    pooled_low = packed[:, D : 2 * D].astype(bfloat)
    weight_total = jnp.sum(packed[:, 2 * D])

    def held(u):
        return lax.dynamic_index_in_dim(master_low, place[u], 0, keepdims=False)

    zero = jnp.zeros((), bfloat)
    cond_part = matmul(
        "bd,ed->be", jnp.where(owner[24] == index, sinus_low, zero), held(24)
    ) + matmul("bd,ed->be", jnp.where(owner[25] == index, pooled_low, zero), held(25))
    row = jnp.arange(n_dp * clips)
    reorder = (row[:, None] ^ (index * clips)) == row[None, :]
    reorder = reorder.astype(single)

    def reordered(values):
        return jnp.einsum("bc,cd->bd", reorder, values, precision=highest)

    cond_part = reordered(cond_part)
    cond_part = cond_part + swap(cond_part, "dp", 0)
    for bit in range(1, dp_bits()):
        cond_part = cond_part + swap(cond_part, "dp", bit)
        if bit == 1:
            cond_part = land(cond_part, near_a, near_b, cross)
            near_a.send("x")
            near_b.send(0)
            cross.send_ring()
    cond_part = land(cond_part, cross)
    cross.send_ring()
    cond = pair(pair(cond_part, 1, "mc"), 1, "mx").reshape(n_dp * clips, D)
    cond = tie(reordered(cond))[0]
    active = jax.nn.silu(cond).astype(bfloat)
    all_rows = matmul("bd,sed->bse", active, master_low)
    ada = pick[:, 16:24]
    rows = jnp.einsum("sj,bse->bje", ada.astype(single), all_rows, precision=highest)
    rows = rows.reshape(n_dp, clips, 8, width)
    rows = land(rows, near_a, near_b, cross)
    cross_a, cross_b = cross.halves()
    cross_a.pieces, cross_b.pieces, far.ring[0] = tie(
        cross_a.pieces, cross_b.pieces, far.ring[0]
    )
    cross_a.send(0)
    cross_b.send("x")
    far.send_ring()
    for bit in reversed(range(dp_bits())):
        half = rows.shape[0] // 2
        rows = rows[:half] + swap(rows[half:], "dp", bit)
        if bit == 2:
            rows = land(rows, far)
            far.send_ring()
        if bit == 0:
            rows = land(rows, far, cross_a, cross_b)
            cross_a.send("x")
            cross_b.send(0)
            far.send_ring()
    rows = rows[0]
    mine = lax.dynamic_index_in_dim(rows, clip, 0, keepdims=False)
    theirs = swap(lax.dynamic_index_in_dim(rows, 1 - clip, 0, keepdims=False), "mx")
    by_x = jnp.stack(
        [jnp.where(clip == 0, mine, theirs), jnp.where(clip == 0, theirs, mine)], axis=1
    )
    modulation = tie(pair(by_x, 2, "mc").reshape(8, D))[0]

    text = lax.dynamic_index_in_dim(captions, clip, 0, keepdims=False)
    text_len = lax.dynamic_index_in_dim(caption_len, clip, 0, keepdims=False)
    my_step = lax.dynamic_index_in_dim(timestep, clip, 0, keepdims=False)
    my_weight = lax.dynamic_index_in_dim(clip_weight, clip, 0, keepdims=False)
    latents = jnp.stack([clean_latent, noise_draw], axis=1)
    away = swap(lax.dynamic_index_in_dim(latents, 1 - clip, 0, keepdims=False), "mx")
    latents = jnp.concatenate(
        [lax.dynamic_index_in_dim(latents, clip, 0, keepdims=False), away], axis=1
    )
    level = (my_step.astype(single) + 0.5) / NT
    noisy = (1.0 - level) * latents[0] + level * latents[1]
    target = latents[1] - latents[0]

    hidden_zero = jnp.einsum("fc,cd->fd", noisy, latent_master[0], precision=highest)
    first_in = spread(modulate(hidden_zero, modulation[0], modulation[1]).astype(bfloat))
    w_self = jnp.concatenate([near_a.laid(), near_b.laid()], axis=0)
    first_in = land(first_in, far)
    up, down = far.halves()
    up.send(0)
    down.send("x")
    self_query, self_keys, self_values = (
        matmul("fd,ed->fe", first_in, w_self[u]).astype(bfloat) for u in range(3)
    )
    self_query = land(self_query, cross_a, cross_b)
    self_flat, self_total = attention(self_query, self_keys, self_values, None)
    self_flat = land(self_flat, up, down)
    up.send("x")
    down.send(0)
    w_cross = jnp.concatenate([cross_a.laid(), cross_b.laid()], axis=0)
    weights = [w_self[i] for i in range(4)] + [w_cross[i] for i in range(4)]
    self_branch = collect(self_flat, weights[3])
    hidden_one = hidden_zero + modulation[2] * self_branch
    second_in = spread(normed(hidden_one).astype(bfloat))
    cross_query = matmul("fd,ed->fe", second_in, weights[4]).astype(bfloat)
    cross_keys = matmul("ld,ed->le", text, weights[5]).astype(bfloat)
    cross_values = matmul("ld,ed->le", text, weights[6]).astype(bfloat)
    cross_flat, cross_total = attention(cross_query, cross_keys, cross_values, text_len)
    cross_branch = collect(cross_flat, weights[7])
    hidden_two = hidden_one + cross_branch
    third_in = spread(modulate(hidden_two, modulation[3], modulation[4]).astype(bfloat))
    third_in = land(third_in, up)
    w_up = up.pieces.reshape(-1, D)
    upper = matmul("fd,kd->fk", third_in, w_up).astype(bfloat)
    upper_wide = upper.astype(single)
    activated = jax.nn.gelu(upper_wide, approximate=True).astype(bfloat)
    activated, got = tie(activated, down.got)
    w_down = jnp.stack([down.pieces, got], axis=1).reshape(-1, D)
    mlp_branch = collect(activated, w_down)
    hidden_three = hidden_two + modulation[5] * mlp_branch
    final_wide = modulate(hidden_three, modulation[6], modulation[7]).astype(bfloat).astype(single)
    predicted = jnp.einsum("fd,cd->fc", final_wide, latent_master[1], precision=highest)
    error = predicted - target
    loss_local = jnp.sum(my_weight * error * error)

    grad_pred = 2.0 / (C * FRAMES) * my_weight * error / weight_total
    grad_out_proj = jnp.einsum("fc,fd->cd", grad_pred, final_wide, precision=highest)
    grad_final = jnp.einsum("fc,cd->fd", grad_pred, latent_master[1], precision=highest)
    grad_three, shift_f, scale_f = modulate_back(
        hidden_three, modulation[6], modulation[7], grad_final
    )
    gate_m_grad = jnp.sum(grad_three * mlp_branch, axis=0)
    grad_mlp = spread((modulation[5] * grad_three).astype(bfloat))
    grad_w_down = matmul("fk,fd->kd", activated, grad_mlp)
    down = Scatter(cut_far(grad_w_down, unit_tail, True))
    grad_mlp, down.pieces = tie(grad_mlp, down.pieces)
    down.send("x")
    grad_act = matmul("fd,kd->fk", grad_mlp, w_down)
    _, gelu_back = jax.vjp(lambda inner_in: jax.nn.gelu(inner_in, approximate=True), upper_wide)
    grad_upper = gelu_back(grad_act)[0].astype(bfloat)
    grad_w_up = matmul("fk,fd->kd", grad_upper, third_in)
    up = Scatter(cut_far(grad_w_up, unit_tail, False))
    up.send(0)
    grad_third = collect(grad_upper, w_up)
    grad_two, shift_m, scale_m = modulate_back(hidden_two, modulation[3], modulation[4], grad_third)
    grad_two = grad_two + grad_three
    grad_cross = spread(grad_two.astype(bfloat))
    grad_cross_flat = matmul("fd,kd->fk", grad_cross, weights[7]).astype(bfloat)
    grad_w_cross_out = matmul("fk,fd->kd", cross_flat, grad_cross)
    cq_grad, ck_grad, cv_grad = attention_back(
        cross_query, cross_keys, cross_values, text_len, grad_cross_flat, cross_total
    )
    cq_grad = land(cq_grad, down, up)
    down.send(0)
    up.send("x")
    grad_w_cq = matmul("fk,fd->kd", cq_grad, second_in)
    grad_w_ck = matmul("lk,ld->kd", ck_grad, text)
    grad_w_cv = matmul("lk,ld->kd", cv_grad, text)
    cross_a = Scatter(cut_units(jnp.stack([grad_w_cq, grad_w_ck]), True))
    cross_b = Scatter(cut_units(jnp.stack([grad_w_cv, grad_w_cross_out]), False))
    cross_a.send("x")
    cross_b.send(0)
    grad_second = collect(cq_grad, weights[4])
    _, norm_back = jax.vjp(normed, hidden_one)
    grad_one = grad_two + norm_back(grad_second)[0]
    gate_a_grad = jnp.sum(grad_one * self_branch, axis=0)
    grad_self = spread((modulation[2] * grad_one).astype(bfloat))
    grad_self_flat = matmul("fd,kd->fk", grad_self, weights[3]).astype(bfloat)
    grad_self_flat = land(grad_self_flat, down, up)
    far = up.join(down)
    far.send_ring()
    grad_w_self_out = matmul("fk,fd->kd", self_flat, grad_self)
    self_grads = attention_back(
        self_query, self_keys, self_values, None, grad_self_flat, self_total
    )
    self_grads = jnp.concatenate(self_grads, axis=1)
    self_grads = land(self_grads, cross_a, cross_b, far)
    far.send_ring()
    cross_a.send(0)
    cross_b.send("x")
    grad_w_attn = matmul("fk,fd->kd", self_grads, first_in)
    grad_w_attn = land(grad_w_attn, far)
    far.send_ring()
    near_a = Scatter(cut_units(grad_w_attn[: 4 * width].reshape(2, 2 * width, D), True))
    near_b = Scatter(cut_units(jnp.stack([grad_w_attn[4 * width :], grad_w_self_out]), False))
    near_a.send("x")
    near_b.send(0)
    grad_first = collect(self_grads, jnp.concatenate(weights[0:3], axis=0))
    grad_first = land(grad_first, cross_a, cross_b)
    cross = cross_a.join(cross_b)
    cross.send_ring()
    grad_zero, shift_a, scale_a = modulate_back(
        hidden_zero, modulation[0], modulation[1], grad_first
    )
    grad_zero = land(grad_zero, near_a, near_b, cross, far)
    cross.send_ring()
    near_a.send(0)
    near_b.send("x")
    grad_zero = grad_zero + grad_one
    grad_in_proj = jnp.einsum("fc,fd->cd", noisy, grad_zero, precision=highest)

    grad_mod = jnp.stack(
        [shift_a, scale_a, gate_a_grad, shift_m, scale_m, gate_m_grad, shift_f, scale_f], axis=0
    )
    grad_mod = (grad_mod + swap(grad_mod, "mc")).astype(bfloat)
    for i, bit in enumerate(reversed(range(1, dp_bits()))):
        grad_mod = jnp.stack([grad_mod, swap(grad_mod, "dp", bit)], axis=i)
    grad_mod = land(grad_mod, near_a, near_b, cross)
    near = near_a.join(near_b).pieces
    z_got = [shift(near[j], -j) for j in range(1, high())]
    cross.send_ring()
    grad_mod = pair(grad_mod, dp_bits() - 1, "mx")
    grad_mod = jnp.stack([grad_mod, swap(grad_mod, "dp", 0)], axis=dp_bits() - 1)
    grad_mod = tie(grad_mod.reshape(n_dp * clips, 8, D))[0]
    mod_cols = lax.dynamic_index_in_dim(
        grad_mod.reshape(n_dp * clips, 8, D // width, width), column, 2, keepdims=False
    )
    slot_mod = matmul("sj,bje->sbe", ada.astype(bfloat), mod_cols).astype(bfloat)
    grad_active = matmul("sbe,sed->bd", slot_mod, master_low)
    small = jnp.concatenate([grad_in_proj, grad_out_proj], axis=0)
    pad = jnp.full((2 * C, 128), loss_local, single)
    mixed = jnp.concatenate(
        [
            jnp.pad(reordered(grad_active), ((0, 0), (0, 128))),
            jnp.concatenate([small, pad], axis=1),
        ],
        axis=0,
    )
    mixed = sum_dp(sum_mp(mixed))
    grad_active, small = reordered(mixed[: n_dp * clips, :D]), mixed[n_dp * clips :]
    latent_grad = small[:, :D].reshape(2, C, D)
    loss_sum = small[0, D]

    total = near[0].astype(single)
    for item in z_got:
        total = total + item.astype(single)
    cross.take(cross.got)
    reduced = [total] + [item.sum.astype(single) for item in (cross, far)]
    reduced = jnp.concatenate(reduced, axis=0)
    wide_square = sum_mp(jnp.broadcast_to(jnp.sum(reduced * reduced), (8, 128)))
    wide_at = jnp.where((unit_at >= 0) & (unit_at < WIDE), unit_at, 0)
    routes = route_blocks(reduced.astype(bfloat), wide_at, wide_square, n_dp)
    routed = exchange_dp(routes)
    _, silu_back = jax.vjp(jax.nn.silu, cond)
    grad_cond = silu_back(grad_active)[0].astype(bfloat)
    cond_cols = lax.dynamic_index_in_dim(
        grad_cond.reshape(n_dp * clips, D // width, width), column, 1, keepdims=False
    )
    is_time, is_pool = pick[:, 24], pick[:, 25]
    slot_out = jnp.where((is_time | is_pool)[:, None, None], cond_cols[None], slot_mod)
    slot_in = jnp.where(
        is_time[:, None, None],
        sinus_low[None],
        jnp.where(is_pool[:, None, None], pooled_low[None], active[None]),
    )
    def gram(values):
        return matmul("bd,cd->bc", values, values)

    flat_mod = grad_mod.reshape(n_dp * clips, 8 * D)
    thin_square = jnp.sum(gram(active) * gram(flat_mod)) + jnp.sum(
        (gram(sinus_low) + gram(pooled_low)) * gram(grad_cond)
    )

    rest_square = thin_square + jnp.sum(latent_grad * latent_grad)
    count = step_count[0].astype(single)
    is_wide = jnp.any(pick[:, :WIDE], axis=1)
    kind = jnp.where(is_wide, 1, jnp.where(live_slot, 2, 0)).astype(jnp.int32)
    fixes = [1.0 - jnp.power(beta_first, count), 1.0 - jnp.power(beta_second, count)]
    *outputs, grad_norm = adam_places(
        index.reshape(1).astype(jnp.int32),
        kind,
        jnp.stack([rest_square] + fixes),
        routed,
        slot_out,
        slot_in,
        (master, first_moment, second_moment),
        latent_grad,
        (latent_master, latent_first, latent_second),
    )
    loss_value = loss_sum / (C * FRAMES * weight_total)
    return (*outputs, grad_norm, loss_value)


def solution(mesh):
    n_dp, n_mp = mesh.shape["dp"], mesh.shape["mp"]
    fine = Mesh(mesh.devices.reshape(n_dp, n_mp // 2, 2), ("dp", "mx", "mc"))
    frames = P("dp", ("mx", "mc"), None)
    placed = (
        frames,
        frames,
        P("dp", None, None),
        P("dp"),
        P("dp"),
        P(),
        P(),
        P(),
        frames,
        frames,
        frames,
        P(),
        P(),
        P(),
    )
    return jax.shard_map(
        body,
        mesh=fine,
        in_specs=placed,
        out_specs=(frames, frames, frames, P(), P(), P(), P(), P()),
        check_vma=False,
    )
```

time: 578 us -> 500 us (0.87)
  the two profiles are of different devices: /device:TPU:0 before, /device:TPU:8 now
where the time goes in v2:
time: 500 us; the launch traced here: 491 us
  waiting for transfers between devices  167 us (33%)
  starting transfers between devices  111 us (22%)
  matrix products  58.3 us (12%)
  local copies, waits for them, and re-layouts  52 us (10%)
  other arithmetic  47.1 us (9%)
  Pallas kernels  40.5 us (8%)
  between operations  15.5 us (3%)
    ppermute x62, waiting for transfers between devices, swap(): return lax.ppermute(values, axis, [(i, i ^ 1 << bit) for i in range(count)])  104 us
    ppermute x62, starting transfers between devices, swap(): return lax.ppermute(values, axis, [(i, i ^ 1 << bit) for i in range(count)])  64.9 us
    dot_general x40, matrix products, matmul(): return jnp.einsum(form, left, right, preferred_element_type=single)  48.6 us
    ppermute x14, waiting for transfers between devices, exchange_dp(): got[k] = lax.ppermute(blocks[k], 'dp', [(i, i ^ k) for i in range(count)])  32 us
    ppermute x18, waiting for transfers between devices, shift(): lax.ppermute(values, 'dp', [(i, (i + 2 * by) % count) for i in range(coun...  30.4 us
    pallas_call x4, Pallas kernels, pair_call(): pl.pallas_call(functools.partial(kernel, masked), out_shape=outs, grid_sp...  29.9 us
    unnamed x280, local copies, waits for them, and re-layouts  28.7 us
    ppermute x18, starting transfers between devices, shift(): lax.ppermute(values, 'dp', [(i, (i + 2 * by) % count) for i in range(coun...  26.6 us
  transfers between devices with their start and end apart: 94, of which 50 were waited for; matrix products, arithmetic and copies ran while one was open for 18% of the time, Pallas kernels for 6%

profile of v2, /device:TPU:8, one launch (start us, length us, event | category | flops | bytes accessed | tf_op | source)
XLA Modules:
  0.0 490.6 jit_solution(11743635714963592392)
XLA Ops:
  3.7 2.5 collective-permute-start.6
  6.7 4.3 collective-permute-start.4
  21.1 7.8 %collective-permute-done.6.refs_7_ = bf16[5,3,8,768]{3,2,1,0:T(8,128)(2,1)S(1)} collective-permute-done((bf16[5,3,8,768]{3,2,1,0:T(8,128)(2,1)}, bf16[5,3,8,768]{3,2,1,0:T(8,128)(2,1)S(1)}, u32[]{:S(2)}, u32[]{:S(2)}) %collective-permute-start.6) | collective-permute-done | bytes 184352 | tf_op jit(solution)/shard_map/ppermute | solution.py:280
  29.0 3.1 collective-permute-done.5.refs_6_
  32.6 2.7 collective-permute-done.4.refs_5_
  44.9 3.4 collective-permute-done.8
  48.4 3.9 collective-permute-start.9
  54.1 3.3 collective-permute-done.10
  66.1 3.8 collective-permute-done.12
  72.6 2.5 collective-permute-start.17
  80.2 2.9 collective-permute-done.14
  87.9 2.6 collective-permute-done.19
  96.4 11.6 %collective-permute-done.21 = f32[16,2,192]{2,0,1:T(8,128)S(1)} collective-permute-done((f32[16,2,192]{2,0,1:T(8,128)S(1)}, f32[16,2,192]{2,0,1:T(8,128)S(1)}, u32[]{:S(2)}, u32[]{:S(2)}) %collective-permute-start.21) | collective-permute-done | bytes 24608 | tf_op jit(solution)/shard_map/ppermute | solution.py:35
  115.2 2.4 collective-permute-done.26
  117.6 4.5 collective-permute-done.27
  122.1 3.8 collective-permute-start.28
  129.7 5.3 %collective-permute-done.29 = f32[1,2,8,192]{3,2,1,0:T(8,128)S(1)} collective-permute-done((f32[1,2,8,192]{3,2,1,0:T(8,128)S(1)}, f32[1,2,8,192]{3,2,1,0:T(8,128)S(1)}, u32[]{:S(2)}, u32[]{:S(2)}) %collective-permute-start.29) | collective-permute-done | bytes 12320 | tf_op jit(solution)/shard_map/ppermute | solution.py:35
  149.6 7.3 %collective-permute-done.36 = bf16[8,3,8,768]{3,2,1,0:T(8,128)(2,1)S(1)} collective-permute-done((bf16[8,3,8,768]{3,2,1,0:T(8,128)(2,1)S(1)}, bf16[8,3,8,768]{3,2,1,0:T(8,128)(2,1)S(1)}, u32[]{:S(2)}, u32[]{:S(2)}) %collective-permute-start.36) | collective-permute-done | bytes 294944 | tf_op jit(solution)/shard_map/ppermute | solution.py:80
  158.8 4.3 collective-permute-done.37
  166.2 7.6 %shard_map.270 = (bf16[768,384]{1,0:T(8,128)(2,1)S(1)}, f32[3,2,768]{2,1,0:T(2,128)S(1)}) custom-call(s32[1]{0:T(128)} %constant.191.clone.1.length, bf16[768,384]{1,0:T(8,128)(2,1)S(1)} %convolution_convert_fusion.19.query, bf16[768,384]{1,0:T(8,128)(2,1)S(1)} %convolution_convert_fusion.18.keys, bf16[768,384]{1,0:T(8,128)(2,1)S(1)} %convolution_convert_fusion.17.values), custom_call_target="tpu_custom_call" | custom-call | flops 3623878656 | bytes 8388608 | tf_op jit(solution)/shard_map/pallas_call | solution.py:468
  173.8 4.2 collective-permute-done.39
  186.8 4.7 shard_map.271
  198.1 22.6 %collective-permute-done.45 = bf16[2,4,4,3,8,768]{5,4,3,2,1,0:T(8,128)(2,1)S(1)} collective-permute-done((bf16[2,4,4,3,8,768]{5,4,3,2,1,0:T(8,128)(2,1)S(1)}, bf16[2,4,4,3,8,768]{5,4,3,2,1,0:T(8,128)(2,1)S(1)}, u32[]{:S(2)}, u32[]{:S(2)}) %collective-permute-start.45) | collective-permute-done | bytes 1179680 | tf_op jit(solution)/shard_map/ppermute | solution.py:35
  221.0 4.2 fusion.7
  234.0 4.5 fusion.174
  247.6 4.1 convolution_convert_fusion.1
  254.6 4.6 fusion.3
  276.9 6.1 %shard_map.272 = (bf16[768,384]{1,0:T(8,128)(2,1)S(1)}, bf16[256,384]{1,0:T(8,128)(2,1)S(1)}, bf16[256,384]{1,0:T(8,128)(2,1)S(1)}) custom-call(s32[1]{0:T(128)} %dynamic_slice.90.length, bf16[768,384]{1,0:T(8,128)(2,1)S(1)} %copy-done.16, bf16[256,384]{1,0:T(8,128)(2,1)S(1)} %convolution_convert_fusion.21.keys, ...), custom_call_target="tpu_custom_call" | custom-call | flops 3019898880 | bytes 8388608 | tf_op jit(solution)/shard_map/pallas_call | solution.py:468
  287.1 13.1 %collective-permute-done.51 = bf16[2,4,4,3,8,768]{5,4,3,2,1,0:T(8,128)(2,1)} collective-permute-done((bf16[2,4,4,3,8,768]{5,4,3,2,1,0:T(8,128)(2,1)}, bf16[2,4,4,3,8,768]{5,4,3,2,1,0:T(8,128)(2,1)}, u32[]{:S(2)}, u32[]{:S(2)}) %collective-permute-start.51) | collective-permute-done | bytes 1179680 | tf_op jit(solution)/shard_map/ppermute | solution.py:35
  300.2 2.9 collective-permute-done.52
  317.5 6.1 %collective-permute-done.56 = bf16[4,4,3,8,768]{4,3,2,1,0:T(8,128)(2,1)S(1)} collective-permute-done((bf16[4,4,3,8,768]{4,3,2,1,0:T(8,128)(2,1)S(1)}, bf16[4,4,3,8,768]{4,3,2,1,0:T(8,128)(2,1)S(1)}, u32[]{:S(2)}, u32[]{:S(2)}) %collective-permute-start.56) | collective-permute-done | bytes 589856 | tf_op jit(solution)/shard_map/ppermute | solution.py:35
  323.6 3.6 collective-permute-done.55
  328.8 11.5 %shard_map.273 = (bf16[768,384]{1,0:T(8,128)(2,1)S(1)}, bf16[768,384]{1,0:T(8,128)(2,1)S(1)}, bf16[768,384]{1,0:T(8,128)(2,1)S(1)}) custom-call(s32[1]{0:T(128)} %constant.191.clone.1.length, bf16[768,384]{1,0:T(8,128)(2,1)S(1)} %copy-done.12, bf16[768,384]{1,0:T(8,128)(2,1)S(1)} %copy-done.14, bf16[768,384]{1,0:T(8,128)(2,1)S(1)} %copy-done.10, ...), custom_call_target="tpu_custom_call" | custom-call | flops 9059696640 | bytes 8388608 | tf_op jit(solution)/shard_map/pallas_call | solution.py:468
  341.6 3.8 collective-permute-start.66
  364.5 3.5 collective-permute-start.64
  371.6 2.6 collective-permute-done.65
  383.5 3.1 collective-permute-done.71
  396.1 5.6 %collective-permute-start.82 = (bf16[4,3,8,768]{3,2,1,0:T(8,128)(2,1)}, bf16[4,3,8,768]{3,2,1,0:T(8,128)(2,1)}, u32[]{:S(2)}, u32[]{:S(2)}) collective-permute-start(bf16[4,3,8,768]{3,2,1,0:T(8,128)(2,1)} %get-tuple-element.301), channel_id=1, source_target_pairs={{0,16},{4,20},{8,24},{12,28},{16,0},{20,4},{24,8},{28,12},{1,17},{... | collective-permute-start | bytes 442376 | tf_op jit(solution)/shard_map/ppermute | solution.py:80
  412.1 2.3 collective-permute-done.77
  415.8 4.5 collective-permute-done.78
  420.3 2.9 collective-permute-start.79
  427.0 2.8 collective-permute-start.80
  437.3 3.0 collective-permute-start.91
  455.4 3.5 collective-permute-done.90
  458.8 4.4 collective-permute-done.91
  463.2 4.4 collective-permute-done.92
  467.6 3.3 collective-permute-done.93
  478.2 7.5 %shard_map.275 = (f32[5,3,64,768]{3,2,1,0:T(8,128)}, f32[5,3,64,768]{3,2,1,0:T(8,128)}, f32[5,3,64,768]{3,2,1,0:T(8,128)}, f32[2,20,768]{2,1,0:T(8,128)S(1)}, f3...) custom-call(s32[1]{0:T(128)} %bitcast.me, s32[5]{0:T(128)S(1)} %select_select_fusion.1.kind, ...), custom_call_target="tpu_custom_call" | custom-call | tf_op jit(solution)/shard_map/pallas_call | solution.py:344
  (716 shorter events, 236.1 us)
Async XLA Ops:
  3.7 25.2 %collective-permute-start.6 = (bf16[5,3,8,768]{3,2,1,0:T(8,128)(2,1)}, bf16[5,3,8,768]{3,2,1,0:T(8,128)(2,1)S(1)}, u32[]{:S(2)}, u32[]{:S(2)}) collective-permute-start(bf16[5,3,8,768]{3,2,1,0:T(8,128)(2,1)} %get-tuple-element.275), channel_id=1, source_target_pairs={{0,28},{4,24},{8,20},{12,16},{16,12},{20,8},{24,4},{28,0},{1,29},{... | collective-permute-start | bytes 552968 | tf_op jit(solution)/shard_map/ppermute | solution.py:280
  6.3 25.8 %collective-permute-start.5 = (bf16[5,3,8,768]{3,2,1,0:T(8,128)(2,1)}, bf16[5,3,8,768]{3,2,1,0:T(8,128)(2,1)S(1)}, u32[]{:S(2)}, u32[]{:S(2)}) collective-permute-start(bf16[5,3,8,768]{3,2,1,0:T(8,128)(2,1)} %get-tuple-element.276), channel_id=1, source_target_pairs={{0,24},{4,28},{8,16},{12,20},{16,8},{20,12},{24,0},{28,4},{1,25},{... | collective-permute-start | bytes 552968 | tf_op jit(solution)/shard_map/ppermute | solution.py:280
  6.7 28.7 %collective-permute-start.4 = (bf16[5,3,8,768]{3,2,1,0:T(8,128)(2,1)}, bf16[5,3,8,768]{3,2,1,0:T(8,128)(2,1)S(1)}, u32[]{:S(2)}, u32[]{:S(2)}) collective-permute-start(bf16[5,3,8,768]{3,2,1,0:T(8,128)(2,1)} %get-tuple-element.277), channel_id=1, source_target_pairs={{0,20},{4,16},{8,28},{12,24},{16,4},{20,0},{24,12},{28,8},{1,21},{... | collective-permute-start | bytes 552968 | tf_op jit(solution)/shard_map/ppermute | solution.py:280
  11.0 27.0 %collective-permute-start.3 = (bf16[5,3,8,768]{3,2,1,0:T(8,128)(2,1)S(1)}, bf16[5,3,8,768]{3,2,1,0:T(8,128)(2,1)S(1)}, u32[]{:S(2)}, u32[]{:S(2)}) collective-permute-start(bf16[5,3,8,768]{3,2,1,0:T(8,128)(2,1)S(1)} %get-tuple-element.278), channel_id=1, source_target_pairs={{0,16},{4,20},{8,24},{12,28},{16,0},{20,4},{24,8},{28,12},{1,17},{... | collective-permute-start | bytes 552968 | tf_op jit(solution)/shard_map/ppermute | solution.py:280
  11.1 27.0 %collective-permute-start.2 = (bf16[5,3,8,768]{3,2,1,0:T(8,128)(2,1)S(1)}, bf16[5,3,8,768]{3,2,1,0:T(8,128)(2,1)S(1)}, u32[]{:S(2)}, u32[]{:S(2)}) collective-permute-start(bf16[5,3,8,768]{3,2,1,0:T(8,128)(2,1)S(1)} %get-tuple-element.279), channel_id=1, source_target_pairs={{0,12},{4,8},{8,4},{12,0},{16,28},{20,24},{24,20},{28,16},{1,13},{... | collective-permute-start | bytes 552968 | tf_op jit(solution)/shard_map/ppermute | solution.py:280
  29.0 10.6 %collective-permute-start.1 = (bf16[5,3,8,768]{3,2,1,0:T(8,128)(2,1)S(1)}, bf16[5,3,8,768]{3,2,1,0:T(8,128)(2,1)S(1)}, u32[]{:S(2)}, u32[]{:S(2)}) collective-permute-start(bf16[5,3,8,768]{3,2,1,0:T(8,128)(2,1)S(1)} %get-tuple-element.280), channel_id=1, source_target_pairs={{0,8},{4,12},{8,0},{12,4},{16,24},{20,28},{24,16},{28,20},{1,9},{5... | collective-permute-start | bytes 552968 | tf_op jit(solution)/shard_map/ppermute | solution.py:280
  35.4 44.0 %collective-permute-start.22 = (f32[2,192,20]{1,2,0:T(8,128)}, f32[2,192,20]{1,2,0:T(8,128)}, u32[]{:S(2)}, u32[]{:S(2)}) collective-permute-start(f32[2,192,20]{1,2,0:T(8,128)} %copy.168), channel_id=1, source_target_pairs={{0,2},{2,0},{1,3},{3,1},{4,6},{6,4},{5,7},{7,5},{8,10},{10,8},{9,1... | collective-permute-start | bytes 92168 | tf_op jit(solution)/shard_map/ppermute | solution.py:35
  72.6 10.5 %collective-permute-start.17 = (bf16[4,3,8,768]{3,2,1,0:T(8,128)(2,1)S(1)}, bf16[4,3,8,768]{3,2,1,0:T(8,128)(2,1)S(1)}, u32[]{:S(2)}, u32[]{:S(2)}) collective-permute-start(bf16[4,3,8,768]{3,2,1,0:T(8,128)(2,1)S(1)} %get-tuple-element.124), channel_id=1, source_target_pairs={{0,8},{4,12},{8,16},{12,20},{16,24},{20,28},{24,0},{28,4},{1,9},{5... | collective-permute-start | bytes 442376 | tf_op jit(solution)/shard_map/ppermute | solution.py:80
  91.4 19.3 %collective-permute-start.23 = (bf16[2,4,2,3,8,768]{5,4,3,2,1,0:T(8,128)(2,1)}, bf16[2,4,2,3,8,768]{5,4,3,2,1,0:T(8,128)(2,1)}, u32[]{:S(2)}, u32[]{:S(2)}) collective-permute-start(bf16[2,4,2,3,8,768]{5,4,3,2,1,0:T(8,128)(2,1)} %get-tuple-element.309), channel_id=1, source_target_pairs={{0,2},{2,0},{1,3},{3,1},{4,6},{6,4},{5,7},{7,5},{8,10},{10,8},{9,1... | collective-permute-start | bytes 1769480 | tf_op jit(solution)/shard_map/ppermute | solution.py:35
  92.3 15.8 %collective-permute-start.21 = (f32[16,2,192]{2,0,1:T(8,128)S(1)}, f32[16,2,192]{2,0,1:T(8,128)S(1)}, u32[]{:S(2)}, u32[]{:S(2)}) collective-permute-start(f32[16,2,192]{2,0,1:T(8,128)S(1)} %pad_maximum_fusion.39), channel_id=1, source_target_pairs={{0,2},{2,0},{1,3},{3,1},{4,6},{6,4},{5,7},{7,5},{8,10},{10,8},{9,1... | collective-permute-start | bytes 73736 | tf_op jit(solution)/shard_map/ppermute | solution.py:35
  94.4 16.3 %collective-permute-start.24 = (bf16[2,4,2,3,8,768]{5,4,3,2,1,0:T(8,128)(2,1)}, bf16[2,4,2,3,8,768]{5,4,3,2,1,0:T(8,128)(2,1)}, u32[]{:S(2)}, u32[]{:S(2)}) collective-permute-start(bf16[2,4,2,3,8,768]{5,4,3,2,1,0:T(8,128)(2,1)} %get-tuple-element.307), channel_id=1, source_target_pairs={{0,4},{4,0},{8,12},{12,8},{16,20},{20,16},{24,28},{28,24},{1,5},{5... | collective-permute-start | bytes 1769480 | tf_op jit(solution)/shard_map/ppermute | solution.py:35
  96.2 14.4 %collective-permute-start.25 = (bf16[4,3,8,768]{3,2,1,0:T(8,128)(2,1)}, bf16[4,3,8,768]{3,2,1,0:T(8,128)(2,1)S(1)}, u32[]{:S(2)}, u32[]{:S(2)}) collective-permute-start(bf16[4,3,8,768]{3,2,1,0:T(8,128)(2,1)} %collective-permute-done.19), channel_id=1, source_target_pairs={{0,8},{4,12},{8,16},{12,20},{16,24},{20,28},{24,0},{28,4},{1,9},{5... | collective-permute-start | bytes 442376 | tf_op jit(solution)/shard_map/ppermute | solution.py:80
  113.0 9.2 %collective-permute-start.27 = (bf16[8,3,8,768]{3,2,1,0:T(8,128)(2,1)S(1)}, bf16[8,3,8,768]{3,2,1,0:T(8,128)(2,1)S(1)}, u32[]{:S(2)}, u32[]{:S(2)}) collective-permute-start(bf16[8,3,8,768]{3,2,1,0:T(8,128)(2,1)S(1)} %get-tuple-element.136), channel_id=1, source_target_pairs={{0,8},{4,12},{8,16},{12,20},{16,24},{20,28},{24,0},{28,4},{1,9},{5... | collective-permute-start | bytes 884744 | tf_op jit(solution)/shard_map/ppermute | solution.py:80
  126.2 8.8 %collective-permute-start.31 = (bf16[4,2,3,8,768]{4,3,2,1,0:T(8,128)(2,1)S(1)}, bf16[4,2,3,8,768]{4,3,2,1,0:T(8,128)(2,1)S(1)}, u32[]{:S(2)}, u32[]{:S(2)}) collective-permute-start(bf16[4,2,3,8,768]{4,3,2,1,0:T(8,128)(2,1)S(1)} %get-tuple-element.139), channel_id=1, source_target_pairs={{0,4},{4,0},{8,12},{12,8},{16,20},{20,16},{24,28},{28,24},{1,5},{5... | collective-permute-start | bytes 884744 | tf_op jit(solution)/shard_map/ppermute | solution.py:35
  147.4 9.5 %collective-permute-start.36 = (bf16[8,3,8,768]{3,2,1,0:T(8,128)(2,1)S(1)}, bf16[8,3,8,768]{3,2,1,0:T(8,128)(2,1)S(1)}, u32[]{:S(2)}, u32[]{:S(2)}) collective-permute-start(bf16[8,3,8,768]{3,2,1,0:T(8,128)(2,1)S(1)} %copy-done.84), channel_id=1, source_target_pairs={{0,8},{4,12},{8,16},{12,20},{16,24},{20,28},{24,0},{28,4},{1,9},{5... | collective-permute-start | bytes 884744 | tf_op jit(solution)/shard_map/ppermute | solution.py:80
  147.9 15.1 %collective-permute-start.37 = (bf16[2,4,2,3,8,768]{5,4,3,2,1,0:T(8,128)(2,1)S(1)}, bf16[2,4,2,3,8,768]{5,4,3,2,1,0:T(8,128)(2,1)S(1)}, u32[]{:S(2)}, u32[]{:S(2)}) collective-permute-start(bf16[2,4,2,3,8,768]{5,4,3,2,1,0:T(8,128)(2,1)S(1)} %get-tuple-element.305), channel_id=1, source_target_pairs={{0,2},{2,0},{1,3},{3,1},{4,6},{6,4},{5,7},{7,5},{8,10},{10,8},{9,1... | collective-permute-start | bytes 1769480 | tf_op jit(solution)/shard_map/ppermute | solution.py:35
  149.1 14.9 %collective-permute-start.38 = (bf16[2,4,2,3,8,768]{5,4,3,2,1,0:T(8,128)(2,1)S(1)}, bf16[2,4,2,3,8,768]{5,4,3,2,1,0:T(8,128)(2,1)S(1)}, u32[]{:S(2)}, u32[]{:S(2)}) collective-permute-start(bf16[2,4,2,3,8,768]{5,4,3,2,1,0:T(8,128)(2,1)S(1)} %get-tuple-element.303), channel_id=1, source_target_pairs={{0,4},{4,0},{8,12},{12,8},{16,20},{20,16},{24,28},{28,24},{1,5},{5... | collective-permute-start | bytes 1769480 | tf_op jit(solution)/shard_map/ppermute | solution.py:35
  164.0 14.0 %collective-permute-start.39 = (bf16[4,4,3,8,768]{4,3,2,1,0:T(8,128)(2,1)S(1)}, bf16[4,4,3,8,768]{4,3,2,1,0:T(8,128)(2,1)S(1)}, u32[]{:S(2)}, u32[]{:S(2)}) collective-permute-start(bf16[4,4,3,8,768]{4,3,2,1,0:T(8,128)(2,1)S(1)} %get-tuple-element.151), channel_id=1, source_target_pairs={{0,4},{4,0},{8,12},{12,8},{16,20},{20,16},{24,28},{28,24},{1,5},{5... | collective-permute-start | bytes 1769480 | tf_op jit(solution)/shard_map/ppermute | solution.py:35
  164.3 13.7 %collective-permute-start.40 = (bf16[4,4,3,8,768]{4,3,2,1,0:T(8,128)(2,1)S(1)}, bf16[4,4,3,8,768]{4,3,2,1,0:T(8,128)(2,1)S(1)}, u32[]{:S(2)}, u32[]{:S(2)}) collective-permute-start(bf16[4,4,3,8,768]{4,3,2,1,0:T(8,128)(2,1)S(1)} %get-tuple-element.152), channel_id=1, source_target_pairs={{0,2},{2,0},{1,3},{3,1},{4,6},{6,4},{5,7},{7,5},{8,10},{10,8},{9,1... | collective-permute-start | bytes 1769480 | tf_op jit(solution)/shard_map/ppermute | solution.py:35
  192.6 28.2 %collective-permute-start.45 = (bf16[2,4,4,3,8,768]{5,4,3,2,1,0:T(8,128)(2,1)S(1)}, bf16[2,4,4,3,8,768]{5,4,3,2,1,0:T(8,128)(2,1)S(1)}, u32[]{:S(2)}, u32[]{:S(2)}) collective-permute-start(bf16[2,4,4,3,8,768]{5,4,3,2,1,0:T(8,128)(2,1)S(1)} %get-tuple-element.288), channel_id=1, source_target_pairs={{0,2},{2,0},{1,3},{3,1},{4,6},{6,4},{5,7},{7,5},{8,10},{10,8},{9,1... | collective-permute-start | bytes 3538952 | tf_op jit(solution)/shard_map/ppermute | solution.py:35
  195.8 29.4 %collective-permute-start.46 = (bf16[2,4,4,3,8,768]{5,4,3,2,1,0:T(8,128)(2,1)S(1)}, bf16[2,4,4,3,8,768]{5,4,3,2,1,0:T(8,128)(2,1)S(1)}, u32[]{:S(2)}, u32[]{:S(2)}) collective-permute-start(bf16[2,4,4,3,8,768]{5,4,3,2,1,0:T(8,128)(2,1)S(1)} %get-tuple-element.286), channel_id=1, source_target_pairs={{0,4},{4,0},{8,12},{12,8},{16,20},{20,16},{24,28},{28,24},{1,5},{5... | collective-permute-start | bytes 3538952 | tf_op jit(solution)/shard_map/ppermute | solution.py:35
  271.9 28.3 %collective-permute-start.51 = (bf16[2,4,4,3,8,768]{5,4,3,2,1,0:T(8,128)(2,1)}, bf16[2,4,4,3,8,768]{5,4,3,2,1,0:T(8,128)(2,1)}, u32[]{:S(2)}, u32[]{:S(2)}) collective-permute-start(bf16[2,4,4,3,8,768]{5,4,3,2,1,0:T(8,128)(2,1)} %slice_bitcast_fusion.2), channel_id=1, source_target_pairs={{0,2},{2,0},{1,3},{3,1},{4,6},{6,4},{5,7},{7,5},{8,10},{10,8},{9,1... | collective-permute-start | bytes 3538952 | tf_op jit(solution)/shard_map/ppermute | solution.py:35
  273.9 29.2 %collective-permute-start.52 = (bf16[2,4,4,3,8,768]{5,4,3,2,1,0:T(8,128)(2,1)}, bf16[2,4,4,3,8,768]{5,4,3,2,1,0:T(8,128)(2,1)}, u32[]{:S(2)}, u32[]{:S(2)}) collective-permute-start(bf16[2,4,4,3,8,768]{5,4,3,2,1,0:T(8,128)(2,1)} %slice_bitcast_fusion.1), channel_id=1, source_target_pairs={{0,4},{4,0},{8,12},{12,8},{16,20},{20,16},{24,28},{28,24},{1,5},{5... | collective-permute-start | bytes 3538952 | tf_op jit(solution)/shard_map/ppermute | solution.py:35
  286.7 54.4 %collective-permute-start.58 = (bf16[2,4,2,3,8,768]{5,4,3,2,1,0:T(8,128)(2,1)S(1)}, bf16[2,4,2,3,8,768]{5,4,3,2,1,0:T(8,128)(2,1)S(1)}, u32[]{:S(2)}, u32[]{:S(2)}) collective-permute-start(bf16[2,4,2,3,8,768]{5,4,3,2,1,0:T(8,128)(2,1)S(1)} %slice_bitcast_fusion.11), channel_id=1, source_target_pairs={{0,4},{4,0},{8,12},{12,8},{16,20},{20,16},{24,28},{28,24},{1,5},{5... | collective-permute-start | bytes 1769480 | tf_op jit(solution)/shard_map/ppermute | solution.py:35
  307.4 16.2 %collective-permute-start.56 = (bf16[4,4,3,8,768]{4,3,2,1,0:T(8,128)(2,1)S(1)}, bf16[4,4,3,8,768]{4,3,2,1,0:T(8,128)(2,1)S(1)}, u32[]{:S(2)}, u32[]{:S(2)}) collective-permute-start(bf16[4,4,3,8,768]{4,3,2,1,0:T(8,128)(2,1)S(1)} %slice_bitcast_fusion.13), channel_id=1, source_target_pairs={{0,2},{2,0},{1,3},{3,1},{4,6},{6,4},{5,7},{7,5},{8,10},{10,8},{9,1... | collective-permute-start | bytes 1769480 | tf_op jit(solution)/shard_map/ppermute | solution.py:35
  308.6 18.5 %collective-permute-start.55 = (bf16[4,4,3,8,768]{4,3,2,1,0:T(8,128)(2,1)S(1)}, bf16[4,4,3,8,768]{4,3,2,1,0:T(8,128)(2,1)S(1)}, u32[]{:S(2)}, u32[]{:S(2)}) collective-permute-start(bf16[4,4,3,8,768]{4,3,2,1,0:T(8,128)(2,1)S(1)} %slice_bitcast_fusion.14), channel_id=1, source_target_pairs={{0,4},{4,0},{8,12},{12,8},{16,20},{20,16},{24,28},{28,24},{1,5},{5... | collective-permute-start | bytes 1769480 | tf_op jit(solution)/shard_map/ppermute | solution.py:35
  315.7 25.4 %collective-permute-start.57 = (bf16[2,4,2,3,8,768]{5,4,3,2,1,0:T(8,128)(2,1)S(1)}, bf16[2,4,2,3,8,768]{5,4,3,2,1,0:T(8,128)(2,1)S(1)}, u32[]{:S(2)}, u32[]{:S(2)}) collective-permute-start(bf16[2,4,2,3,8,768]{5,4,3,2,1,0:T(8,128)(2,1)S(1)} %slice_bitcast_fusion.12), channel_id=1, source_target_pairs={{0,2},{2,0},{1,3},{3,1},{4,6},{6,4},{5,7},{7,5},{8,10},{10,8},{9,1... | collective-permute-start | bytes 1769480 | tf_op jit(solution)/shard_map/ppermute | solution.py:35
  327.5 13.6 %collective-permute-start.59 = (bf16[8,3,8,768]{3,2,1,0:T(8,128)(2,1)S(1)}, bf16[8,3,8,768]{3,2,1,0:T(8,128)(2,1)S(1)}, u32[]{:S(2)}, u32[]{:S(2)}) collective-permute-start(bf16[8,3,8,768]{3,2,1,0:T(8,128)(2,1)S(1)} %fusion.47), channel_id=1, source_target_pairs={{0,8},{4,12},{8,16},{12,20},{16,24},{20,28},{24,0},{28,4},{1,9},{5... | collective-permute-start | bytes 884744 | tf_op jit(solution)/shard_map/ppermute | solution.py:80
  341.6 9.1 %collective-permute-start.66 = (bf16[8,3,8,768]{3,2,1,0:T(8,128)(2,1)S(1)}, bf16[8,3,8,768]{3,2,1,0:T(8,128)(2,1)S(1)}, u32[]{:S(2)}, u32[]{:S(2)}) collective-permute-start(bf16[8,3,8,768]{3,2,1,0:T(8,128)(2,1)S(1)} %fusion.36), channel_id=1, source_target_pairs={{0,8},{4,12},{8,16},{12,20},{16,24},{20,28},{24,0},{28,4},{1,9},{5... | collective-permute-start | bytes 884744 | tf_op jit(solution)/shard_map/ppermute | solution.py:80
  345.4 14.4 %collective-permute-start.62 = (bf16[4,2,3,8,768]{4,3,2,1,0:T(8,128)(2,1)S(1)}, bf16[4,2,3,8,768]{4,3,2,1,0:T(8,128)(2,1)S(1)}, u32[]{:S(2)}, u32[]{:S(2)}) collective-permute-start(bf16[4,2,3,8,768]{4,3,2,1,0:T(8,128)(2,1)S(1)} %slice_bitcast_fusion.21), channel_id=1, source_target_pairs={{0,2},{2,0},{1,3},{3,1},{4,6},{6,4},{5,7},{7,5},{8,10},{10,8},{9,1... | collective-permute-start | bytes 884744 | tf_op jit(solution)/shard_map/ppermute | solution.py:35
  346.4 13.4 %collective-permute-start.61 = (bf16[4,2,3,8,768]{4,3,2,1,0:T(8,128)(2,1)S(1)}, bf16[4,2,3,8,768]{4,3,2,1,0:T(8,128)(2,1)S(1)}, u32[]{:S(2)}, u32[]{:S(2)}) collective-permute-start(bf16[4,2,3,8,768]{4,3,2,1,0:T(8,128)(2,1)S(1)} %slice_bitcast_fusion.22), channel_id=1, source_target_pairs={{0,4},{4,0},{8,12},{12,8},{16,20},{20,16},{24,28},{28,24},{1,5},{5... | collective-permute-start | bytes 884744 | tf_op jit(solution)/shard_map/ppermute | solution.py:35
  352.7 21.6 %collective-permute-start.70 = (bf16[8,3,8,768]{3,2,1,0:T(8,128)(2,1)}, bf16[8,3,8,768]{3,2,1,0:T(8,128)(2,1)}, u32[]{:S(2)}, u32[]{:S(2)}) collective-permute-start(bf16[8,3,8,768]{3,2,1,0:T(8,128)(2,1)} %fusion.33), channel_id=1, source_target_pairs={{0,8},{4,12},{8,16},{12,20},{16,24},{20,28},{24,0},{28,4},{1,9},{5... | collective-permute-start | bytes 884744 | tf_op jit(solution)/shard_map/ppermute | solution.py:80
  354.8 19.4 %collective-permute-start.67 = (bf16[2,4,2,3,8,768]{5,4,3,2,1,0:T(8,128)(2,1)}, bf16[2,4,2,3,8,768]{5,4,3,2,1,0:T(8,128)(2,1)}, u32[]{:S(2)}, u32[]{:S(2)}) collective-permute-start(bf16[2,4,2,3,8,768]{5,4,3,2,1,0:T(8,128)(2,1)} %slice_bitcast_fusion.5), channel_id=1, source_target_pairs={{0,2},{2,0},{1,3},{3,1},{4,6},{6,4},{5,7},{7,5},{8,10},{10,8},{9,1... | collective-permute-start | bytes 1769480 | tf_op jit(solution)/shard_map/ppermute | solution.py:35
  357.1 17.1 %collective-permute-start.68 = (bf16[2,4,2,3,8,768]{5,4,3,2,1,0:T(8,128)(2,1)}, bf16[2,4,2,3,8,768]{5,4,3,2,1,0:T(8,128)(2,1)}, u32[]{:S(2)}, u32[]{:S(2)}) collective-permute-start(bf16[2,4,2,3,8,768]{5,4,3,2,1,0:T(8,128)(2,1)} %slice_bitcast_fusion.4), channel_id=1, source_target_pairs={{0,4},{4,0},{8,12},{12,8},{16,20},{20,16},{24,28},{28,24},{1,5},{5... | collective-permute-start | bytes 1769480 | tf_op jit(solution)/shard_map/ppermute | solution.py:35
  388.5 21.1 %collective-permute-start.84 = (bf16[4,3,8,768]{3,2,1,0:T(8,128)(2,1)}, bf16[4,3,8,768]{3,2,1,0:T(8,128)(2,1)}, u32[]{:S(2)}, u32[]{:S(2)}) collective-permute-start(bf16[4,3,8,768]{3,2,1,0:T(8,128)(2,1)} %fusion.51), channel_id=1, source_target_pairs={{0,8},{4,12},{8,16},{12,20},{16,24},{20,28},{24,0},{28,4},{1,9},{5... | collective-permute-start | bytes 442376 | tf_op jit(solution)/shard_map/ppermute | solution.py:80
  391.0 10.6 %collective-permute-start.75 = (bf16[2,2,2,8,768]{4,3,0,1,2:T(8,128)(2,1)S(1)}, bf16[2,2,2,8,768]{4,3,0,1,2:T(8,128)(2,1)S(1)}, u32[]{:S(2)}, u32[]{:S(2)}) collective-permute-start(bf16[2,2,2,8,768]{4,3,0,1,2:T(8,128)(2,1)S(1)} %get-tuple-element.317), channel_id=1, source_target_pairs={{0,4},{4,0},{8,12},{12,8},{16,20},{20,16},{24,28},{28,24},{1,5},{5... | collective-permute-start | bytes 294920 | tf_op jit(solution)/shard_map/ppermute | solution.py:35
  393.6 10.4 %collective-permute-start.81 = (bf16[4,3,8,768]{3,2,1,0:T(8,128)(2,1)}, bf16[4,3,8,768]{3,2,1,0:T(8,128)(2,1)}, u32[]{:S(2)}, u32[]{:S(2)}) collective-permute-start(bf16[4,3,8,768]{3,2,1,0:T(8,128)(2,1)} %get-tuple-element.299), channel_id=1, source_target_pairs={{0,24},{4,28},{8,0},{12,4},{16,8},{20,12},{24,16},{28,20},{1,25},{... | collective-permute-start | bytes 442376 | tf_op jit(solution)/shard_map/ppermute | solution.py:80
  395.5 9.5 %collective-permute-start.83 = (bf16[4,3,8,768]{3,2,1,0:T(8,128)(2,1)}, bf16[4,3,8,768]{3,2,1,0:T(8,128)(2,1)}, u32[]{:S(2)}, u32[]{:S(2)}) collective-permute-start(bf16[4,3,8,768]{3,2,1,0:T(8,128)(2,1)} %get-tuple-element.300), channel_id=1, source_target_pairs={{0,8},{4,12},{8,16},{12,20},{16,24},{20,28},{24,0},{28,4},{1,9},{5... | collective-permute-start | bytes 442376 | tf_op jit(solution)/shard_map/ppermute | solution.py:80
  396.1 11.2 %collective-permute-start.82 = (bf16[4,3,8,768]{3,2,1,0:T(8,128)(2,1)}, bf16[4,3,8,768]{3,2,1,0:T(8,128)(2,1)}, u32[]{:S(2)}, u32[]{:S(2)}) collective-permute-start(bf16[4,3,8,768]{3,2,1,0:T(8,128)(2,1)} %get-tuple-element.301), channel_id=1, source_target_pairs={{0,16},{4,20},{8,24},{12,28},{16,0},{20,4},{24,8},{28,12},{1,17},{... | collective-permute-start | bytes 442376 | tf_op jit(solution)/shard_map/ppermute | solution.py:80
  412.1 11.1 %collective-permute-start.85 = (f32[8,128]{1,0:T(8,128)S(1)}, f32[8,128]{1,0:T(8,128)S(1)}, u32[]{:S(2)}, u32[]{:S(2)}) collective-permute-start(f32[8,128]{1,0:T(8,128)S(1)} %broadcast_in_dim.239), channel_id=1, source_target_pairs={{0,1},{1,0},{2,3},{3,2},{4,5},{5,4},{6,7},{7,6},{8,9},{9,8},{10,11... | collective-permute-start | bytes 12296 | tf_op jit(solution)/shard_map/ppermute | solution.py:35
  427.0 10.2 %collective-permute-start.80 = (f32[56,896]{1,0:T(8,128)S(1)}, f32[56,896]{1,0:T(8,128)S(1)}, u32[]{:S(2)}, u32[]{:S(2)}) collective-permute-start(f32[56,896]{1,0:T(8,128)S(1)} %add.467), channel_id=1, source_target_pairs={{0,16},{4,20},{8,24},{12,28},{16,0},{20,4},{24,8},{28,12},{1,17},{... | collective-permute-start | bytes 602120 | tf_op jit(solution)/shard_map/ppermute | solution.py:35
  433.4 15.8 %collective-permute-start.87 = (bf16[16,8,768]{2,1,0:T(8,128)(2,1)}, bf16[16,8,768]{2,1,0:T(8,128)(2,1)S(1)}, u32[]{:S(2)}, u32[]{:S(2)}) collective-permute-start(bf16[16,8,768]{2,1,0:T(8,128)(2,1)} %get-tuple-element.198), channel_id=1, source_target_pairs={{0,4},{4,0},{8,12},{12,8},{16,20},{20,16},{24,28},{28,24},{1,5},{5... | collective-permute-start | bytes 589832 | tf_op jit(solution)/shard_map/ppermute | solution.py:280
  434.4 16.0 %collective-permute-start.88 = (bf16[16,8,768]{2,1,0:T(8,128)(2,1)}, bf16[16,8,768]{2,1,0:T(8,128)(2,1)}, u32[]{:S(2)}, u32[]{:S(2)}) collective-permute-start(bf16[16,8,768]{2,1,0:T(8,128)(2,1)} %get-tuple-element.199), channel_id=1, source_target_pairs={{0,8},{4,12},{8,0},{12,4},{16,24},{20,28},{24,16},{28,20},{1,9},{5... | collective-permute-start | bytes 589832 | tf_op jit(solution)/shard_map/ppermute | solution.py:280
  434.7 20.7 %collective-permute-start.89 = (bf16[16,8,768]{2,1,0:T(8,128)(2,1)}, bf16[16,8,768]{2,1,0:T(8,128)(2,1)}, u32[]{:S(2)}, u32[]{:S(2)}) collective-permute-start(bf16[16,8,768]{2,1,0:T(8,128)(2,1)} %get-tuple-element.200), channel_id=1, source_target_pairs={{0,12},{4,8},{8,4},{12,0},{16,28},{20,24},{24,20},{28,16},{1,13},{... | collective-permute-start | bytes 589832 | tf_op jit(solution)/shard_map/ppermute | solution.py:280
  436.9 21.9 %collective-permute-start.90 = (bf16[16,8,768]{2,1,0:T(8,128)(2,1)}, bf16[16,8,768]{2,1,0:T(8,128)(2,1)}, u32[]{:S(2)}, u32[]{:S(2)}) collective-permute-start(bf16[16,8,768]{2,1,0:T(8,128)(2,1)} %get-tuple-element.201), channel_id=1, source_target_pairs={{0,16},{4,20},{8,24},{12,28},{16,0},{20,4},{24,8},{28,12},{1,17},{... | collective-permute-start | bytes 589832 | tf_op jit(solution)/shard_map/ppermute | solution.py:280
  437.3 25.9 %collective-permute-start.91 = (bf16[16,8,768]{2,1,0:T(8,128)(2,1)}, bf16[16,8,768]{2,1,0:T(8,128)(2,1)}, u32[]{:S(2)}, u32[]{:S(2)}) collective-permute-start(bf16[16,8,768]{2,1,0:T(8,128)(2,1)} %get-tuple-element.202), channel_id=1, source_target_pairs={{0,20},{4,16},{8,28},{12,24},{16,4},{20,0},{24,12},{28,8},{1,21},{... | collective-permute-start | bytes 589832 | tf_op jit(solution)/shard_map/ppermute | solution.py:280
  449.2 18.5 %collective-permute-start.92 = (bf16[16,8,768]{2,1,0:T(8,128)(2,1)}, bf16[16,8,768]{2,1,0:T(8,128)(2,1)}, u32[]{:S(2)}, u32[]{:S(2)}) collective-permute-start(bf16[16,8,768]{2,1,0:T(8,128)(2,1)} %copy-done.8), channel_id=1, source_target_pairs={{0,24},{4,28},{8,16},{12,20},{16,8},{20,12},{24,0},{28,4},{1,25},{... | collective-permute-start | bytes 589832 | tf_op jit(solution)/shard_map/ppermute | solution.py:280
  450.5 20.5 %collective-permute-start.93 = (bf16[16,8,768]{2,1,0:T(8,128)(2,1)}, bf16[16,8,768]{2,1,0:T(8,128)(2,1)}, u32[]{:S(2)}, u32[]{:S(2)}) collective-permute-start(bf16[16,8,768]{2,1,0:T(8,128)(2,1)} %copy-done.7), channel_id=1, source_target_pairs={{0,28},{4,24},{8,20},{12,16},{16,12},{20,8},{24,4},{28,0},{1,29},{... | collective-permute-start | bytes 589832 | tf_op jit(solution)/shard_map/ppermute | solution.py:280
  (180 other events, 1333.2 us)

commit v3 on v2

--- a/solution.py
+++ b/solution.py
@@ -105,13 +105,18 @@
         if self.closed():
             self.pieces = jnp.stack(self.ring)
 
-    def halves(self):
-        units = self.pieces.shape[1] // 2
-        parts = tie(self.pieces[:, :units], self.pieces[:, units:])
-        both = Gather(), Gather()
-        for part, pieces in zip(both, parts):
+    def parts(self, count):
+        size = self.pieces.shape[1] // count
+        cuts = tie(*(self.pieces[:, i * size : (i + 1) * size] for i in range(count)))
+        parts = [Gather() for _ in cuts]
+        for part, pieces in zip(parts, cuts):
             part.pieces = pieces
-        return both
+        return parts
+
+    def units(self, first, last):
+        part = Gather()
+        part.pieces = lax.slice_in_dim(self.pieces, first, last, axis=2)
+        return part
 
     def laid(self):
         x, y = (0, 1) if self.done[-1] == "x" else (1, 0)
@@ -161,8 +166,9 @@
 
 
 def cut_far(grads, tail, x_first):
-    pieces = grads.astype(bfloat).reshape((2, 2, high(), 4) + tail)
-    return pieces if x_first else pieces.swapaxes(0, 1)
+    pieces = grads.astype(bfloat).reshape((high(), 2, 2, 4) + tail)
+    perm = [1, 2, 0, 3, 4, 5, 6] if x_first else [2, 1, 0, 3, 4, 5, 6]
+    return jnp.transpose(pieces, perm)
 
 
 def land(anchor, *streams):
@@ -267,8 +273,10 @@
     )(ids.astype(jnp.int32), source, square)
 
 
-def exchange_dp(blocks):
+def exchange_dp(blocks, before=None):
     count = lax.axis_size("dp")
+    if count != 8 and before is not None:
+        return exchange_dp(blocks), before()
     if count != 8:
         relative = jnp.arange(count) ^ lax.axis_index("dp")
         ranked = pick_blocks(jnp.stack(blocks), relative, (count,))[0]
@@ -276,16 +284,20 @@
         got = pick_blocks(got, relative, (count,))[0]
         return [got.reshape((-1,) + got.shape[2:])]
     got = [blocks[0]] * count
+    blocks = list(blocks)
+    value = None
     for k in (7, 6, 5, 4, 1, 2, 3):
+        if k == 1 and before is not None:
+            value, *blocks[1:4] = tie(before(), *blocks[1:4])
         got[k] = lax.ppermute(blocks[k], "dp", [(i, i ^ k) for i in range(count)])
-    return got
+    return got if before is None else (got, value)
 
 
 def adamw(weight, moment, square, grad, first_fix, second_fix):
     moment = beta_first * moment + (1.0 - beta_first) * grad
     square = beta_second * square + (1.0 - beta_second) * grad * grad
-    update = (moment / first_fix) / (
-        jnp.sqrt(square / second_fix) + adam_epsilon
+    update = (moment * first_fix) / (
+        jnp.sqrt(square * second_fix) + adam_epsilon
     ) + decay_rate * weight
     return (weight - learn_rate * update, moment, square)
 
@@ -340,11 +352,12 @@
     routed = [item.reshape((-1, 3 * slots + 1, rows, depth)) for item in routed]
     per = routed[0].shape[0]
     big = pl.BlockSpec((1, 3, head, depth), lambda s, *_: (s, 0, 0, 0))
-    small = pl.BlockSpec(latent_grad.shape, lambda s, *_: (0, 0, 0))
+    latents_shape = (latent_grad.shape[1], 2, depth)
+    small = pl.BlockSpec(latents_shape, lambda s, *_: (0, 0, 0))
     out = pl.pallas_call(
         functools.partial(adam_kernel, len(routed)),
         out_shape=[jax.ShapeDtypeStruct((slots, 3, head, depth), single)] * 3
-        + [jax.ShapeDtypeStruct(item.shape, single) for item in latents]
+        + [jax.ShapeDtypeStruct(latents_shape, single) for _ in latents]
         + [jax.ShapeDtypeStruct((8, 128), single)],
         grid_spec=pltpu.PrefetchScalarGridSpec(
             num_scalar_prefetch=3,
@@ -364,7 +377,7 @@
             out_specs=[big] * 3 + [small] * 3 + [pl.BlockSpec((8, 128), lambda s, *_: (0, 0))],
             scratch_shapes=[pltpu.VMEM((3, head, depth), single)],
         ),
-        compiler_params=pltpu.CompilerParams(vmem_limit_bytes=40 << 20),
+        compiler_params=pltpu.CompilerParams(vmem_limit_bytes=60 << 20),
     )(
         me,
         kind,
@@ -374,11 +387,11 @@
         slot_out.reshape(slots, clips, 3, head).swapaxes(1, 2),
         slot_in,
         *(item.reshape(slots, 3, head, depth) for item in held),
-        latent_grad,
-        *latents,
+        latent_grad.swapaxes(0, 1),
+        *(item.swapaxes(0, 1) for item in latents),
     )
     places = [item.reshape(slots, width, depth) for item in out[:3]]
-    return places + list(out[3:6]) + [out[6][0, 0]]
+    return places + [item.swapaxes(0, 1) for item in out[3:6]] + [out[6][0, 0]]
 
 
 def normed(values):
@@ -556,7 +569,34 @@
     blocks = [
         lax.dynamic_index_in_dim(split, index ^ k, 2, keepdims=False) for k in range(n_dp)
     ]
-    got = exchange_dp(blocks)
+    def gather_packed():
+        values = packed
+        for i, bit in enumerate(reversed(range(dp_bits()))):
+            values = jnp.stack([values, swap(values, "dp", bit)], axis=i)
+        return values.reshape(n_dp * clips, -1)
+
+    got, packed = exchange_dp(blocks, gather_packed)
+
+    sinus_low = packed[:, :D].astype(bfloat)
+    pooled_low = packed[:, D : 2 * D].astype(bfloat)
+    weight_total = jnp.sum(packed[:, 2 * D])
+
+    def held(u):
+        return lax.dynamic_index_in_dim(master_low, place[u], 0, keepdims=False)
+
+    zero = jnp.zeros((), bfloat)
+    cond_part = matmul(
+        "bd,ed->be", jnp.where(owner[24] == index, sinus_low, zero), held(24)
+    ) + matmul("bd,ed->be", jnp.where(owner[25] == index, pooled_low, zero), held(25))
+    row = jnp.arange(n_dp * clips)
+    reorder = (row[:, None] ^ (index * clips)) == row[None, :]
+    reorder = reorder.astype(single)
+
+    def reordered(values):
+        return jnp.einsum("bc,cd->bd", reorder, values, precision=highest)
+
+    cond_part = pair(reordered(cond_part), 1, "mx")
+    cond_part, *got = tie(cond_part, *got)
     unit_of = jnp.sum(
         jnp.where(
             unit_slot[None, :] == jnp.arange(n_dp * slots)[:, None],
@@ -572,89 +612,63 @@
         ]
     )
     unit_at = lax.dynamic_index_in_dim(table, index, 0, keepdims=False).reshape(-1)
-    chunk_self, chunk_cross, chunk_far = place_blocks(got, unit_at, (4, 4, 8))
-    unit_tail = chunk_far.shape[1:]
-    chunk_self, packed = tie(chunk_self, packed)
-    near, cross, far = Gather(chunk_self), Gather(chunk_cross), Gather(chunk_far)
-
+    chunk_near, chunk_cross, chunk_up, chunk_down = place_blocks(got, unit_at, (4, 4, 4, 4))
+    unit_tail = chunk_near.shape[1:]
+    chunk_near, chunk_up, chunk_down, cond_part = tie(
+        chunk_near, chunk_up, chunk_down, cond_part
+    )
+    near, cross = Gather(chunk_near), Gather(chunk_cross)
     near.send_ring()
-    packed = packed[None]
+    got_up, got_down = swap(chunk_up, "dp", 0), swap(chunk_down, "mx")
+    cond_part = pair(cond_part, 2, "mc").reshape(n_dp * clips, D)
     for bit in range(dp_bits()):
-        packed = jnp.concatenate([packed, swap(packed, "dp", bit)], axis=0)
+        cond_part = cond_part + swap(cond_part, "dp", bit)
         if bit < 3:
-            packed = land(packed, near)
+            cond_part = land(cond_part, near)
             if bit < 2:
                 near.send_ring()
-    near_a, near_b = near.halves()
-    near_a.pieces, near_b.pieces, cross.ring[0] = tie(
-        near_a.pieces, near_b.pieces, cross.ring[0]
-    )
-    near_a.send(0)
-    near_b.send("x")
-    cross.send_ring()
-    packed = packed.reshape(n_dp * clips, -1)
-    sinus_low = packed[:, :D].astype(bfloat)
-    pooled_low = packed[:, D : 2 * D].astype(bfloat)
-    weight_total = jnp.sum(packed[:, 2 * D])
-
-    def held(u):
-        return lax.dynamic_index_in_dim(master_low, place[u], 0, keepdims=False)
-
-    zero = jnp.zeros((), bfloat)
-    cond_part = matmul(
-        "bd,ed->be", jnp.where(owner[24] == index, sinus_low, zero), held(24)
-    ) + matmul("bd,ed->be", jnp.where(owner[25] == index, pooled_low, zero), held(25))
-    row = jnp.arange(n_dp * clips)
-    reorder = (row[:, None] ^ (index * clips)) == row[None, :]
-    reorder = reorder.astype(single)
-
-    def reordered(values):
-        return jnp.einsum("bc,cd->bd", reorder, values, precision=highest)
-
-    cond_part = reordered(cond_part)
-    cond_part = cond_part + swap(cond_part, "dp", 0)
-    for bit in range(1, dp_bits()):
-        cond_part = cond_part + swap(cond_part, "dp", bit)
         if bit == 1:
-            cond_part = land(cond_part, near_a, near_b, cross)
-            near_a.send("x")
-            near_b.send(0)
-            cross.send_ring()
-    cond_part = land(cond_part, cross)
-    cross.send_ring()
-    cond = pair(pair(cond_part, 1, "mc"), 1, "mx").reshape(n_dp * clips, D)
-    cond = tie(reordered(cond))[0]
+            cond_part, got_up, got_down = tie(cond_part, got_up, got_down)
+    far = Gather(jnp.stack([chunk_up, got_up, chunk_down, got_down]).reshape((2, 2, 4) + unit_tail))
+    cond = tie(reordered(cond_part))[0]
     active = jax.nn.silu(cond).astype(bfloat)
     all_rows = matmul("bd,sed->bse", active, master_low)
     ada = pick[:, 16:24]
     rows = jnp.einsum("sj,bse->bje", ada.astype(single), all_rows, precision=highest)
     rows = rows.reshape(n_dp, clips, 8, width)
+    near_a, near_b = near.parts(2)
+    rows, near_a.pieces, near_b.pieces, cross.ring[0] = tie(
+        rows, near_a.pieces, near_b.pieces, cross.ring[0]
+    )
+    near_a.send(0)
+    near_b.send("x")
+    cross.send_ring()
+    for bit in reversed(range(1, dp_bits())):
+        half = rows.shape[0] // 2
+        rows = rows[:half] + swap(rows[half:], "dp", bit)
+        if bit == 2:
+            rows = land(rows, near_a, near_b, cross)
+            near_a.send("x")
+            near_b.send(0)
+            cross.send_ring()
+    rows = land(rows, cross)
+    rows, far.ring[0] = tie(rows, far.ring[0])
+    cross.send_ring()
+    far.send_ring()
+    mine = lax.dynamic_index_in_dim(rows, clip, 1, keepdims=False)
+    theirs = swap(lax.dynamic_index_in_dim(rows, 1 - clip, 1, keepdims=False), "mx")
+    rows = jnp.stack(
+        [jnp.where(clip == 0, mine, theirs), jnp.where(clip == 0, theirs, mine)], axis=2
+    )
     rows = land(rows, near_a, near_b, cross)
-    cross_a, cross_b = cross.halves()
-    cross_a.pieces, cross_b.pieces, far.ring[0] = tie(
-        cross_a.pieces, cross_b.pieces, far.ring[0]
-    )
+    rows = rows[0] + swap(rows[1], "dp", 0)
+    cross_a, cross_b = cross.parts(2)
+    rows, cross_a.pieces, cross_b.pieces = tie(rows, cross_a.pieces, cross_b.pieces)
+    rows = land(rows, far)
     cross_a.send(0)
     cross_b.send("x")
     far.send_ring()
-    for bit in reversed(range(dp_bits())):
-        half = rows.shape[0] // 2
-        rows = rows[:half] + swap(rows[half:], "dp", bit)
-        if bit == 2:
-            rows = land(rows, far)
-            far.send_ring()
-        if bit == 0:
-            rows = land(rows, far, cross_a, cross_b)
-            cross_a.send("x")
-            cross_b.send(0)
-            far.send_ring()
-    rows = rows[0]
-    mine = lax.dynamic_index_in_dim(rows, clip, 0, keepdims=False)
-    theirs = swap(lax.dynamic_index_in_dim(rows, 1 - clip, 0, keepdims=False), "mx")
-    by_x = jnp.stack(
-        [jnp.where(clip == 0, mine, theirs), jnp.where(clip == 0, theirs, mine)], axis=1
-    )
-    modulation = tie(pair(by_x, 2, "mc").reshape(8, D))[0]
+    modulation = tie(pair(rows, 2, "mc").reshape(8, D))[0]
 
     text = lax.dynamic_index_in_dim(captions, clip, 0, keepdims=False)
     text_len = lax.dynamic_index_in_dim(caption_len, clip, 0, keepdims=False)
@@ -672,37 +686,54 @@
     hidden_zero = jnp.einsum("fc,cd->fd", noisy, latent_master[0], precision=highest)
     first_in = spread(modulate(hidden_zero, modulation[0], modulation[1]).astype(bfloat))
     w_self = jnp.concatenate([near_a.laid(), near_b.laid()], axis=0)
-    first_in = land(first_in, far)
-    up, down = far.halves()
-    up.send(0)
-    down.send("x")
     self_query, self_keys, self_values = (
         matmul("fd,ed->fe", first_in, w_self[u]).astype(bfloat) for u in range(3)
     )
-    self_query = land(self_query, cross_a, cross_b)
     self_flat, self_total = attention(self_query, self_keys, self_values, None)
-    self_flat = land(self_flat, up, down)
-    up.send("x")
-    down.send(0)
+    self_flat = land(self_flat, cross_a, cross_b, far)
+    cross_a.send("x")
+    cross_b.send(0)
+    far.send_ring()
+    self_branch = collect(self_flat, w_self[3])
+    hidden_one = hidden_zero + modulation[2] * self_branch
+    second_in = spread(normed(hidden_one).astype(bfloat))
+    second_in = land(second_in, cross_a, cross_b, far)
+    ups, downs = far.parts(2)
+    ups.pieces, downs.pieces = ups.pieces[:, 0], downs.pieces[:, 0]
+    last = []
+    for i in range(2):
+        last += [ups.units(2 * i, 2 * i + 2), downs.units(2 * i, 2 * i + 2)]
+    cuts = tie(*(item.pieces for item in last))
+    for item, pieces in zip(last, cuts):
+        item.pieces = pieces
+    last[0].send("x")
+    last[1].send(0)
     w_cross = jnp.concatenate([cross_a.laid(), cross_b.laid()], axis=0)
     weights = [w_self[i] for i in range(4)] + [w_cross[i] for i in range(4)]
-    self_branch = collect(self_flat, weights[3])
-    hidden_one = hidden_zero + modulation[2] * self_branch
-    second_in = spread(normed(hidden_one).astype(bfloat))
     cross_query = matmul("fd,ed->fe", second_in, weights[4]).astype(bfloat)
     cross_keys = matmul("ld,ed->le", text, weights[5]).astype(bfloat)
     cross_values = matmul("ld,ed->le", text, weights[6]).astype(bfloat)
     cross_flat, cross_total = attention(cross_query, cross_keys, cross_values, text_len)
+    cross_flat, *far_got = tie(cross_flat, last[0].got, last[1].got)
+    cross_flat, last[2].pieces, last[3].pieces = tie(
+        cross_flat, last[2].pieces, last[3].pieces
+    )
+    last[2].send("x")
+    last[3].send(0)
     cross_branch = collect(cross_flat, weights[7])
     hidden_two = hidden_one + cross_branch
     third_in = spread(modulate(hidden_two, modulation[3], modulation[4]).astype(bfloat))
-    third_in = land(third_in, up)
-    w_up = up.pieces.reshape(-1, D)
+    third_in, *more = tie(third_in, last[2].got, last[3].got)
+    far_got += more
+    w_up, w_down = (
+        jnp.concatenate(
+            [jnp.stack([last[i].pieces, far_got[i]], axis=axis) for i in (part, part + 2)], axis=3
+        ).reshape(-1, D)
+        for part, axis in ((0, 1), (1, 2))
+    )
     upper = matmul("fd,kd->fk", third_in, w_up).astype(bfloat)
     upper_wide = upper.astype(single)
     activated = jax.nn.gelu(upper_wide, approximate=True).astype(bfloat)
-    activated, got = tie(activated, down.got)
-    w_down = jnp.stack([down.pieces, got], axis=1).reshape(-1, D)
     mlp_branch = collect(activated, w_down)
     hidden_three = hidden_two + modulation[5] * mlp_branch
     final_wide = modulate(hidden_three, modulation[6], modulation[7]).astype(bfloat).astype(single)
@@ -792,10 +823,11 @@
     grad_mod = (grad_mod + swap(grad_mod, "mc")).astype(bfloat)
     for i, bit in enumerate(reversed(range(1, dp_bits()))):
         grad_mod = jnp.stack([grad_mod, swap(grad_mod, "dp", bit)], axis=i)
-    grad_mod = land(grad_mod, near_a, near_b, cross)
-    near = near_a.join(near_b).pieces
-    z_got = [shift(near[j], -j) for j in range(1, high())]
-    cross.send_ring()
+        if i == 0:
+            grad_mod = land(grad_mod, near_a, near_b, cross)
+            near = near_a.join(near_b).pieces
+            z_got = [shift(near[j], -j) for j in range(1, high())]
+            cross.send_ring()
     grad_mod = pair(grad_mod, dp_bits() - 1, "mx")
     grad_mod = jnp.stack([grad_mod, swap(grad_mod, "dp", 0)], axis=dp_bits() - 1)
     grad_mod = tie(grad_mod.reshape(n_dp * clips, 8, D))[0]
@@ -813,11 +845,7 @@
         ],
         axis=0,
     )
-    mixed = sum_dp(sum_mp(mixed))
-    grad_active, small = reordered(mixed[: n_dp * clips, :D]), mixed[n_dp * clips :]
-    latent_grad = small[:, :D].reshape(2, C, D)
-    loss_sum = small[0, D]
-
+    mixed = sum_mp(mixed)
     total = near[0].astype(single)
     for item in z_got:
         total = total + item.astype(single)
@@ -826,6 +854,11 @@
     reduced = jnp.concatenate(reduced, axis=0)
     wide_square = sum_mp(jnp.broadcast_to(jnp.sum(reduced * reduced), (8, 128)))
     wide_at = jnp.where((unit_at >= 0) & (unit_at < WIDE), unit_at, 0)
+    wide_square, mixed = tie(wide_square, mixed)
+    mixed = sum_dp(mixed)
+    grad_active, small = reordered(mixed[: n_dp * clips, :D]), mixed[n_dp * clips :]
+    latent_grad = small[:, :D].reshape(2, C, D)
+    loss_sum = small[0, D]
     routes = route_blocks(reduced.astype(bfloat), wide_at, wide_square, n_dp)
     routed = exchange_dp(routes)
     _, silu_back = jax.vjp(jax.nn.silu, cond)
@@ -852,7 +885,7 @@
     count = step_count[0].astype(single)
     is_wide = jnp.any(pick[:, :WIDE], axis=1)
     kind = jnp.where(is_wide, 1, jnp.where(live_slot, 2, 0)).astype(jnp.int32)
-    fixes = [1.0 - jnp.power(beta_first, count), 1.0 - jnp.power(beta_second, count)]
+    fixes = [1.0 / (1.0 - jnp.power(beta, count)) for beta in (beta_first, beta_second)]
     *outputs, grad_norm = adam_places(
         index.reshape(1).astype(jnp.int32),
         kind,

time: 500 us -> 478 us (0.956)
  local copies, waits for them, and re-layouts: 52 us -> 44.5 us
  other arithmetic: 47.1 us -> 40.3 us
  starting transfers between devices: 111 us -> 105 us
    unnamed x280 -> x320, local copies, waits for them, and re-layouts: 28.7 us -> 17.9 us
    ppermute x18, starting transfers between devices: 26.6 us -> 19.6 us  [shift(): lax.ppermute(values, 'dp', [(i, (i + 2 * by) % count) for i in range(coun...]
    ppermute x62 -> x64, waiting for transfers between devices: 104 us -> 101 us  [swap(): return lax.ppermute(values, axis, [(i, i ^ 1 << bit) for i in range(count)])]
    ppermute x62 -> x64, starting transfers between devices: 64.9 us -> 67 us  [swap(): return lax.ppermute(values, axis, [(i, i ^ 1 << bit) for i in range(count)])]
  transfers between devices with their start and end apart: 94 -> 96, of which waited for: 50 -> 47; matrix products, arithmetic and copies ran while one was open for 18% -> 15% of each run, Pallas kernels for 6% -> 7%
where the time goes in v3:
time: 478 us; the launch traced here: 470 us
  waiting for transfers between devices  164 us (34%)
  starting transfers between devices  105 us (22%)
  matrix products  56.1 us (12%)
  local copies, waits for them, and re-layouts  44.5 us (9%)
  Pallas kernels  44.1 us (9%)
  other arithmetic  40.3 us (8%)
  between operations  15.5 us (3%)
    ppermute x64, waiting for transfers between devices, swap(): return lax.ppermute(values, axis, [(i, i ^ 1 << bit) for i in range(count)])  101 us
    ppermute x64, starting transfers between devices, swap(): return lax.ppermute(values, axis, [(i, i ^ 1 << bit) for i in range(count)])  67 us
    dot_general x40, matrix products, matmul(): return jnp.einsum(form, left, right, preferred_element_type=single)  46.8 us
    ppermute x18, waiting for transfers between devices, shift(): lax.ppermute(values, 'dp', [(i, (i + 2 * by) % count) for i in range(coun...  35 us
    pallas_call x4, Pallas kernels, pair_call(): pl.pallas_call(functools.partial(kernel, masked), out_shape=outs, grid_sp...  29.8 us
    ppermute x14, waiting for transfers between devices, exchange_dp(): got[k] = lax.ppermute(blocks[k], 'dp', [(i, i ^ k) for i in range(count)])  27.7 us
    ppermute x18, starting transfers between devices, shift(): lax.ppermute(values, 'dp', [(i, (i + 2 * by) % count) for i in range(coun...  19.6 us
    ppermute x14, starting transfers between devices, exchange_dp(): got[k] = lax.ppermute(blocks[k], 'dp', [(i, i ^ k) for i in range(count)])  18.6 us
  transfers between devices with their start and end apart: 96, of which 47 were waited for; matrix products, arithmetic and copies ran while one was open for 15% of the time, Pallas kernels for 7%

profile of v3, /device:TPU:8, one launch (start us, length us, event | category | flops | bytes accessed | tf_op | source)
XLA Modules:
  0.0 469.6 jit_solution(6369654580934142775)
XLA Ops:
  5.3 2.6 collective-permute-start
  11.3 2.7 collective-permute-start.9
  26.2 4.3 collective-permute-done.1
  45.6 3.0 collective-permute-done.4.refs_1_
  49.0 3.8 collective-permute-done.6.refs_3_
  61.8 3.5 collective-permute-start.14
  67.5 3.0 collective-permute-done.15
  70.8 4.2 collective-permute-start.18
  75.2 3.4 collective-permute-done.18
  87.7 3.4 collective-permute-done.24
  91.2 2.5 collective-permute-start.25
  96.3 4.1 collective-permute-done.26
  105.0 2.7 collective-permute-done.30
  109.1 2.5 collective-permute-done.31
  111.6 2.5 collective-permute-done.32
  124.4 7.6 %shard_map.270 = (bf16[768,384]{1,0:T(8,128)(2,1)S(1)}, f32[3,2,768]{2,1,0:T(2,128)S(1)}) custom-call(s32[1]{0:T(128)} %constant.191.clone.1.length, bf16[768,384]{1,0:T(8,128)(2,1)S(1)} %convolution_convert_fusion.19.query, bf16[768,384]{1,0:T(8,128)(2,1)S(1)} %convolution_convert_fusion.18.keys, bf16[768,384]{1,0:T(8,128)(2,1)S(1)} %convolution_convert_fusion.17.values), custom_call_target="tpu_custom_call" | custom-call | flops 3623878656 | bytes 8388608 | tf_op jit(solution)/shard_map/pallas_call | solution.py:481
  132.0 4.7 collective-permute-done.37
  145.8 11.8 %collective-permute-done.40 = bf16[2,4,2,3,8,768]{5,4,3,2,1,0:T(8,128)(2,1)S(1)} collective-permute-done((bf16[2,4,2,3,8,768]{5,4,3,2,1,0:T(8,128)(2,1)S(1)}, bf16[2,4,2,3,8,768]{5,4,3,2,1,0:T(8,128)(2,1)S(1)}, u32[]{:S(2)}, u32[]{:S(2)}) %collective-permute-start.40) | collective-permute-done | bytes 589856 | tf_op jit(solution)/shard_map/ppermute | solution.py:35
  158.8 3.1 collective-permute-done.42
  168.3 4.7 shard_map.271
  173.0 7.4 %collective-permute-done.43 = bf16[4,2,2,3,8,768]{5,4,3,2,1,0:T(8,128)(2,1)S(1)} collective-permute-done((bf16[4,2,2,3,8,768]{5,4,3,2,1,0:T(8,128)(2,1)S(1)}, bf16[4,2,2,3,8,768]{5,4,3,2,1,0:T(8,128)(2,1)S(1)}, u32[]{:S(2)}, u32[]{:S(2)}) %collective-permute-start.43) | collective-permute-done | bytes 589856 | tf_op jit(solution)/shard_map/ppermute | solution.py:35
  186.6 13.5 %collective-permute-done.47 = bf16[4,2,2,3,8,768]{5,4,3,2,1,0:T(8,128)(2,1)S(1)} collective-permute-done((bf16[4,2,2,3,8,768]{5,4,3,2,1,0:T(8,128)(2,1)S(1)}, bf16[4,2,2,3,8,768]{5,4,3,2,1,0:T(8,128)(2,1)S(1)}, u32[]{:S(2)}, u32[]{:S(2)}) %collective-permute-start.47) | collective-permute-done | bytes 589856 | tf_op jit(solution)/shard_map/ppermute | solution.py:35
  202.1 4.2 fusion.7
  212.1 4.3 fusion.177
  219.4 2.7 multiply_reduce_fusion.2
  226.9 4.9 %convolution_convert_fusion.1 = bf16[1536,768]{1,0:T(8,128)(2,1)S(1)} fusion(bf16[384,768]{1,0:T(8,128)(2,1)} %collective-permute-done.50, bf16[384,768]{1,0:T(8,128)(2,1)} %multiply_convert_fusion.1, bf16[768,1536]{1,0:T(8,128)(2,1)} %get-tuple-element.382), kind=kOutput, calls=%fused_computation.24 | convolution fusion | flops 1827274752 | bytes 5898240 | tf_op jit(solution)/shard_map/fk,fd->kd/dot_general | solution.py:420
  235.3 4.4 fusion.3
  258.9 6.0 %shard_map.272 = (bf16[768,384]{1,0:T(8,128)(2,1)S(1)}, bf16[256,384]{1,0:T(8,128)(2,1)S(1)}, bf16[256,384]{1,0:T(8,128)(2,1)S(1)}) custom-call(s32[1]{0:T(128)} %dynamic_slice.90.length, bf16[768,384]{1,0:T(8,128)(2,1)S(1)} %convolution_convert_fusion.15.query, bf16[256,384]{1,0:T(8,128)(2,1)S(1)} %convolution_convert_fusion.21.keys, ...), custom_call_target="tpu_custom_call" | custom-call | flops 3019898880 | bytes 8388608 | tf_op jit(solution)/shard_map/pallas_call | solution.py:481
  270.9 11.3 %collective-permute-done.53 = bf16[2,4,4,3,8,768]{5,4,3,2,1,0:T(8,128)(2,1)} collective-permute-done((bf16[2,4,4,3,8,768]{5,4,3,2,1,0:T(8,128)(2,1)}, bf16[2,4,4,3,8,768]{5,4,3,2,1,0:T(8,128)(2,1)}, u32[]{:S(2)}, u32[]{:S(2)}) %collective-permute-start.53) | collective-permute-done | bytes 1179680 | tf_op jit(solution)/shard_map/ppermute | solution.py:35
  282.2 2.7 collective-permute-done.54
  298.4 6.9 %collective-permute-done.58 = bf16[4,4,3,8,768]{4,3,2,1,0:T(8,128)(2,1)S(1)} collective-permute-done((bf16[4,4,3,8,768]{4,3,2,1,0:T(8,128)(2,1)S(1)}, bf16[4,4,3,8,768]{4,3,2,1,0:T(8,128)(2,1)S(1)}, u32[]{:S(2)}, u32[]{:S(2)}) %collective-permute-start.58) | collective-permute-done | bytes 589856 | tf_op jit(solution)/shard_map/ppermute | solution.py:35
  305.4 3.8 collective-permute-done.57
  310.7 11.5 %shard_map.273 = (bf16[768,384]{1,0:T(8,128)(2,1)S(1)}, bf16[768,384]{1,0:T(8,128)(2,1)S(1)}, bf16[768,384]{1,0:T(8,128)(2,1)S(1)}) custom-call(s32[1]{0:T(128)} %constant.191.clone.1.length, bf16[768,384]{1,0:T(8,128)(2,1)S(1)} %copy-done.6, bf16[768,384]{1,0:T(8,128)(2,1)S(1)} %copy-done.2, bf16[768,384]{1,0:T(8,128)(2,1)S(1)} %copy-done.4, ...), custom_call_target="tpu_custom_call" | custom-call | flops 9059696640 | bytes 8388608 | tf_op jit(solution)/shard_map/pallas_call | solution.py:481
  328.9 4.6 collective-permute-done.67
  345.1 3.8 collective-permute-start.66
  367.5 2.7 collective-permute-start.81
  371.5 2.5 collective-permute-start.78
  374.3 4.4 collective-permute-start.79
  379.2 5.1 %collective-permute-done.78 = bf16[4,3,8,768]{3,2,1,0:T(8,128)(2,1)S(1)} collective-permute-done((bf16[4,3,8,768]{3,2,1,0:T(8,128)(2,1)S(1)}, bf16[4,3,8,768]{3,2,1,0:T(8,128)(2,1)S(1)}, u32[]{:S(2)}, u32[]{:S(2)}) %collective-permute-start.78) | collective-permute-done | bytes 147488 | tf_op jit(solution)/shard_map/ppermute | solution.py:80
  394.8 3.5 collective-permute-done.85
  399.1 5.2 %collective-permute-done.86 = f32[56,896]{1,0:T(8,128)S(1)} collective-permute-done((f32[56,896]{1,0:T(8,128)S(1)}, f32[56,896]{1,0:T(8,128)S(1)}, u32[]{:S(2)}, u32[]{:S(2)}) %collective-permute-start.86) | collective-permute-done | bytes 200736 | tf_op jit(solution)/shard_map/ppermute | solution.py:35
  407.4 2.8 collective-permute-done.87
  410.2 3.4 collective-permute-start.88
  416.5 2.9 collective-permute-start.91
  420.9 3.3 collective-permute-start.93
  433.9 12.4 %collective-permute-done.93 = bf16[16,8,768]{2,1,0:T(8,128)(2,1)S(1)} collective-permute-done((bf16[16,8,768]{2,1,0:T(8,128)(2,1)S(1)}, bf16[16,8,768]{2,1,0:T(8,128)(2,1)S(1)}, u32[]{:S(2)}, u32[]{:S(2)}) %collective-permute-start.93) | collective-permute-done | bytes 196640 | tf_op jit(solution)/shard_map/ppermute | solution.py:292
  446.2 5.2 %collective-permute-done.94 = bf16[16,8,768]{2,1,0:T(8,128)(2,1)S(1)} collective-permute-done((bf16[16,8,768]{2,1,0:T(8,128)(2,1)S(1)}, bf16[16,8,768]{2,1,0:T(8,128)(2,1)S(1)}, u32[]{:S(2)}, u32[]{:S(2)}) %collective-permute-start.94) | collective-permute-done | bytes 196640 | tf_op jit(solution)/shard_map/ppermute | solution.py:292
  454.2 11.9 %shard_map.275 = (f32[5,3,64,768]{3,2,1,0:T(8,128)}, f32[5,3,64,768]{3,2,1,0:T(8,128)}, f32[5,3,64,768]{3,2,1,0:T(8,128)}, f32[20,2,768]{2,1,0:T(2,128)}, f32[20...) custom-call(s32[1]{0:T(128)} %bitcast.me, s32[5]{0:T(128)} %select_select_fusion.1.kind, ...), custom_call_target="tpu_custom_call" | custom-call | tf_op jit(solution)/shard_map/pallas_call | solution.py:357
  (765 shorter events, 216.4 us)
Async XLA Ops:
  5.3 18.0 %collective-permute-start = (f32[2,1664]{1,0:T(2,128)S(1)}, f32[2,1664]{1,0:T(2,128)S(1)}, u32[]{:S(2)}, u32[]{:S(2)}) collective-permute-start(f32[2,1664]{1,0:T(2,128)S(1)} %pad_maximum_fusion.40), channel_id=1, source_target_pairs={{0,16},{4,20},{8,24},{12,28},{16,0},{20,4},{24,8},{28,12},{1,17},{... | collective-permute-start | bytes 39944 | tf_op jit(solution)/shard_map/ppermute | solution.py:35
  11.0 31.6 %collective-permute-start.10 = (bf16[5,3,8,768]{3,2,1,0:T(8,128)(2,1)}, bf16[5,3,8,768]{3,2,1,0:T(8,128)(2,1)S(1)}, u32[]{:S(2)}, u32[]{:S(2)}) collective-permute-start(bf16[5,3,8,768]{3,2,1,0:T(8,128)(2,1)} %get-tuple-element.303), channel_id=1, source_target_pairs={{0,28},{4,24},{8,20},{12,16},{16,12},{20,8},{24,4},{28,0},{1,29},{... | collective-permute-start | bytes 552968 | tf_op jit(solution)/shard_map/ppermute | solution.py:292
  11.3 31.3 %collective-permute-start.9 = (bf16[5,3,8,768]{3,2,1,0:T(8,128)(2,1)}, bf16[5,3,8,768]{3,2,1,0:T(8,128)(2,1)S(1)}, u32[]{:S(2)}, u32[]{:S(2)}) collective-permute-start(bf16[5,3,8,768]{3,2,1,0:T(8,128)(2,1)} %get-tuple-element.304), channel_id=1, source_target_pairs={{0,24},{4,28},{8,16},{12,20},{16,8},{20,12},{24,0},{28,4},{1,25},{... | collective-permute-start | bytes 552968 | tf_op jit(solution)/shard_map/ppermute | solution.py:292
  14.0 30.6 %collective-permute-start.8 = (bf16[5,3,8,768]{3,2,1,0:T(8,128)(2,1)}, bf16[5,3,8,768]{3,2,1,0:T(8,128)(2,1)S(1)}, u32[]{:S(2)}, u32[]{:S(2)}) collective-permute-start(bf16[5,3,8,768]{3,2,1,0:T(8,128)(2,1)} %get-tuple-element.305), channel_id=1, source_target_pairs={{0,20},{4,16},{8,28},{12,24},{16,4},{20,0},{24,12},{28,8},{1,21},{... | collective-permute-start | bytes 552968 | tf_op jit(solution)/shard_map/ppermute | solution.py:292
  16.1 29.5 %collective-permute-start.7 = (bf16[5,3,8,768]{3,2,1,0:T(8,128)(2,1)}, bf16[5,3,8,768]{3,2,1,0:T(8,128)(2,1)S(1)}, u32[]{:S(2)}, u32[]{:S(2)}) collective-permute-start(bf16[5,3,8,768]{3,2,1,0:T(8,128)(2,1)} %get-tuple-element.306), channel_id=1, source_target_pairs={{0,16},{4,20},{8,24},{12,28},{16,0},{20,4},{24,8},{28,12},{1,17},{... | collective-permute-start | bytes 552968 | tf_op jit(solution)/shard_map/ppermute | solution.py:292
  42.6 10.2 %collective-permute-start.6 = (bf16[5,3,8,768]{3,2,1,0:T(8,128)(2,1)S(1)}, bf16[5,3,8,768]{3,2,1,0:T(8,128)(2,1)S(1)}, u32[]{:S(2)}, u32[]{:S(2)}) collective-permute-start(bf16[5,3,8,768]{3,2,1,0:T(8,128)(2,1)S(1)} %get-tuple-element.142), channel_id=1, source_target_pairs={{0,12},{4,8},{8,4},{12,0},{16,28},{20,24},{24,20},{28,16},{1,13},{... | collective-permute-start | bytes 552968 | tf_op jit(solution)/shard_map/ppermute | solution.py:292
  44.6 10.2 %collective-permute-start.20 = (f32[2,192,20]{1,2,0:T(8,128)S(1)}, f32[2,192,20]{1,2,0:T(8,128)S(1)}, u32[]{:S(2)}, u32[]{:S(2)}) collective-permute-start(f32[2,192,20]{1,2,0:T(8,128)S(1)} %copy.173), channel_id=1, source_target_pairs={{0,2},{2,0},{1,3},{3,1},{4,6},{6,4},{5,7},{7,5},{8,10},{10,8},{9,1... | collective-permute-start | bytes 92168 | tf_op jit(solution)/shard_map/ppermute | solution.py:35
  58.0 12.8 %collective-permute-start.16 = (bf16[4,3,8,768]{3,2,1,0:T(8,128)(2,1)S(1)}, bf16[4,3,8,768]{3,2,1,0:T(8,128)(2,1)S(1)}, u32[]{:S(2)}, u32[]{:S(2)}) collective-permute-start(bf16[4,3,8,768]{3,2,1,0:T(8,128)(2,1)S(1)} %get-tuple-element.160), channel_id=1, source_target_pairs={{0,4},{4,0},{8,12},{12,8},{16,20},{20,16},{24,28},{28,24},{1,5},{5... | collective-permute-start | bytes 442376 | tf_op jit(solution)/shard_map/ppermute | solution.py:35
  59.6 11.2 %collective-permute-start.17 = (bf16[4,3,8,768]{3,2,1,0:T(8,128)(2,1)S(1)}, bf16[4,3,8,768]{3,2,1,0:T(8,128)(2,1)S(1)}, u32[]{:S(2)}, u32[]{:S(2)}) collective-permute-start(bf16[4,3,8,768]{3,2,1,0:T(8,128)(2,1)S(1)} %get-tuple-element.161), channel_id=1, source_target_pairs={{0,2},{2,0},{1,3},{3,1},{4,6},{6,4},{5,7},{7,5},{8,10},{10,8},{9,1... | collective-permute-start | bytes 442376 | tf_op jit(solution)/shard_map/ppermute | solution.py:35
  93.9 13.9 %collective-permute-start.28 = (bf16[2,4,2,3,8,768]{5,4,3,2,1,0:T(8,128)(2,1)S(1)}, bf16[2,4,2,3,8,768]{5,4,3,2,1,0:T(8,128)(2,1)S(1)}, u32[]{:S(2)}, u32[]{:S(2)}) collective-permute-start(bf16[2,4,2,3,8,768]{5,4,3,2,1,0:T(8,128)(2,1)S(1)} %get-tuple-element.337), channel_id=1, source_target_pairs={{0,2},{2,0},{1,3},{3,1},{4,6},{6,4},{5,7},{7,5},{8,10},{10,8},{9,1... | collective-permute-start | bytes 1769480 | tf_op jit(solution)/shard_map/ppermute | solution.py:35
  95.6 12.2 %collective-permute-start.29 = (bf16[2,4,2,3,8,768]{5,4,3,2,1,0:T(8,128)(2,1)S(1)}, bf16[2,4,2,3,8,768]{5,4,3,2,1,0:T(8,128)(2,1)S(1)}, u32[]{:S(2)}, u32[]{:S(2)}) collective-permute-start(bf16[2,4,2,3,8,768]{5,4,3,2,1,0:T(8,128)(2,1)S(1)} %get-tuple-element.333), channel_id=1, source_target_pairs={{0,4},{4,0},{8,12},{12,8},{16,20},{20,16},{24,28},{28,24},{1,5},{5... | collective-permute-start | bytes 1769480 | tf_op jit(solution)/shard_map/ppermute | solution.py:35
  101.0 13.1 %collective-permute-start.32 = (bf16[2,2,4,3,8,768]{5,4,3,2,1,0:T(8,128)(2,1)S(1)}, bf16[2,2,4,3,8,768]{5,4,3,2,1,0:T(8,128)(2,1)S(1)}, u32[]{:S(2)}, u32[]{:S(2)}) collective-permute-start(bf16[2,2,4,3,8,768]{5,4,3,2,1,0:T(8,128)(2,1)S(1)} %bitcast.518), channel_id=1, source_target_pairs={{0,8},{4,12},{8,16},{12,20},{16,24},{20,28},{24,0},{28,4},{1,9},{5... | collective-permute-start | bytes 1769480 | tf_op jit(solution)/shard_map/ppermute | solution.py:80
  119.6 12.3 %collective-permute-start.35 = (bf16[4,2,3,8,768]{4,3,2,1,0:T(8,128)(2,1)S(1)}, bf16[4,2,3,8,768]{4,3,2,1,0:T(8,128)(2,1)S(1)}, u32[]{:S(2)}, u32[]{:S(2)}) collective-permute-start(bf16[4,2,3,8,768]{4,3,2,1,0:T(8,128)(2,1)S(1)} %copy-done.52), channel_id=1, source_target_pairs={{0,4},{4,0},{8,12},{12,8},{16,20},{20,16},{24,28},{28,24},{1,5},{5... | collective-permute-start | bytes 884744 | tf_op jit(solution)/shard_map/ppermute | solution.py:35
  120.1 11.8 %collective-permute-start.36 = (bf16[4,2,3,8,768]{4,3,2,1,0:T(8,128)(2,1)S(1)}, bf16[4,2,3,8,768]{4,3,2,1,0:T(8,128)(2,1)S(1)}, u32[]{:S(2)}, u32[]{:S(2)}) collective-permute-start(bf16[4,2,3,8,768]{4,3,2,1,0:T(8,128)(2,1)S(1)} %get-tuple-element.193), channel_id=1, source_target_pairs={{0,2},{2,0},{1,3},{3,1},{4,6},{6,4},{5,7},{7,5},{8,10},{10,8},{9,1... | collective-permute-start | bytes 884744 | tf_op jit(solution)/shard_map/ppermute | solution.py:35
  121.1 15.5 %collective-permute-start.37 = (bf16[2,2,4,3,8,768]{5,4,3,2,1,0:T(8,128)(2,1)S(1)}, bf16[2,2,4,3,8,768]{5,4,3,2,1,0:T(8,128)(2,1)S(1)}, u32[]{:S(2)}, u32[]{:S(2)}) collective-permute-start(bf16[2,2,4,3,8,768]{5,4,3,2,1,0:T(8,128)(2,1)S(1)} %copy-done.64), channel_id=1, source_target_pairs={{0,8},{4,12},{8,16},{12,20},{16,24},{20,28},{24,0},{28,4},{1,9},{5... | collective-permute-start | bytes 1769480 | tf_op jit(solution)/shard_map/ppermute | solution.py:80
  141.9 15.7 %collective-permute-start.40 = (bf16[2,4,2,3,8,768]{5,4,3,2,1,0:T(8,128)(2,1)S(1)}, bf16[2,4,2,3,8,768]{5,4,3,2,1,0:T(8,128)(2,1)S(1)}, u32[]{:S(2)}, u32[]{:S(2)}) collective-permute-start(bf16[2,4,2,3,8,768]{5,4,3,2,1,0:T(8,128)(2,1)S(1)} %get-tuple-element.331), channel_id=1, source_target_pairs={{0,2},{2,0},{1,3},{3,1},{4,6},{6,4},{5,7},{7,5},{8,10},{10,8},{9,1... | collective-permute-start | bytes 1769480 | tf_op jit(solution)/shard_map/ppermute | solution.py:35
  143.4 15.4 %collective-permute-start.41 = (bf16[2,4,2,3,8,768]{5,4,3,2,1,0:T(8,128)(2,1)S(1)}, bf16[2,4,2,3,8,768]{5,4,3,2,1,0:T(8,128)(2,1)S(1)}, u32[]{:S(2)}, u32[]{:S(2)}) collective-permute-start(bf16[2,4,2,3,8,768]{5,4,3,2,1,0:T(8,128)(2,1)S(1)} %get-tuple-element.329), channel_id=1, source_target_pairs={{0,4},{4,0},{8,12},{12,8},{16,20},{20,16},{24,28},{28,24},{1,5},{5... | collective-permute-start | bytes 1769480 | tf_op jit(solution)/shard_map/ppermute | solution.py:35
  145.1 16.8 %collective-permute-start.42 = (bf16[2,2,4,3,8,768]{5,4,3,2,1,0:T(8,128)(2,1)S(1)}, bf16[2,2,4,3,8,768]{5,4,3,2,1,0:T(8,128)(2,1)S(1)}, u32[]{:S(2)}, u32[]{:S(2)}) collective-permute-start(bf16[2,2,4,3,8,768]{5,4,3,2,1,0:T(8,128)(2,1)S(1)} %collective-permute-done.37), channel_id=1, source_target_pairs={{0,8},{4,12},{8,16},{12,20},{16,24},{20,28},{24,0},{28,4},{1,9},{5... | collective-permute-start | bytes 1769480 | tf_op jit(solution)/shard_map/ppermute | solution.py:80
  165.9 14.5 %collective-permute-start.43 = (bf16[4,2,2,3,8,768]{5,4,3,2,1,0:T(8,128)(2,1)S(1)}, bf16[4,2,2,3,8,768]{5,4,3,2,1,0:T(8,128)(2,1)S(1)}, u32[]{:S(2)}, u32[]{:S(2)}) collective-permute-start(bf16[4,2,2,3,8,768]{5,4,3,2,1,0:T(8,128)(2,1)S(1)} %get-tuple-element.206), channel_id=1, source_target_pairs={{0,2},{2,0},{1,3},{3,1},{4,6},{6,4},{5,7},{7,5},{8,10},{10,8},{9,1... | collective-permute-start | bytes 1769480 | tf_op jit(solution)/shard_map/ppermute | solution.py:35
  166.5 14.2 %collective-permute-start.44 = (bf16[4,2,2,3,8,768]{5,4,3,2,1,0:T(8,128)(2,1)S(1)}, bf16[4,2,2,3,8,768]{5,4,3,2,1,0:T(8,128)(2,1)S(1)}, u32[]{:S(2)}, u32[]{:S(2)}) collective-permute-start(bf16[4,2,2,3,8,768]{5,4,3,2,1,0:T(8,128)(2,1)S(1)} %get-tuple-element.207), channel_id=1, source_target_pairs={{0,4},{4,0},{8,12},{12,8},{16,20},{20,16},{24,28},{28,24},{1,5},{5... | collective-permute-start | bytes 1769480 | tf_op jit(solution)/shard_map/ppermute | solution.py:35
  184.6 15.6 %collective-permute-start.47 = (bf16[4,2,2,3,8,768]{5,4,3,2,1,0:T(8,128)(2,1)S(1)}, bf16[4,2,2,3,8,768]{5,4,3,2,1,0:T(8,128)(2,1)S(1)}, u32[]{:S(2)}, u32[]{:S(2)}) collective-permute-start(bf16[4,2,2,3,8,768]{5,4,3,2,1,0:T(8,128)(2,1)S(1)} %get-tuple-element.212), channel_id=1, source_target_pairs={{0,2},{2,0},{1,3},{3,1},{4,6},{6,4},{5,7},{7,5},{8,10},{10,8},{9,1... | collective-permute-start | bytes 1769480 | tf_op jit(solution)/shard_map/ppermute | solution.py:35
  186.1 15.3 %collective-permute-start.48 = (bf16[4,2,2,3,8,768]{5,4,3,2,1,0:T(8,128)(2,1)S(1)}, bf16[4,2,2,3,8,768]{5,4,3,2,1,0:T(8,128)(2,1)S(1)}, u32[]{:S(2)}, u32[]{:S(2)}) collective-permute-start(bf16[4,2,2,3,8,768]{5,4,3,2,1,0:T(8,128)(2,1)S(1)} %get-tuple-element.213), channel_id=1, source_target_pairs={{0,4},{4,0},{8,12},{12,8},{16,20},{20,16},{24,28},{28,24},{1,5},{5... | collective-permute-start | bytes 1769480 | tf_op jit(solution)/shard_map/ppermute | solution.py:35
  254.0 28.2 %collective-permute-start.53 = (bf16[2,4,4,3,8,768]{5,4,3,2,1,0:T(8,128)(2,1)}, bf16[2,4,4,3,8,768]{5,4,3,2,1,0:T(8,128)(2,1)}, u32[]{:S(2)}, u32[]{:S(2)}) collective-permute-start(bf16[2,4,4,3,8,768]{5,4,3,2,1,0:T(8,128)(2,1)} %slice_bitcast_fusion.2), channel_id=1, source_target_pairs={{0,2},{2,0},{1,3},{3,1},{4,6},{6,4},{5,7},{7,5},{8,10},{10,8},{9,1... | collective-permute-start | bytes 3538952 | tf_op jit(solution)/shard_map/ppermute | solution.py:35
  255.8 29.1 %collective-permute-start.54 = (bf16[2,4,4,3,8,768]{5,4,3,2,1,0:T(8,128)(2,1)}, bf16[2,4,4,3,8,768]{5,4,3,2,1,0:T(8,128)(2,1)}, u32[]{:S(2)}, u32[]{:S(2)}) collective-permute-start(bf16[2,4,4,3,8,768]{5,4,3,2,1,0:T(8,128)(2,1)} %slice_bitcast_fusion.1), channel_id=1, source_target_pairs={{0,4},{4,0},{8,12},{12,8},{16,20},{20,16},{24,28},{28,24},{1,5},{5... | collective-permute-start | bytes 3538952 | tf_op jit(solution)/shard_map/ppermute | solution.py:35
  269.5 53.6 %collective-permute-start.60 = (bf16[2,4,2,3,8,768]{5,4,3,2,1,0:T(8,128)(2,1)}, bf16[2,4,2,3,8,768]{5,4,3,2,1,0:T(8,128)(2,1)S(1)}, u32[]{:S(2)}, u32[]{:S(2)}) collective-permute-start(bf16[2,4,2,3,8,768]{5,4,3,2,1,0:T(8,128)(2,1)} %slice_bitcast_fusion.11), channel_id=1, source_target_pairs={{0,4},{4,0},{8,12},{12,8},{16,20},{20,16},{24,28},{28,24},{1,5},{5... | collective-permute-start | bytes 1769480 | tf_op jit(solution)/shard_map/ppermute | solution.py:35
  289.2 16.2 %collective-permute-start.58 = (bf16[4,4,3,8,768]{4,3,2,1,0:T(8,128)(2,1)S(1)}, bf16[4,4,3,8,768]{4,3,2,1,0:T(8,128)(2,1)S(1)}, u32[]{:S(2)}, u32[]{:S(2)}) collective-permute-start(bf16[4,4,3,8,768]{4,3,2,1,0:T(8,128)(2,1)S(1)} %slice_bitcast_fusion.13), channel_id=1, source_target_pairs={{0,2},{2,0},{1,3},{3,1},{4,6},{6,4},{5,7},{7,5},{8,10},{10,8},{9,1... | collective-permute-start | bytes 1769480 | tf_op jit(solution)/shard_map/ppermute | solution.py:35
  290.8 18.4 %collective-permute-start.57 = (bf16[4,4,3,8,768]{4,3,2,1,0:T(8,128)(2,1)S(1)}, bf16[4,4,3,8,768]{4,3,2,1,0:T(8,128)(2,1)S(1)}, u32[]{:S(2)}, u32[]{:S(2)}) collective-permute-start(bf16[4,4,3,8,768]{4,3,2,1,0:T(8,128)(2,1)S(1)} %slice_bitcast_fusion.14), channel_id=1, source_target_pairs={{0,4},{4,0},{8,12},{12,8},{16,20},{20,16},{24,28},{28,24},{1,5},{5... | collective-permute-start | bytes 1769480 | tf_op jit(solution)/shard_map/ppermute | solution.py:35
  296.6 26.5 %collective-permute-start.59 = (bf16[2,4,2,3,8,768]{5,4,3,2,1,0:T(8,128)(2,1)S(1)}, bf16[2,4,2,3,8,768]{5,4,3,2,1,0:T(8,128)(2,1)S(1)}, u32[]{:S(2)}, u32[]{:S(2)}) collective-permute-start(bf16[2,4,2,3,8,768]{5,4,3,2,1,0:T(8,128)(2,1)S(1)} %slice_bitcast_fusion.12), channel_id=1, source_target_pairs={{0,2},{2,0},{1,3},{3,1},{4,6},{6,4},{5,7},{7,5},{8,10},{10,8},{9,1... | collective-permute-start | bytes 1769480 | tf_op jit(solution)/shard_map/ppermute | solution.py:35
  309.5 13.6 %collective-permute-start.61 = (bf16[8,3,8,768]{3,2,1,0:T(8,128)(2,1)S(1)}, bf16[8,3,8,768]{3,2,1,0:T(8,128)(2,1)S(1)}, u32[]{:S(2)}, u32[]{:S(2)}) collective-permute-start(bf16[8,3,8,768]{3,2,1,0:T(8,128)(2,1)S(1)} %fusion.48), channel_id=1, source_target_pairs={{0,8},{4,12},{8,16},{12,20},{16,24},{20,28},{24,0},{28,4},{1,9},{5... | collective-permute-start | bytes 884744 | tf_op jit(solution)/shard_map/ppermute | solution.py:80
  323.6 9.9 %collective-permute-start.67 = (bf16[8,3,8,768]{3,2,1,0:T(8,128)(2,1)S(1)}, bf16[8,3,8,768]{3,2,1,0:T(8,128)(2,1)S(1)}, u32[]{:S(2)}, u32[]{:S(2)}) collective-permute-start(bf16[8,3,8,768]{3,2,1,0:T(8,128)(2,1)S(1)} %fusion.37), channel_id=1, source_target_pairs={{0,8},{4,12},{8,16},{12,20},{16,24},{20,28},{24,0},{28,4},{1,9},{5... | collective-permute-start | bytes 884744 | tf_op jit(solution)/shard_map/ppermute | solution.py:80
  324.6 15.6 %collective-permute-start.64 = (bf16[4,2,3,8,768]{4,3,2,1,0:T(8,128)(2,1)S(1)}, bf16[4,2,3,8,768]{4,3,2,1,0:T(8,128)(2,1)S(1)}, u32[]{:S(2)}, u32[]{:S(2)}) collective-permute-start(bf16[4,2,3,8,768]{4,3,2,1,0:T(8,128)(2,1)S(1)} %slice_bitcast_fusion.21), channel_id=1, source_target_pairs={{0,2},{2,0},{1,3},{3,1},{4,6},{6,4},{5,7},{7,5},{8,10},{10,8},{9,1... | collective-permute-start | bytes 884744 | tf_op jit(solution)/shard_map/ppermute | solution.py:35
  325.7 14.5 %collective-permute-start.63 = (bf16[4,2,3,8,768]{4,3,2,1,0:T(8,128)(2,1)S(1)}, bf16[4,2,3,8,768]{4,3,2,1,0:T(8,128)(2,1)S(1)}, u32[]{:S(2)}, u32[]{:S(2)}) collective-permute-start(bf16[4,2,3,8,768]{4,3,2,1,0:T(8,128)(2,1)S(1)} %slice_bitcast_fusion.22), channel_id=1, source_target_pairs={{0,4},{4,0},{8,12},{12,8},{16,20},{20,16},{24,28},{28,24},{1,5},{5... | collective-permute-start | bytes 884744 | tf_op jit(solution)/shard_map/ppermute | solution.py:35
  327.2 10.5 %collective-permute-start.62 = (bf16[384,768]{1,0:T(8,128)(2,1)S(1)}, bf16[384,768]{1,0:T(8,128)(2,1)S(1)}, u32[]{:S(2)}, u32[]{:S(2)}) collective-permute-start(bf16[384,768]{1,0:T(8,128)(2,1)S(1)} %convolution_convert_fusion.6), channel_id=1, source_target_pairs={{0,1},{1,0},{2,3},{3,2},{4,5},{5,4},{6,7},{7,6},{8,9},{9,8},{10,11... | collective-permute-start | bytes 1769480 | tf_op jit(solution)/shard_map/ppermute | solution.py:35
  333.6 19.0 %collective-permute-start.71 = (bf16[8,3,8,768]{3,2,1,0:T(8,128)(2,1)S(1)}, bf16[8,3,8,768]{3,2,1,0:T(8,128)(2,1)}, u32[]{:S(2)}, u32[]{:S(2)}) collective-permute-start(bf16[8,3,8,768]{3,2,1,0:T(8,128)(2,1)S(1)} %fusion.34), channel_id=1, source_target_pairs={{0,8},{4,12},{8,16},{12,20},{16,24},{20,28},{24,0},{28,4},{1,9},{5... | collective-permute-start | bytes 884744 | tf_op jit(solution)/shard_map/ppermute | solution.py:80
  335.5 17.2 %collective-permute-start.68 = (bf16[2,4,2,3,8,768]{5,4,3,2,1,0:T(8,128)(2,1)}, bf16[2,4,2,3,8,768]{5,4,3,2,1,0:T(8,128)(2,1)}, u32[]{:S(2)}, u32[]{:S(2)}) collective-permute-start(bf16[2,4,2,3,8,768]{5,4,3,2,1,0:T(8,128)(2,1)} %slice_bitcast_fusion.5), channel_id=1, source_target_pairs={{0,2},{2,0},{1,3},{3,1},{4,6},{6,4},{5,7},{7,5},{8,10},{10,8},{9,1... | collective-permute-start | bytes 1769480 | tf_op jit(solution)/shard_map/ppermute | solution.py:35
  337.7 15.5 %collective-permute-start.69 = (bf16[2,4,2,3,8,768]{5,4,3,2,1,0:T(8,128)(2,1)}, bf16[2,4,2,3,8,768]{5,4,3,2,1,0:T(8,128)(2,1)}, u32[]{:S(2)}, u32[]{:S(2)}) collective-permute-start(bf16[2,4,2,3,8,768]{5,4,3,2,1,0:T(8,128)(2,1)} %slice_bitcast_fusion.4), channel_id=1, source_target_pairs={{0,4},{4,0},{8,12},{12,8},{16,20},{20,16},{24,28},{28,24},{1,5},{5... | collective-permute-start | bytes 1769480 | tf_op jit(solution)/shard_map/ppermute | solution.py:35
  367.5 18.1 %collective-permute-start.81 = (bf16[4,3,8,768]{3,2,1,0:T(8,128)(2,1)S(1)}, bf16[4,3,8,768]{3,2,1,0:T(8,128)(2,1)S(1)}, u32[]{:S(2)}, u32[]{:S(2)}) collective-permute-start(bf16[4,3,8,768]{3,2,1,0:T(8,128)(2,1)S(1)} %fusion.52), channel_id=1, source_target_pairs={{0,8},{4,12},{8,16},{12,20},{16,24},{20,28},{24,0},{28,4},{1,9},{5... | collective-permute-start | bytes 442376 | tf_op jit(solution)/shard_map/ppermute | solution.py:80
  371.5 12.8 %collective-permute-start.78 = (bf16[4,3,8,768]{3,2,1,0:T(8,128)(2,1)S(1)}, bf16[4,3,8,768]{3,2,1,0:T(8,128)(2,1)S(1)}, u32[]{:S(2)}, u32[]{:S(2)}) collective-permute-start(bf16[4,3,8,768]{3,2,1,0:T(8,128)(2,1)S(1)} %get-tuple-element.325), channel_id=1, source_target_pairs={{0,24},{4,28},{8,0},{12,4},{16,8},{20,12},{24,16},{28,20},{1,25},{... | collective-permute-start | bytes 442376 | tf_op jit(solution)/shard_map/ppermute | solution.py:80
  374.0 10.3 %collective-permute-start.80 = (bf16[4,3,8,768]{3,2,1,0:T(8,128)(2,1)S(1)}, bf16[4,3,8,768]{3,2,1,0:T(8,128)(2,1)S(1)}, u32[]{:S(2)}, u32[]{:S(2)}) collective-permute-start(bf16[4,3,8,768]{3,2,1,0:T(8,128)(2,1)S(1)} %get-tuple-element.326), channel_id=1, source_target_pairs={{0,8},{4,12},{8,16},{12,20},{16,24},{20,28},{24,0},{28,4},{1,9},{5... | collective-permute-start | bytes 442376 | tf_op jit(solution)/shard_map/ppermute | solution.py:80
  374.3 11.2 %collective-permute-start.79 = (bf16[4,3,8,768]{3,2,1,0:T(8,128)(2,1)S(1)}, bf16[4,3,8,768]{3,2,1,0:T(8,128)(2,1)S(1)}, u32[]{:S(2)}, u32[]{:S(2)}) collective-permute-start(bf16[4,3,8,768]{3,2,1,0:T(8,128)(2,1)S(1)} %get-tuple-element.327), channel_id=1, source_target_pairs={{0,16},{4,20},{8,24},{12,28},{16,0},{20,4},{24,8},{28,12},{1,17},{... | collective-permute-start | bytes 442376 | tf_op jit(solution)/shard_map/ppermute | solution.py:80
  410.2 10.7 %collective-permute-start.88 = (f32[56,896]{1,0:T(8,128)S(1)}, f32[56,896]{1,0:T(8,128)S(1)}, u32[]{:S(2)}, u32[]{:S(2)}) collective-permute-start(f32[56,896]{1,0:T(8,128)S(1)} %add.477), channel_id=1, source_target_pairs={{0,16},{4,20},{8,24},{12,28},{16,0},{20,4},{24,8},{28,12},{1,17},{... | collective-permute-start | bytes 602120 | tf_op jit(solution)/shard_map/ppermute | solution.py:35
  415.9 11.6 %collective-permute-start.89 = (bf16[16,8,768]{2,1,0:T(8,128)(2,1)S(1)}, bf16[16,8,768]{2,1,0:T(8,128)(2,1)S(1)}, u32[]{:S(2)}, u32[]{:S(2)}) collective-permute-start(bf16[16,8,768]{2,1,0:T(8,128)(2,1)S(1)} %get-tuple-element.256), channel_id=1, source_target_pairs={{0,4},{4,0},{8,12},{12,8},{16,20},{20,16},{24,28},{28,24},{1,5},{5... | collective-permute-start | bytes 589832 | tf_op jit(solution)/shard_map/ppermute | solution.py:292
  416.4 12.1 %collective-permute-start.90 = (bf16[16,8,768]{2,1,0:T(8,128)(2,1)S(1)}, bf16[16,8,768]{2,1,0:T(8,128)(2,1)S(1)}, u32[]{:S(2)}, u32[]{:S(2)}) collective-permute-start(bf16[16,8,768]{2,1,0:T(8,128)(2,1)S(1)} %get-tuple-element.257), channel_id=1, source_target_pairs={{0,8},{4,12},{8,0},{12,4},{16,24},{20,28},{24,16},{28,20},{1,9},{5... | collective-permute-start | bytes 589832 | tf_op jit(solution)/shard_map/ppermute | solution.py:292
  416.5 17.3 %collective-permute-start.91 = (bf16[16,8,768]{2,1,0:T(8,128)(2,1)S(1)}, bf16[16,8,768]{2,1,0:T(8,128)(2,1)S(1)}, u32[]{:S(2)}, u32[]{:S(2)}) collective-permute-start(bf16[16,8,768]{2,1,0:T(8,128)(2,1)S(1)} %get-tuple-element.258), channel_id=1, source_target_pairs={{0,12},{4,8},{8,4},{12,0},{16,28},{20,24},{24,20},{28,16},{1,13},{... | collective-permute-start | bytes 589832 | tf_op jit(solution)/shard_map/ppermute | solution.py:292
  419.4 14.5 %collective-permute-start.92 = (bf16[16,8,768]{2,1,0:T(8,128)(2,1)S(1)}, bf16[16,8,768]{2,1,0:T(8,128)(2,1)S(1)}, u32[]{:S(2)}, u32[]{:S(2)}) collective-permute-start(bf16[16,8,768]{2,1,0:T(8,128)(2,1)S(1)} %get-tuple-element.259), channel_id=1, source_target_pairs={{0,16},{4,20},{8,24},{12,28},{16,0},{20,4},{24,8},{28,12},{1,17},{... | collective-permute-start | bytes 589832 | tf_op jit(solution)/shard_map/ppermute | solution.py:292
  420.9 25.3 %collective-permute-start.93 = (bf16[16,8,768]{2,1,0:T(8,128)(2,1)S(1)}, bf16[16,8,768]{2,1,0:T(8,128)(2,1)S(1)}, u32[]{:S(2)}, u32[]{:S(2)}) collective-permute-start(bf16[16,8,768]{2,1,0:T(8,128)(2,1)S(1)} %get-tuple-element.260), channel_id=1, source_target_pairs={{0,20},{4,16},{8,28},{12,24},{16,4},{20,0},{24,12},{28,8},{1,21},{... | collective-permute-start | bytes 589832 | tf_op jit(solution)/shard_map/ppermute | solution.py:292
  427.5 24.0 %collective-permute-start.94 = (bf16[16,8,768]{2,1,0:T(8,128)(2,1)S(1)}, bf16[16,8,768]{2,1,0:T(8,128)(2,1)S(1)}, u32[]{:S(2)}, u32[]{:S(2)}) collective-permute-start(bf16[16,8,768]{2,1,0:T(8,128)(2,1)S(1)} %get-tuple-element.261), channel_id=1, source_target_pairs={{0,24},{4,28},{8,16},{12,20},{16,8},{20,12},{24,0},{28,4},{1,25},{... | collective-permute-start | bytes 589832 | tf_op jit(solution)/shard_map/ppermute | solution.py:292
  428.4 25.1 %collective-permute-start.95 = (bf16[16,8,768]{2,1,0:T(8,128)(2,1)S(1)}, bf16[16,8,768]{2,1,0:T(8,128)(2,1)S(1)}, u32[]{:S(2)}, u32[]{:S(2)}) collective-permute-start(bf16[16,8,768]{2,1,0:T(8,128)(2,1)S(1)} %get-tuple-element.262), channel_id=1, source_target_pairs={{0,28},{4,24},{8,20},{12,16},{16,12},{20,8},{24,4},{28,0},{1,29},{... | collective-permute-start | bytes 589832 | tf_op jit(solution)/shard_map/ppermute | solution.py:292
  (205 other events, 1516.8 us)
